TPU v7x, 32 devices: a whole 2x2x4 slice. The times are simulated.
32 devices in a mesh: groups: 2 (over y), gx: 4 (over z), gy: 2 (over x), gz: 2 (over core).
Axes of the slice: x: 2, y: 2, z: 4, core: 2. Of those that a mesh axis runs over, the one named last changes fastest.
Arguments:
- fields: float32 [5, 64, 128, 256], P(None, 'gz', ('groups', 'gx'), 'gy'), parts along dimension 2, may hold values from -6 to 6
- parent_wind: float32 [3, 128], P(None, ('groups', 'gz')), parts along dimension 1, may hold values from -1 to 1
- diffusivity: float32 [5], replicated, may hold values from 0.05 to 0.3
- wall_type: int32 [128, 256], P(('groups', 'gx'), 'gy'), parts along dimension 0, may hold values from 0 to 3
- building_count: int32 [128], P(('groups', 'gx')), parts along dimension 0, may hold values from 0 to 32, as said below
- slot_of: int32 [128], P('groups'), parts along dimension 0, may hold values from -1 to 31, as said below
- parent_of: int32 [128], P('groups'), parts along dimension 0, may hold values from 0 to 7, as said below
Outputs:
- new_fields: float32 [5, 64, 128, 256], P(None, 'gz', ('groups', 'gx'), 'gy'), parts along dimension 2
- wall_stress: float32 [64, 64, 256], P('gz', ('groups', 'gx'), 'gy'), parts along dimension 1
- parent_mean: float32 [16, 5, 8, 32], P(('groups', 'gx'), None, 'gz', 'gy'), parts along dimension 0
There are 2 independent parts, one for each index of `groups`. A program takes and returns all parts, laid end to end along the dimension named above; an argument that names none is the same for every part. Nothing has to cross between parts.
Inputs may be any that keep to these rules, and one draw needn't show every extreme that they name: `slot_of`: exactly 32 tiles have a slot; every value 0 to 31 names exactly one tile, so each block of 8 slots (one device's) is full. Of the tiles of one block of 16 tiles (one device's), at most 4 have slots of the same block of 8, and some block reaches 4. `building_count`: positive exactly where slot_of is not -1. Parent column p begins at tile p * 8 - o[p], with o[0] = 0 and each other o[p] one of 0 to 7; parent_of[x] is the last column that begins at or before x. So it is non-decreasing, every parent column gets at least one tile, and a tile's parent column belongs to its own block of 2 parent columns or is the first of the next block.
All inputs are finite; a program needn't handle non-finite values.
Results may differ from a plain program's by a relative error of at most 0.00011.
Values sent between devices are 32-bit elements; how exact they have to be, the bound alone decides.
No kernel may reach another device: no remote copies, remote signals or barrier semaphores. Data moves between devices by JAX's collectives and lax.ppermute only.
A program may use at most 64 MiB of HBM per device.

v0:
```python
import jax
import jax.numpy as jnp
from jax import lax
from jax.sharding import PartitionSpec as P

FIELDS = 5
RATIO = 8
BMAX = 32
SLOTS = 8


TABLE = (0.4, 0.8, 1.3, 2.0)
STEP = 0.25


def padded_2(cells, sides, width):
    for axis, dim in sides:
        count = lax.axis_size(axis)
        ends = count - 1
        head = lax.slice_in_dim(cells, 0, width, axis=dim)
        tail = lax.slice_in_dim(cells, cells.shape[dim] - width, cells.shape[dim], axis=dim)
        cells = jnp.concatenate(
            [
                lax.ppermute(tail, axis, [(i, (i + 1) % count) for i in range(ends)]),
                cells,
                lax.ppermute(head, axis, [((i + 1) % count, i) for i in range(ends)]),
            ],
            axis=dim,
        )
    return cells


def passed_along(block, axis, distance):
    devices = range(lax.axis_size(axis))
    route = [(i - distance, i) for i in devices if i - distance in devices]
    return lax.ppermute(block, axis, route)


def lookup(wall_type):
    result = jnp.zeros(wall_type.shape, jnp.float32)
    for wall_code, wall_value in enumerate(TABLE):
        result = result + jnp.where(wall_type == wall_code, wall_value, 0.0)
    return result


def tendency(fields, padded, parent_wind, diffusivity):
    diff_x = padded[:, 1:-1, 2:, 1:-1] - padded[:, 1:-1, :-2, 1:-1]
    diff_y = padded[:, 1:-1, 1:-1, 2:] - padded[:, 1:-1, 1:-1, :-2]
    diff_z = padded[:, 2:, 1:-1, 1:-1] - padded[:, :-2, 1:-1, 1:-1]
    beside = padded[:, 1:-1, 2:, 1:-1] + padded[:, 1:-1, :-2, 1:-1]
    beside = beside + padded[:, 1:-1, 1:-1, 2:] + padded[:, 1:-1, 1:-1, :-2]
    beside = beside + padded[:, 2:, 1:-1, 1:-1] + padded[:, :-2, 1:-1, 1:-1]
    advect = 0.5 * (
        parent_wind[0][None, :, None, None] * diff_x
        + parent_wind[1][None, :, None, None] * diff_y
        + parent_wind[2][None, :, None, None] * diff_z
    )
    return -advect + diffusivity[:, None, None, None] * (beside - 6.0 * fields)


def body(fields, parent_wind, diffusivity, wall_type, building_count, slot_of, parent_of):
    highest = lax.Precision.HIGHEST
    width_gx = lax.axis_size("gx")
    gx_index = lax.axis_index("gx")
    levels_dev = fields.shape[1]
    tiles_dev = fields.shape[2]
    columns_dev = fields.shape[3]
    all_tiles = slot_of.shape[0]
    capacity = (tiles_dev + width_gx - 1) // width_gx
    buffers = width_gx * capacity
    first_tile = gx_index * tiles_dev
    tile_ids = jnp.arange(all_tiles, dtype=jnp.int32)
    source = tile_ids // tiles_dev
    target = jnp.where(slot_of >= 0, slot_of // SLOTS, -1)
    earlier = (
        (source[:, None] == source[None, :])
        & (target[:, None] == target[None, :])
        & (tile_ids[None, :] < tile_ids[:, None])
    )
    rank_within = jnp.sum(earlier.astype(jnp.int32), axis=1)
    buffer_index = jnp.where(slot_of >= 0, target * capacity + rank_within, -1)
    incoming_index = jnp.where(slot_of >= 0, source * capacity + rank_within, -1)
    buffer_ids = jnp.arange(buffers, dtype=jnp.int32)
    my_buffer = lax.dynamic_slice_in_dim(buffer_index, first_tile, tiles_dev)
    send_pick = (buffer_ids[:, None] == my_buffer[None, :]).astype(jnp.float32)
    slot_ids = gx_index * SLOTS + jnp.arange(SLOTS, dtype=jnp.int32)
    take_from = (slot_ids[:, None] == slot_of[None, :]).astype(jnp.float32)
    place_at = (incoming_index[:, None] == buffer_ids[None, :]).astype(jnp.float32)
    recv_pick = jnp.dot(take_from, place_at, precision=highest)
    my_slots = lax.dynamic_slice_in_dim(slot_of, first_tile, tiles_dev)
    strength = jnp.where(my_slots >= 0, building_count.astype(jnp.float32) / BMAX, 0.0)
    wall_coef = lookup(wall_type) * strength[:, None]
    factor_local = jnp.zeros((levels_dev, tiles_dev, columns_dev), jnp.float32)
    for step_number in range(2):
        padded = padded_2(fields, (("gx", 2), ("gy", 3), ("gz", 1)), 1)
        change = tendency(fields, padded, parent_wind, diffusivity)
        factor_local = wall_coef[None] * jnp.sqrt(
            fields[0] * fields[0] + fields[1] * fields[1] + fields[2] * fields[2] + 1.0
        )
        wall_part = -(factor_local[None] * fields[:3])
        fields = fields + STEP * jnp.concatenate([change[:3] + wall_part, change[3:]], axis=0)
    sent_factor = jnp.einsum("kt,zty->kzy", send_pick, factor_local, precision=highest)
    sent_factor = sent_factor.reshape(width_gx, capacity, levels_dev, columns_dev)
    got_factor = lax.all_to_all(sent_factor, "gx", split_axis=0, concat_axis=0, tiled=True)
    wall_stress = jnp.einsum(
        "sk,kzy->zsy",
        recv_pick,
        got_factor.reshape(buffers, levels_dev, columns_dev),
        precision=highest,
    )
    coarse = fields.reshape(
        FIELDS, levels_dev // RATIO, RATIO, tiles_dev, columns_dev // RATIO, RATIO
    ).sum(axis=(2, 5))
    parents_dev = tiles_dev // RATIO
    my_parents = lax.dynamic_slice_in_dim(parent_of, first_tile, tiles_dev)
    local_index = my_parents - gx_index * parents_dev
    owner_pick = (
        local_index[:, None] == jnp.arange(parents_dev + 1, dtype=jnp.int32)[None, :]
    ).astype(jnp.float32)
    contrib = jnp.einsum("fzty,tp->pfzy", coarse, owner_pick, precision=highest)
    incoming = passed_along(contrib[parents_dev:], "gx", 1)
    parent_sums = contrib[:parents_dev].at[0].add(incoming[0])
    owned = gx_index * parents_dev + jnp.arange(parents_dev, dtype=jnp.int32)
    tile_tally = jnp.sum((parent_of[None, :] == owned[:, None]).astype(jnp.float32), axis=1)
    parent_mean = parent_sums / (tile_tally[:, None, None, None] * (RATIO * RATIO))
    return (fields, wall_stress, parent_mean)


def solution(mesh):
    in_specs = (
        P(None, "gz", ("groups", "gx"), "gy"),
        P(None, ("groups", "gz")),
        P(),
        P(("groups", "gx"), "gy"),
        P(("groups", "gx")),
        P("groups"),
        P("groups"),
    )
    out_specs = (
        P(None, "gz", ("groups", "gx"), "gy"),
        P("gz", ("groups", "gx"), "gy"),
        P(("groups", "gx"), None, "gz", "gy"),
    )
    return jax.shard_map(body, mesh=mesh, in_specs=in_specs, out_specs=out_specs, check_vma=False)
```

profile of v0, /device:TPU:0, one launch (start us, length us, event | category | flops | bytes accessed | tf_op | source)
XLA Modules:
  0.0 139.1 jit_solution(6306187987761017313)
XLA Ops:
  0.7 1.5 %fusion.30 = (f32[5,32,1,128]{3,2,1,0:T(1,128)S(1)}, f32[5,32,1,128]{3,2,1,0:T(1,128)S(1)}) fusion(f32[5,32,16,128]{3,2,1,0:T(8,128)} %param.9), kind=kLoop, calls=%fused_computation.105 | loop fusion | bytes 327680 | tf_op jit(solution)/shard_map/slice | solution.py:21
  2.2 1.3 collective-permute-start
  3.5 5.6 %collective-permute-start.1 = (f32[5,32,1,128]{3,1,2,0:T(8,128)S(1)}, f32[5,32,1,128]{3,1,2,0:T(8,128)S(1)}, u32[]{:S(2)}, u32[]{:S(2)}) collective-permute-start(f32[5,32,1,128]{3,1,2,0:T(8,128)S(1)} %bitcast.53), channel_id=1, source_target_pairs={{0,4},{4,8},{8,12},{1,5},{5,9},{9,13},{2,6},{6,10},{10,14},{3,7},{... | collective-permute-start | bytes 245768 | tf_op jit(solution)/shard_map/ppermute | solution.py:24
  9.1 0.7 and_select_fusion
  9.7 0.2 convert_reduce_fusion
  9.9 1.3 add_select_fusion.1
  11.2 1.4 slice_bitcast_fusion.2
  12.5 0.7 compare_select_fusion
  13.3 0.8 add_multiply_fusion
  14.1 1.2 multiply_bitcast_fusion
  15.3 0.2 fusion.24
  15.5 0.5 broadcast_multiply_fusion
  16.0 0.6 copy-done.8
  16.7 1.2 pad_maximum_fusion
  17.9 2.5 %fusion.28 = (f32[5,32,18,1]{3,2,1,0:T(8,128)}, f32[5,32,18,1]{3,2,1,0:T(8,128)}) fusion(f32[5,32,18,128]{3,2,1,0:T(8,128)S(1)} %pad_maximum_fusion), kind=kLoop, calls=%fused_computation.103 | loop fusion | bytes 46080 | tf_op jit(solution)/shard_map/slice | solution.py:21
  20.4 2.8 %copy.208 = f32[5,32,18,1]{1,3,2,0:T(1,128)} copy(f32[5,32,18,1]{3,2,1,0:T(8,128)} %get-tuple-element.43) | data formatting | bytes 23040 | tf_op jit(solution)/shard_map/slice | solution.py:21
  23.1 2.8 %copy.206 = f32[5,32,18,1]{1,3,2,0:T(1,128)} copy(f32[5,32,18,1]{3,2,1,0:T(8,128)} %get-tuple-element.44) | data formatting | bytes 23040 | tf_op jit(solution)/shard_map/slice | solution.py:20
  25.9 1.3 collective-permute-start.2
  27.2 5.8 %collective-permute-start.3 = (f32[5,32,18,1]{1,3,2,0:T(1,128)}, f32[5,32,18,1]{1,3,2,0:T(1,128)}, u32[]{:S(2)}, u32[]{:S(2)}) collective-permute-start(f32[5,32,18,1]{1,3,2,0:T(1,128)} %copy.208), channel_id=1, source_target_pairs={{0,2},{1,3},{4,6},{5,7},{8,10},{9,11},{12,14},{13,15},{16,18},{17,... | collective-permute-start | bytes 34568 | tf_op jit(solution)/shard_map/ppermute | solution.py:24
  32.9 0.5 iota_add_fusion.1
  33.4 1.4 %copy.211 = f32[5,32,18,128]{3,1,2,0:T(8,128)} copy(f32[5,32,18,128]{3,2,1,0:T(8,128)S(1)} %pad_maximum_fusion) | data formatting | bytes 2949120 | tf_op jit(solution)/shard_map/concatenate | solution.py:22
  34.8 2.7 %copy.210 = f32[5,32,18,1]{3,1,2,0:T(8,128)} copy(f32[5,32,18,1]{1,3,2,0:T(1,128)} %collective-permute-done.3) | data formatting | bytes 23040 | tf_op jit(solution)/shard_map/ppermute | solution.py:24
  37.5 2.6 %copy.212 = f32[5,32,18,1]{3,1,2,0:T(8,128)} copy(f32[5,32,18,1]{1,3,2,0:T(1,128)} %collective-permute-done.2) | data formatting | bytes 23040 | tf_op jit(solution)/shard_map/ppermute | solution.py:26
  40.1 2.6 %pad_maximum_fusion.35 = (f32[5,1,18,130]{3,1,2,0:T(1,128)}, f32[5,1,18,130]{3,1,2,0:T(1,128)S(1)}) fusion(f32[5,32,18,1]{3,1,2,0:T(8,128)} %copy.212, f32[5,32,18,128]{3,1,2,0:T(8,128)S(1)} %copy-done.1, f32[5,32,18,1]{3,1,2,0:T(8,128)} %copy.210), kind=kLoop, calls=%fused_computation.59 | loop fusion | flops 46800 | bytes 1591200 | tf_op jit(solution)/shard_map/slice | solution.py:20
  42.7 1.3 collective-permute-start.4
  44.0 3.0 %collective-permute-start.5 = (f32[5,1,18,130]{3,1,2,0:T(1,128)S(1)}, f32[5,1,18,130]{3,1,2,0:T(1,128)S(1)}, u32[]{:S(2)}, u32[]{:S(2)}) collective-permute-start(f32[5,1,18,130]{3,1,2,0:T(1,128)S(1)} %get-tuple-element.40), channel_id=1, source_target_pairs={{0,1},{2,3},{4,5},{6,7},{8,9},{10,11},{12,13},{14,15},{16,17},{18,... | collective-permute-start | bytes 140408 | tf_op jit(solution)/shard_map/ppermute | solution.py:24
  47.1 0.8 convolution_bitcast_fusion.1
  47.8 2.8 %copy.207 = f32[5,32,18,1]{3,2,1,0:T(8,128)} copy(f32[5,32,18,1]{1,3,2,0:T(1,128)} %collective-permute-done.2) | data formatting | bytes 23040 | tf_op jit(solution)/shard_map/ppermute | solution.py:26
  50.7 2.8 %copy.209 = f32[5,32,18,1]{3,2,1,0:T(8,128)} copy(f32[5,32,18,1]{1,3,2,0:T(1,128)} %collective-permute-done.3) | data formatting | bytes 23040 | tf_op jit(solution)/shard_map/ppermute | solution.py:24
  53.5 2.8 %pad_maximum_fusion.19 = (f32[5,32,16,128]{3,1,2,0:T(8,128)S(1)}, f32[5,32,16,128]{3,1,2,0:T(8,128)S(1)}) fusion(f32[5,1,18,130]{3,1,2,0:T(1,128)S(1)} %collective-permute-done.4, f32[5,32,18,1]{3,1,2,0:T(8,128)} %copy.212, f32[5,32,18,128]{3,1,2,0:T(8,128)S(1)} %copy-done.1, f32[5,32,18,1]{3,1,2,0:T(8,128)} %copy.210, ...), kind=kLoop, calls=%fused_computation.19 | loop fusion | flops 1966080 | bytes 4212640 | tf_op jit(solution)/shard_map/concatenate | solution.py:22
  56.5 3.6 %multiply_add_fusion.1 = f32[5,32,16,128]{3,2,1,0:T(8,128)S(1)} fusion(f32[5,32,16,128]{3,2,1,0:T(8,128)S(1)} %copy-done, f32[5,32,16,128]{3,1,2,0:T(8,128)S(1)} %get-tuple-element.38, f32[5,32,16,128]{3,1,2,0:T(8,128)S(1)} %get-tuple-element.37, f32[5,32,18,1]{3,2,1,0:T(8,128)S(1)} %copy-done.5, f32[5,32,1,128]{3,2,1,0:T(1,128)S(1)} %bitcast.46, ...), kind=kLoop, calls=%fused_computation.35 | loop fusion | flops 8847360 | bytes 5430164 | tf_op jit(solution)/shard_map/add | solution.py:58
  60.3 0.2 fusion
  60.6 1.3 collective-permute-start.6
  61.9 4.6 %collective-permute-start.7 = (f32[5,32,1,128]{3,1,2,0:T(8,128)S(1)}, f32[5,32,1,128]{3,1,2,0:T(8,128)S(1)}, u32[]{:S(2)}, u32[]{:S(2)}) collective-permute-start(f32[5,32,1,128]{3,1,2,0:T(8,128)S(1)} %bitcast.55), channel_id=1, source_target_pairs={{0,4},{4,8},{8,12},{1,5},{5,9},{9,13},{2,6},{6,10},{10,14},{3,7},{... | collective-permute-start | bytes 245768 | tf_op jit(solution)/shard_map/ppermute | solution.py:24
  66.4 0.6 multiply_add_fusion.2
  67.0 1.5 %collective-permute-done.7 = f32[5,32,1,128]{3,1,2,0:T(8,128)S(1)} collective-permute-done((f32[5,32,1,128]{3,1,2,0:T(8,128)S(1)}, f32[5,32,1,128]{3,1,2,0:T(8,128)S(1)}, u32[]{:S(2)}, u32[]{:S(2)}) %collective-permute-start.7) | collective-permute-done | bytes 81952 | tf_op jit(solution)/shard_map/ppermute | solution.py:24
  68.4 0.3 pad_maximum_fusion.1
  68.7 2.5 %fusion.27 = (f32[5,32,18,1]{3,2,1,0:T(8,128)}, f32[5,32,18,1]{3,2,1,0:T(8,128)}) fusion(f32[5,32,18,128]{3,2,1,0:T(8,128)S(1)} %pad_maximum_fusion.1), kind=kLoop, calls=%fused_computation.102 | loop fusion | bytes 46080 | tf_op jit(solution)/shard_map/slice | solution.py:21
  71.2 2.8 %copy.223 = f32[5,32,18,1]{1,3,2,0:T(1,128)} copy(f32[5,32,18,1]{3,2,1,0:T(8,128)} %get-tuple-element.41) | data formatting | bytes 23040 | tf_op jit(solution)/shard_map/slice | solution.py:21
  74.0 2.8 %copy.221 = f32[5,32,18,1]{1,3,2,0:T(1,128)} copy(f32[5,32,18,1]{3,2,1,0:T(8,128)} %get-tuple-element.42) | data formatting | bytes 23040 | tf_op jit(solution)/shard_map/slice | solution.py:20
  76.7 1.3 collective-permute-start.8
  78.0 4.7 %collective-permute-start.9 = (f32[5,32,18,1]{1,3,2,0:T(1,128)}, f32[5,32,18,1]{1,3,2,0:T(1,128)S(1)}, u32[]{:S(2)}, u32[]{:S(2)}) collective-permute-start(f32[5,32,18,1]{1,3,2,0:T(1,128)} %copy.223), channel_id=1, source_target_pairs={{0,2},{1,3},{4,6},{5,7},{8,10},{9,11},{12,14},{13,15},{16,18},{17,... | collective-permute-start | bytes 34568 | tf_op jit(solution)/shard_map/ppermute | solution.py:24
  82.8 1.3 dynamic-slice_subtract_fusion
  84.0 1.3 dynamic_slice.10
  85.3 1.4 %copy.226 = f32[5,32,18,128]{3,1,2,0:T(8,128)} copy(f32[5,32,18,128]{3,2,1,0:T(8,128)S(1)} %pad_maximum_fusion.1) | data formatting | bytes 2949120 | tf_op jit(solution)/shard_map/concatenate | solution.py:22
  86.7 1.8 %copy.225 = f32[5,32,18,1]{3,1,2,0:T(8,128)} copy(f32[5,32,18,1]{1,3,2,0:T(1,128)S(1)} %collective-permute-done.9) | data formatting | bytes 23040 | tf_op jit(solution)/shard_map/ppermute | solution.py:24
  88.5 1.8 %copy.227 = f32[5,32,18,1]{3,1,2,0:T(8,128)} copy(f32[5,32,18,1]{1,3,2,0:T(1,128)S(1)} %collective-permute-done.8) | data formatting | bytes 23040 | tf_op jit(solution)/shard_map/ppermute | solution.py:26
  90.3 2.6 %pad_maximum_fusion.32 = (f32[5,1,18,130]{3,1,2,0:T(1,128)}, f32[5,1,18,130]{3,1,2,0:T(1,128)}) fusion(f32[5,32,18,1]{3,1,2,0:T(8,128)} %copy.227, f32[5,32,18,128]{3,1,2,0:T(8,128)S(1)} %copy-done.2, f32[5,32,18,1]{3,1,2,0:T(8,128)} %copy.225), kind=kLoop, calls=%fused_computation.56 | loop fusion | flops 46800 | bytes 1591200 | tf_op jit(solution)/shard_map/slice | solution.py:20
  92.9 1.3 collective-permute-start.10
  94.2 3.0 %collective-permute-start.11 = (f32[5,1,18,130]{3,1,2,0:T(1,128)}, f32[5,1,18,130]{3,1,2,0:T(1,128)S(1)}, u32[]{:S(2)}, u32[]{:S(2)}) collective-permute-start(f32[5,1,18,130]{3,1,2,0:T(1,128)} %get-tuple-element.36), channel_id=1, source_target_pairs={{0,1},{2,3},{4,5},{6,7},{8,9},{10,11},{12,13},{14,15},{16,17},{18,... | collective-permute-start | bytes 140408 | tf_op jit(solution)/shard_map/ppermute | solution.py:24
  97.4 2.0 %copy.222 = f32[5,32,18,1]{3,2,1,0:T(8,128)} copy(f32[5,32,18,1]{1,3,2,0:T(1,128)S(1)} %collective-permute-done.8) | data formatting | bytes 23040 | tf_op jit(solution)/shard_map/ppermute | solution.py:26
  99.4 2.0 %copy.224 = f32[5,32,18,1]{3,2,1,0:T(8,128)} copy(f32[5,32,18,1]{1,3,2,0:T(1,128)S(1)} %collective-permute-done.9) | data formatting | bytes 23040 | tf_op jit(solution)/shard_map/ppermute | solution.py:24
  101.4 2.8 %pad_maximum_fusion.5 = (f32[5,32,16,128]{3,1,2,0:T(8,128)S(1)}, f32[5,32,16,128]{3,1,2,0:T(8,128)S(1)}) fusion(f32[5,1,18,130]{3,1,2,0:T(1,128)S(1)} %collective-permute-done.10, f32[5,32,18,1]{3,1,2,0:T(8,128)} %copy.227, f32[5,32,18,128]{3,1,2,0:T(8,128)S(1)} %copy-done.2, f32[5,32,18,1]{3,1,2,0:T(8,128)} %copy.225, ...), kind=kLoop, calls=%fused_computation.5 | loop fusion | flops 1966080 | bytes 4212640 | tf_op jit(solution)/shard_map/concatenate | solution.py:22
  104.4 3.6 %multiply_add_fusion = f32[5,32,16,128]{3,2,1,0:T(8,128)S(1)} fusion(f32[5,32,16,128]{3,2,1,0:T(8,128)S(1)} %fusion, f32[5,32,16,128]{3,1,2,0:T(8,128)S(1)} %get-tuple-element.34, f32[5,32,16,128]{3,1,2,0:T(8,128)S(1)} %get-tuple-element.33, f32[5,32,18,1]{3,2,1,0:T(8,128)S(1)} %copy-done.3, f32[5,32,1,128]{3,2,1,0:T(1,128)S(1)} %bitcast.50, ...), kind=kLoop, calls=%fused_computation.34 | loop fusion | flops 8847360 | bytes 5430164 | tf_op jit(solution)/shard_map/add | solution.py:58
  108.1 0.2 fusion.1
  108.3 5.5 %copy.232 = f32[5,32,16,128]{2,3,1,0:T(8,128)} copy(f32[5,32,16,128]{3,2,1,0:T(8,128)S(1)} %fusion.1) | data formatting | bytes 2621440 | tf_op jit(solution)/shard_map/add | solution.py:101
  113.8 5.5 %reduce_sum.28 = f32[5,4,16,16]{2,3,1,0:T(8,128)S(1)} reduce(f32[5,4,8,16,16,8]{3,5,4,2,1,0:T(8,128)} %bitcast.43, f32[]{:T(128)} %constant.83.clone.1), dimensions={2,5}, to_apply=%region_1.2 | reduce | flops 322560 | bytes 1331204 | tf_op jit(solution)/shard_map/reduce_sum | solution.py:113
  119.4 0.7 fusion.22
  120.1 4.3 %collective-permute-start.12 = (f32[1,5,4,16]{3,0,2,1:T(1,128)S(1)}, f32[1,5,4,16]{3,0,2,1:T(1,128)S(1)}, u32[]{:S(2)}, u32[]{:S(2)}) collective-permute-start(f32[1,5,4,16]{3,0,2,1:T(1,128)S(1)} %slice.242), channel_id=1, source_target_pairs={{0,4},{4,8},{8,12},{1,5},{5,9},{9,13},{2,6},{6,10},{10,14},{3,7},{... | collective-permute-start | bytes 3848 | tf_op jit(solution)/shard_map/ppermute | solution.py:36
  124.4 1.1 fusion.9
  125.5 4.3 %all-to-all-start = ((f32[4,4,32,128]{3,1,2,0:T(4,128)}), f32[4,4,32,128]{3,1,2,0:T(4,128)S(1)}, u32[]{:S(2)}, u32[]{:S(2)}) async-start(f32[4,4,32,128]{3,1,2,0:T(4,128)} %fusion.9), calls=%async_computation | async-start | bytes 524288 | tf_op jit(solution)/shard_map/all_to_all | solution.py:104
  130.0 0.6 copy.234
  130.6 7.4 %all-to-all-done = f32[4,4,32,128]{3,1,2,0:T(4,128)S(1)} async-done(((f32[4,4,32,128]{3,1,2,0:T(4,128)}), f32[4,4,32,128]{3,1,2,0:T(4,128)S(1)}, u32[]{:S(2)}, u32[]{:S(2)}) %all-to-all-start) | async-done | bytes 262176 | tf_op jit(solution)/shard_map/all_to_all | solution.py:104
  138.0 1.1 convolution_bitcast_fusion
  (74 shorter events, 1.1 us)
Async XLA Ops:
  0.6 16.0 %copy-start = (f32[5,32,16,128]{3,2,1,0:T(8,128)S(1)}, f32[5,32,16,128]{3,2,1,0:T(8,128)}, u32[]{:S(2)}) copy-start(f32[5,32,16,128]{3,2,1,0:T(8,128)} %param.9) | copy-start | bytes 3932164
  0.6 14.6 %copy-start.21 = (s32[64]{0:T(128)S(1)}, s32[64]{0:T(128)}, u32[]{:S(2)}) copy-start(s32[64]{0:T(128)} %param.15) | copy-start | bytes 772
  2.2 13.8 %collective-permute-start = (f32[5,32,1,128]{3,1,2,0:T(8,128)S(1)}, f32[5,32,1,128]{3,1,2,0:T(8,128)S(1)}, u32[]{:S(2)}, u32[]{:S(2)}) collective-permute-start(f32[5,32,1,128]{3,1,2,0:T(8,128)S(1)} %bitcast.54), channel_id=1, source_target_pairs={{4,0},{8,4},{12,8},{5,1},{9,5},{13,9},{6,2},{10,6},{14,10},{7,3},{... | collective-permute-start | bytes 245768 | tf_op jit(solution)/shard_map/ppermute | solution.py:26
  3.5 12.5 %collective-permute-start.1 = (f32[5,32,1,128]{3,1,2,0:T(8,128)S(1)}, f32[5,32,1,128]{3,1,2,0:T(8,128)S(1)}, u32[]{:S(2)}, u32[]{:S(2)}) collective-permute-start(f32[5,32,1,128]{3,1,2,0:T(8,128)S(1)} %bitcast.53), channel_id=1, source_target_pairs={{0,4},{4,8},{8,12},{1,5},{5,9},{9,13},{2,6},{6,10},{10,14},{3,7},{... | collective-permute-start | bytes 245768 | tf_op jit(solution)/shard_map/ppermute | solution.py:24
  16.0 0.6 copy-start.8
  16.0 0.7 copy-start.10
  25.9 11.6 %collective-permute-start.2 = (f32[5,32,18,1]{1,3,2,0:T(1,128)}, f32[5,32,18,1]{1,3,2,0:T(1,128)}, u32[]{:S(2)}, u32[]{:S(2)}) collective-permute-start(f32[5,32,18,1]{1,3,2,0:T(1,128)} %copy.206), channel_id=1, source_target_pairs={{2,0},{3,1},{6,4},{7,5},{10,8},{11,9},{14,12},{15,13},{18,16},{19,... | collective-permute-start | bytes 34568 | tf_op jit(solution)/shard_map/ppermute | solution.py:26
  27.2 7.7 %collective-permute-start.3 = (f32[5,32,18,1]{1,3,2,0:T(1,128)}, f32[5,32,18,1]{1,3,2,0:T(1,128)}, u32[]{:S(2)}, u32[]{:S(2)}) collective-permute-start(f32[5,32,18,1]{1,3,2,0:T(1,128)} %copy.208), channel_id=1, source_target_pairs={{0,2},{1,3},{4,6},{5,7},{8,10},{9,11},{12,14},{13,15},{16,18},{17,... | collective-permute-start | bytes 34568 | tf_op jit(solution)/shard_map/ppermute | solution.py:24
  34.8 5.2 %copy-start.1 = (f32[5,32,18,128]{3,1,2,0:T(8,128)S(1)}, f32[5,32,18,128]{3,1,2,0:T(8,128)}, u32[]{:S(2)}) copy-start(f32[5,32,18,128]{3,1,2,0:T(8,128)} %copy.211) | copy-start | bytes 4423684
  40.1 7.0 %copy-start.19 = (s32[64]{0:T(128)S(1)}, s32[64]{0:T(128)}, u32[]{:S(2)}) copy-start(s32[64]{0:T(128)} %param.14) | copy-start | bytes 772
  40.1 7.0 %copy-start.20 = (s32[64]{0:T(128)S(1)}, s32[64]{0:T(128)}, u32[]{:S(2)}) copy-start(s32[64]{0:T(128)} %get-tuple-element.53) | copy-start | bytes 772
  40.1 7.0 %copy-start.24 = (s32[8]{0:T(128)S(1)}, s32[8]{0:T(128)}, u32[]{:S(2)}) copy-start(s32[8]{0:T(128)} %iota_add_fusion.1) | copy-start | bytes 100
  42.7 10.8 %collective-permute-start.4 = (f32[5,1,18,130]{3,1,2,0:T(1,128)}, f32[5,1,18,130]{3,1,2,0:T(1,128)S(1)}, u32[]{:S(2)}, u32[]{:S(2)}) collective-permute-start(f32[5,1,18,130]{3,1,2,0:T(1,128)} %get-tuple-element.39), channel_id=1, source_target_pairs={{1,0},{3,2},{5,4},{7,6},{9,8},{11,10},{13,12},{15,14},{17,16},{19,... | collective-permute-start | bytes 140408 | tf_op jit(solution)/shard_map/ppermute | solution.py:26
  44.0 9.5 %collective-permute-start.5 = (f32[5,1,18,130]{3,1,2,0:T(1,128)S(1)}, f32[5,1,18,130]{3,1,2,0:T(1,128)S(1)}, u32[]{:S(2)}, u32[]{:S(2)}) collective-permute-start(f32[5,1,18,130]{3,1,2,0:T(1,128)S(1)} %get-tuple-element.40), channel_id=1, source_target_pairs={{0,1},{2,3},{4,5},{6,7},{8,9},{10,11},{12,13},{14,15},{16,17},{18,... | collective-permute-start | bytes 140408 | tf_op jit(solution)/shard_map/ppermute | solution.py:24
  53.4 2.9 %copy-start.9 = (f32[5,32,1,128]{3,1,2,0:T(8,128)S(1)}, f32[5,32,1,128]{3,1,2,0:T(8,128)}, u32[]{:S(2)}) copy-start(f32[5,32,1,128]{3,1,2,0:T(8,128)} %copy-done.8) | copy-start | bytes 245764
  53.5 2.9 %copy-start.11 = (f32[5,32,1,128]{3,1,2,0:T(8,128)S(1)}, f32[5,32,1,128]{3,1,2,0:T(8,128)}, u32[]{:S(2)}) copy-start(f32[5,32,1,128]{3,1,2,0:T(8,128)} %copy-done.10) | copy-start | bytes 245764
  53.5 2.9 %copy-start.12 = (f32[32]{0:T(128)S(1)}, f32[32]{0:T(128)}, u32[]{:S(2)}) copy-start(f32[32]{0:T(128)} %get-tuple-element.51) | copy-start | bytes 388
  53.5 2.9 %copy-start.15 = (f32[5]{0:T(128)S(1)}, f32[5]{0:T(128)}, u32[]{:S(2)}) copy-start(f32[5]{0:T(128)} %param.11) | copy-start | bytes 64
  53.5 2.9 %copy-start.5 = (f32[5,32,18,1]{3,2,1,0:T(8,128)S(1)}, f32[5,32,18,1]{3,2,1,0:T(8,128)}, u32[]{:S(2)}) copy-start(f32[5,32,18,1]{3,2,1,0:T(8,128)} %copy.207) | copy-start | bytes 34564
  53.5 3.0 %copy-start.6 = (f32[5,32,18,1]{3,2,1,0:T(8,128)S(1)}, f32[5,32,18,1]{3,2,1,0:T(8,128)}, u32[]{:S(2)}) copy-start(f32[5,32,18,1]{3,2,1,0:T(8,128)} %copy.209) | copy-start | bytes 34564
  60.6 6.4 %collective-permute-start.6 = (f32[5,32,1,128]{3,1,2,0:T(8,128)S(1)}, f32[5,32,1,128]{3,1,2,0:T(8,128)S(1)}, u32[]{:S(2)}, u32[]{:S(2)}) collective-permute-start(f32[5,32,1,128]{3,1,2,0:T(8,128)S(1)} %bitcast.56), channel_id=1, source_target_pairs={{4,0},{8,4},{12,8},{5,1},{9,5},{13,9},{6,2},{10,6},{14,10},{7,3},{... | collective-permute-start | bytes 245768 | tf_op jit(solution)/shard_map/ppermute | solution.py:26
  61.9 6.6 %collective-permute-start.7 = (f32[5,32,1,128]{3,1,2,0:T(8,128)S(1)}, f32[5,32,1,128]{3,1,2,0:T(8,128)S(1)}, u32[]{:S(2)}, u32[]{:S(2)}) collective-permute-start(f32[5,32,1,128]{3,1,2,0:T(8,128)S(1)} %bitcast.55), channel_id=1, source_target_pairs={{0,4},{4,8},{8,12},{1,5},{5,9},{9,13},{2,6},{6,10},{10,14},{3,7},{... | collective-permute-start | bytes 245768 | tf_op jit(solution)/shard_map/ppermute | solution.py:24
  76.7 11.7 %collective-permute-start.8 = (f32[5,32,18,1]{1,3,2,0:T(1,128)}, f32[5,32,18,1]{1,3,2,0:T(1,128)S(1)}, u32[]{:S(2)}, u32[]{:S(2)}) collective-permute-start(f32[5,32,18,1]{1,3,2,0:T(1,128)} %copy.221), channel_id=1, source_target_pairs={{2,0},{3,1},{6,4},{7,5},{10,8},{11,9},{14,12},{15,13},{18,16},{19,... | collective-permute-start | bytes 34568 | tf_op jit(solution)/shard_map/ppermute | solution.py:26
  78.0 8.7 %collective-permute-start.9 = (f32[5,32,18,1]{1,3,2,0:T(1,128)}, f32[5,32,18,1]{1,3,2,0:T(1,128)S(1)}, u32[]{:S(2)}, u32[]{:S(2)}) collective-permute-start(f32[5,32,18,1]{1,3,2,0:T(1,128)} %copy.223), channel_id=1, source_target_pairs={{0,2},{1,3},{4,6},{5,7},{8,10},{9,11},{12,14},{13,15},{16,18},{17,... | collective-permute-start | bytes 34568 | tf_op jit(solution)/shard_map/ppermute | solution.py:24
  86.7 3.5 %copy-start.2 = (f32[5,32,18,128]{3,1,2,0:T(8,128)S(1)}, f32[5,32,18,128]{3,1,2,0:T(8,128)}, u32[]{:S(2)}) copy-start(f32[5,32,18,128]{3,1,2,0:T(8,128)} %copy.226) | copy-start | bytes 4423684
  92.9 8.5 %collective-permute-start.10 = (f32[5,1,18,130]{3,1,2,0:T(1,128)}, f32[5,1,18,130]{3,1,2,0:T(1,128)S(1)}, u32[]{:S(2)}, u32[]{:S(2)}) collective-permute-start(f32[5,1,18,130]{3,1,2,0:T(1,128)} %get-tuple-element.35), channel_id=1, source_target_pairs={{1,0},{3,2},{5,4},{7,6},{9,8},{11,10},{13,12},{15,14},{17,16},{19,... | collective-permute-start | bytes 140408 | tf_op jit(solution)/shard_map/ppermute | solution.py:26
  94.2 7.2 %collective-permute-start.11 = (f32[5,1,18,130]{3,1,2,0:T(1,128)}, f32[5,1,18,130]{3,1,2,0:T(1,128)S(1)}, u32[]{:S(2)}, u32[]{:S(2)}) collective-permute-start(f32[5,1,18,130]{3,1,2,0:T(1,128)} %get-tuple-element.36), channel_id=1, source_target_pairs={{0,1},{2,3},{4,5},{6,7},{8,9},{10,11},{12,13},{14,15},{16,17},{18,... | collective-permute-start | bytes 140408 | tf_op jit(solution)/shard_map/ppermute | solution.py:24
  101.4 2.8 %copy-start.13 = (f32[32]{0:T(128)S(1)}, f32[32]{0:T(128)}, u32[]{:S(2)}) copy-start(f32[32]{0:T(128)} %get-tuple-element.51) | copy-start | bytes 388
  101.4 2.8 %copy-start.16 = (f32[5]{0:T(128)S(1)}, f32[5]{0:T(128)}, u32[]{:S(2)}) copy-start(f32[5]{0:T(128)} %param.11) | copy-start | bytes 64
  101.4 2.8 %copy-start.3 = (f32[5,32,18,1]{3,2,1,0:T(8,128)S(1)}, f32[5,32,18,1]{3,2,1,0:T(8,128)}, u32[]{:S(2)}) copy-start(f32[5,32,18,1]{3,2,1,0:T(8,128)} %copy.222) | copy-start | bytes 34564
  101.4 2.9 %copy-start.4 = (f32[5,32,18,1]{3,2,1,0:T(8,128)S(1)}, f32[5,32,18,1]{3,2,1,0:T(8,128)}, u32[]{:S(2)}) copy-start(f32[5,32,18,1]{3,2,1,0:T(8,128)} %copy.224) | copy-start | bytes 34564
  108.3 5.5 %copy-start.7 = (f32[5,32,16,128]{3,2,1,0:T(8,128)}, f32[5,32,16,128]{3,2,1,0:T(8,128)S(1)}, u32[]{:S(2)}) copy-start(f32[5,32,16,128]{3,2,1,0:T(8,128)S(1)} %fusion.1) | copy-start | bytes 3932164
  113.8 5.5 %copy-start.17 = (s32[16]{0:T(128)S(1)}, s32[16]{0:T(128)}, u32[]{:S(2)}) copy-start(s32[16]{0:T(128)} %dynamic-slice_subtract_fusion) | copy-start | bytes 196
  113.8 10.6 %copy-start.18 = (s32[4,4]{1,0:T(4,128)S(1)}, s32[4,4]{1,0:T(4,128)}, u32[]{:S(2)}) copy-start(s32[4,4]{1,0:T(4,128)} %multiply_add_fusion.2) | copy-start | bytes 196
  113.8 10.6 %copy-start.23 = (s32[16]{0:T(128)S(1)}, s32[16]{0:T(128)}, u32[]{:S(2)}) copy-start(s32[16]{0:T(128)} %dynamic_slice.10) | copy-start | bytes 196
  119.3 10.6 %copy-start.22 = (f32[2]{0:T(128)S(1)}, f32[2]{0:T(128)}, u32[]{:S(2)}) copy-start(f32[2]{0:T(128)} %broadcast_multiply_fusion) | copy-start | bytes 28
  119.3 18.7 %copy-start.14 = (f32[8,16,1]{1,0,2:T(8,128)S(1)}, f32[8,16,1]{1,0,2:T(8,128)}, u32[]{:S(2)}) copy-start(f32[8,16,1]{1,0,2:T(8,128)} %convolution_bitcast_fusion.1) | copy-start | bytes 1540
  120.1 9.8 %collective-permute-start.12 = (f32[1,5,4,16]{3,0,2,1:T(1,128)S(1)}, f32[1,5,4,16]{3,0,2,1:T(1,128)S(1)}, u32[]{:S(2)}, u32[]{:S(2)}) collective-permute-start(f32[1,5,4,16]{3,0,2,1:T(1,128)S(1)} %slice.242), channel_id=1, source_target_pairs={{0,4},{4,8},{8,12},{1,5},{5,9},{9,13},{2,6},{6,10},{10,14},{3,7},{... | collective-permute-start | bytes 3848 | tf_op jit(solution)/shard_map/ppermute | solution.py:36
  125.5 12.5 %all-to-all-start = ((f32[4,4,32,128]{3,1,2,0:T(4,128)}), f32[4,4,32,128]{3,1,2,0:T(4,128)S(1)}, u32[]{:S(2)}, u32[]{:S(2)}) async-start(f32[4,4,32,128]{3,1,2,0:T(4,128)} %fusion.9), calls=%async_computation | async-start | bytes 524288 | tf_op jit(solution)/shard_map/all_to_all | solution.py:104
where the time goes:
time: 140 us; the launch traced here: 139 us
  local copies, waits for them, and re-layouts  48.7 us (35%)
  starting transfers between devices  43 us (31%)
  other arithmetic  33.8 us (24%)
  waiting for transfers between devices  8.84 us (6%)
  matrix products  3.68 us (3%)
    ppermute x6, starting transfers between devices, padded_2(): lax.ppermute(tail, axis, [(i, (i + 1) % count) for i in range(ends)])  26.7 us
    slice x6, local copies, waits for them, and re-layouts, padded_2(): lax.slice_in_dim(cells, cells.shape[dim] - width, cells.shape[dim], axis=...  12.1 us
    ppermute x4, local copies, waits for them, and re-layouts, padded_2(): lax.ppermute(head, axis, [((i + 1) % count, i) for i in range(ends)])  9.21 us
    ppermute x4, local copies, waits for them, and re-layouts, padded_2(): lax.ppermute(tail, axis, [(i, (i + 1) % count) for i in range(ends)])  9.17 us
    ppermute x6, starting transfers between devices, padded_2(): lax.ppermute(head, axis, [((i + 1) % count, i) for i in range(ends)])  7.7 us
    all_to_all x1, waiting for transfers between devices, body(): lax.all_to_all(sent_factor, 'gx', split_axis=0, concat_axis=0, tiled=True)  7.36 us
    add x2, other arithmetic, tendency(): return -advect + diffusivity[:, None, None, None] * (beside - 6.0 * fields)  7.16 us
    concatenate x4, other arithmetic, padded_2(): jnp.concatenate([lax.ppermute(tail, axis, [(i, (i + 1) % count) for i in...  7.1 us
  transfers between devices with their start and end apart: 14, of which 2 were waited for; matrix products, arithmetic and copies ran while one was open for 22% of the time, Pallas kernels for 0%

commit v1 on v0

v1 whole, which is shorter than its diff:
```python
import functools

import jax
import jax.numpy as jnp
from jax import lax
from jax.experimental import pallas as pl
from jax.experimental.pallas import tpu as pltpu
from jax.sharding import PartitionSpec as P

FIELDS = 5
RATIO = 8
BMAX = 32
SLOTS = 8

TABLE = (0.4, 0.8, 1.3, 2.0)
STEP = 0.25

FRONT = 8
LANES = 128
F32 = jnp.float32

VM = pl.BlockSpec(memory_space=pltpu.VMEM)
SM = pl.BlockSpec(memory_space=pltpu.SMEM)


def in_vmem(array):
    return pltpu.with_memory_space_constraint(array, pltpu.VMEM)


class Dims:
    def __init__(self, levels, tiles, columns, all_tiles, n_gx, n_gy):
        self.levels, self.tiles, self.columns = levels, tiles, columns
        self.all_tiles, self.n_gx, self.n_gy = all_tiles, n_gx, n_gy
        self.block = FRONT + tiles
        self.pad_rows = FIELDS * (levels + 2) * self.block + 8
        self.capacity = (tiles + n_gx - 1) // n_gx
        self.per_group = LANES // (2 * levels)
        self.groups = -(-FIELDS // self.per_group)
        self.parents = tiles // RATIO
        self.y_sends = 1 if n_gy == 2 else 2


def base_row(d, f, z):
    return (f * (d.levels + 2) + z + 1) * d.block


def lane_of(d, f, z):
    return 2 * ((f % d.per_group) * d.levels + z)


def y_choices(d):
    if d.n_gy == 2:
        first = lax.axis_index("gy") == 0
        return [(jnp.where(first, d.columns - 1, 0), jnp.where(first, 1, 0))]
    return [(d.columns - 1, 1), (0, 0)]


def x_choices(d):
    even = lax.rem(lax.axis_index("gx"), 2) == 0
    return [jnp.where(even, d.tiles - 1, 0), jnp.where(even, 0, d.tiles - 1)]


def gather_y(d, accs, f, z, cells, lane):
    g = f // d.per_group
    for i, (column, side) in enumerate(y_choices(d)):
        place = lane_of(d, f, z) + side
        moved = pltpu.roll(cells, lax.rem(place - column + 2 * LANES, LANES), 1)
        accs[i][g] = jnp.where(lane == place, moved, accs[i][g])
    return accs


def pack_kernel(d, fields, pad, xa, xb, zface, *yq):
    lane = lax.broadcasted_iota(jnp.int32, (d.tiles, LANES), 1)
    zeros = jnp.zeros((d.tiles, LANES), F32)
    rows = d.levels * d.tiles

    def level(z, accs):
        accs = [list(a) for a in accs]
        for f in range(FIELDS):
            cells = fields[pl.ds(pl.multiple_of(f * rows + z * d.tiles, 8), d.tiles), :]
            pad[pl.ds(pl.multiple_of(base_row(d, f, z) + FRONT, 8), d.tiles), :] = cells
            accs = gather_y(d, accs, f, z, cells, lane)
        return tuple(tuple(a) for a in accs)

    accs = lax.fori_loop(
        0, d.levels, level, tuple(tuple(zeros for _ in range(d.groups)) for _ in range(d.y_sends)), unroll=2
    )
    for i in range(d.y_sends):
        for g in range(d.groups):
            yq[i][:, g * LANES : (g + 1) * LANES] = accs[i][g]
    for out, tile in zip((xa, xb), x_choices(d)):
        for f in range(FIELDS):
            out[f * d.levels : (f + 1) * d.levels, :] = pad[
                pl.ds(base_row(d, f, 0) + FRONT + tile, d.levels, stride=d.block), :
            ]
    z_out = jnp.where(lax.axis_index("gz") == 0, d.levels - 1, 0)
    for f in range(FIELDS):
        zface[f * d.tiles : (f + 1) * d.tiles, :] = fields[
            pl.ds(pl.multiple_of(f * rows + z_out * d.tiles, 8), d.tiles), :
        ]


def set_halos(d, pad, xa, xb, zface):
    me = lax.axis_index("gx")
    even = lax.rem(me, 2) == 0
    zero_x = jnp.zeros((d.levels, LANES), F32)
    for f in range(FIELDS):
        a = xa[f * d.levels : (f + 1) * d.levels, :]
        b = xb[f * d.levels : (f + 1) * d.levels, :]
        left = jnp.where(me == 0, zero_x, jnp.where(even, b, a))
        right = jnp.where(me == d.n_gx - 1, zero_x, jnp.where(even, a, b))
        pad[pl.ds(base_row(d, f, 0) + FRONT - 1, d.levels, stride=d.block), :] = left
        pad[pl.ds(base_row(d, f, 0) + d.block, d.levels, stride=d.block), :] = right
    low = lax.axis_index("gz") == 0
    zero_z = jnp.zeros((d.tiles, LANES), F32)
    for f in range(FIELDS):
        face = zface[f * d.tiles : (f + 1) * d.tiles, :]
        pad[pl.ds(base_row(d, f, -1) + FRONT, d.tiles), :] = jnp.where(low, zero_z, face)
        pad[pl.ds(base_row(d, f, d.levels) + FRONT, d.tiles), :] = jnp.where(low, face, zero_z)


def stencil(d, pad, yq, wind, diff, f, z, lane):
    base = base_row(d, f, z)
    v = pad[pl.ds(pl.multiple_of(base + FRONT, 8), d.tiles), :]
    xm = pad[pl.ds(base + FRONT - 1, d.tiles), :]
    xp = pad[pl.ds(base + FRONT + 1, d.tiles), :]
    zm = pad[pl.ds(pl.multiple_of(base + FRONT - d.block, 8), d.tiles), :]
    zp = pad[pl.ds(pl.multiple_of(base + FRONT + d.block, 8), d.tiles), :]
    g = f // d.per_group
    halo = yq[0][:, g * LANES : (g + 1) * LANES]
    if d.y_sends == 2:
        halo = halo + yq[1][:, g * LANES : (g + 1) * LANES]
    halo = pltpu.roll(halo, LANES - 1 - lane_of(d, f, z), 1)
    yp = jnp.where(lane == d.columns - 1, halo, pltpu.roll(v, LANES - 1, 1))
    ym = jnp.where(lane == 0, halo, pltpu.roll(v, 1, 1))
    spread = STEP * diff[f]
    wx = (0.5 * STEP) * wind[0, z]
    wy = (0.5 * STEP) * wind[1, z]
    wz = (0.5 * STEP) * wind[2, z]
    new = (1.0 - 6.0 * spread) * v
    new = new + ((spread - wx) * xp + (spread + wx) * xm)
    new = new + ((spread - wy) * yp + (spread + wy) * ym)
    new = new + ((spread - wz) * zp + (spread + wz) * zm)
    return v, new


def speed(u, v, w):
    return jnp.sqrt(u * u + v * v + w * w + 1.0)


def wall_coefficients(d, wall_type, count, slot_of):
    first_tile = lax.axis_index("gx") * d.tiles
    row = lax.broadcasted_iota(jnp.int32, (d.tiles, LANES), 0)
    strength = jnp.zeros((d.tiles, LANES), F32)
    for x in range(d.tiles):
        held = jnp.where(slot_of[first_tile + x] >= 0, count[x], 0).astype(F32) * (1.0 / BMAX)
        strength = jnp.where(row == x, held, strength)
    kind = wall_type[...]
    value = jnp.zeros((d.tiles, LANES), F32)
    for code, entry in enumerate(TABLE):
        value = jnp.where(kind == code, entry, value)
    return value * strength


def step_one_kernel(d, pad_in, xa, xb, zface, *refs):
    yq = refs[: d.y_sends]
    wall_type, wind, diff, count, slot_of = refs[d.y_sends : d.y_sends + 5]
    outs = refs[d.y_sends + 5 :]
    pad, new_pad, factor, xa_out, xb_out, z_out = outs[:6]
    yq_out = outs[6 : 6 + d.y_sends]
    stress = outs[6 + d.y_sends : 6 + d.y_sends + d.n_gx]
    table, tally = outs[6 + d.y_sends + d.n_gx :]
    set_halos(d, pad, xa, xb, zface)
    lane = lax.broadcasted_iota(jnp.int32, (d.tiles, LANES), 1)
    zeros = jnp.zeros((d.tiles, LANES), F32)
    coef = wall_coefficients(d, wall_type, count, slot_of)

    def level(z, accs):
        accs = [list(a) for a in accs]
        both = [stencil(d, pad, yq, wind, diff, f, z, lane) for f in range(FIELDS)]
        drag = STEP * (coef * speed(*(both[f][0] for f in range(3))))
        news = [both[f][1] - drag * both[f][0] if f < 3 else both[f][1] for f in range(FIELDS)]
        for f in range(FIELDS):
            new_pad[pl.ds(pl.multiple_of(base_row(d, f, z) + FRONT, 8), d.tiles), :] = news[f]
            accs = gather_y(d, accs, f, z, news[f], lane)
        factor[pl.ds(pl.multiple_of(z * d.tiles, 8), d.tiles), :] = coef * speed(*news[:3])
        return tuple(tuple(a) for a in accs)

    accs = lax.fori_loop(
        0, d.levels, level, tuple(tuple(zeros for _ in range(d.groups)) for _ in range(d.y_sends)), unroll=2
    )
    for i in range(d.y_sends):
        for g in range(d.groups):
            yq_out[i][:, g * LANES : (g + 1) * LANES] = accs[i][g]
    for out, tile in zip((xa_out, xb_out), x_choices(d)):
        for f in range(FIELDS):
            out[f * d.levels : (f + 1) * d.levels, :] = new_pad[
                pl.ds(base_row(d, f, 0) + FRONT + tile, d.levels, stride=d.block), :
            ]
    z_level = jnp.where(lax.axis_index("gz") == 0, d.levels - 1, 0)
    for f in range(FIELDS):
        z_out[f * d.tiles : (f + 1) * d.tiles, :] = new_pad[
            pl.ds(pl.multiple_of(base_row(d, f, z_level) + FRONT, 8), d.tiles), :
        ]
    me = lax.axis_index("gx")
    for k in range(d.n_gx):
        tally[k] = 0
    for i in range(d.n_gx * d.capacity):
        table[i] = 0
    for x in range(d.tiles):
        slot = slot_of[me * d.tiles + x]

        @pl.when(slot >= 0)
        def _():
            away = lax.rem(lax.shift_right_logical(slot, 3) - me + d.n_gx, d.n_gx)
            rank = tally[away]
            table[away * d.capacity + rank] = x
            tally[away] = rank + 1

    for k in range(d.n_gx):
        for c in range(d.capacity):
            tile = table[k * d.capacity + c]
            stress[k][c * d.levels : (c + 1) * d.levels, :] = factor[pl.ds(tile, d.levels, stride=d.tiles), :]


def step_two_kernel(d, pad_in, factor, xa, xb, zface, *refs):
    yq = refs[: d.y_sends]
    wind, diff, parent_of = refs[d.y_sends : d.y_sends + 3]
    pad, new_fields, own_sums, sent_sums, coarse = refs[d.y_sends + 3 :]
    set_halos(d, pad, xa, xb, zface)
    lane = lax.broadcasted_iota(jnp.int32, (d.tiles, LANES), 1)
    row = lax.broadcasted_iota(jnp.int32, (d.tiles, LANES), 0)
    zeros = jnp.zeros((d.tiles, LANES), F32)
    me = lax.axis_index("gx")
    held = jnp.full((d.tiles, LANES), -1, jnp.int32)
    for x in range(d.tiles):
        held = jnp.where(row == x, parent_of[me * d.tiles + x] - me * d.parents, held)
    masks = [jnp.where(held == p, 1.0, 0.0) for p in range(d.parents + 1)]
    coarse_levels = d.levels // RATIO
    coarse[...] = jnp.zeros_like(coarse)
    rows = d.levels * d.tiles
    per_parent = own_sums.shape[0] // d.parents

    def coarse_level(k, carry):
        def level(i, sums):
            z = k * RATIO + i
            drag = STEP * factor[pl.ds(pl.multiple_of(z * d.tiles, 8), d.tiles), :]
            added = []
            for f in range(FIELDS):
                v, new = stencil(d, pad, yq, wind, diff, f, z, lane)
                if f < 3:
                    new = new - drag * v
                new_fields[pl.ds(pl.multiple_of(f * rows + z * d.tiles, 8), d.tiles), :] = new
                added.append(sums[f] + new)
            return tuple(added)

        sums = lax.fori_loop(0, RATIO, level, (zeros,) * FIELDS, unroll=2)
        for p in range(d.parents + 1):
            for f in range(FIELDS):
                line = jnp.sum(sums[f] * masks[p], axis=0, keepdims=True)
                coarse[pl.ds(p * per_parent + f * coarse_levels + k, 1), :] = line
        return carry

    lax.fori_loop(0, coarse_levels, coarse_level, 0)
    pick_row = lax.broadcasted_iota(jnp.int32, (LANES, LANES), 0)
    pick_lane = lax.broadcasted_iota(jnp.int32, (LANES, LANES), 1)
    pick = jnp.where(pick_row // RATIO == pick_lane, 1.0, 0.0)
    summed = jnp.dot(coarse[...], pick, precision=lax.Precision.HIGHEST, preferred_element_type=F32)
    own_sums[...] = summed[: d.parents * per_parent, :]
    sent_sums[...] = summed[d.parents * per_parent :, :]


def place_kernel(d, own_sums, got_sums, slot_of, parent_of, *refs):
    stress = refs[: d.n_gx]
    wall_stress, parent_mean, gathered, table = refs[d.n_gx :]
    me = lax.axis_index("gx")
    part = d.capacity * d.levels
    for k in range(d.n_gx):
        gathered[k * part : (k + 1) * part, :] = stress[k][...]

    def source(s, carry):
        away = lax.rem(me - s + d.n_gx, d.n_gx)

        def tile(x, rank):
            slot = slot_of[s * d.tiles + x]
            mine = (slot >= 0) & (lax.shift_right_logical(slot, 3) == me)
            place = jnp.where(mine, slot - me * SLOTS, SLOTS)
            table[place] = away * d.capacity + rank
            return rank + mine.astype(jnp.int32)

        lax.fori_loop(0, d.tiles, tile, 0, unroll=True)
        return carry

    lax.fori_loop(0, d.n_gx, source, 0)
    for s in range(SLOTS):
        start = pl.multiple_of(table[s] * d.levels, 8)
        wall_stress[pl.ds(s, d.levels, stride=SLOTS), :] = gathered[pl.ds(start, d.levels), :]
    before = jnp.maximum(me - 1, 0) * d.tiles
    per_parent = own_sums.shape[0] // d.parents
    coarse_levels = d.levels // RATIO
    cells = d.columns // RATIO
    for p in range(d.parents):
        count = jnp.int32(0)
        for x in range(d.tiles):
            count = count + (parent_of[me * d.tiles + x] == me * d.parents + p).astype(jnp.int32)
            if p == 0:
                earlier = parent_of[before + x] == me * d.parents + p
                count = count + ((me > 0) & earlier).astype(jnp.int32)
        total = own_sums[p * per_parent : (p + 1) * per_parent, :]
        if p == 0:
            total = jnp.where(me == 0, total, total + got_sums[...])
        mean = total / (jnp.full(total.shape, count, jnp.int32).astype(F32) * (RATIO * RATIO))
        for f in range(FIELDS):
            parent_mean[p, f] = mean[f * coarse_levels : (f + 1) * coarse_levels, :cells]


def swapped(block, axis):
    return lax.ppermute(block, axis, [(i, i ^ 1) for i in range(lax.axis_size(axis))])


def swapped_between(block, axis):
    n = lax.axis_size(axis)
    other = lambda i: (i + 1) % n if i % 2 else (i - 1) % n
    return lax.ppermute(block, axis, [(i, other(i)) for i in range(n)])


def rotated(block, axis, distance):
    n = lax.axis_size(axis)
    return lax.ppermute(block, axis, [(i, (i + distance) % n) for i in range(n)])


def faces_swapped(d, xa, xb, zface, yq):
    xa = swapped(xa, "gx")
    xb = swapped_between(xb, "gx")
    if d.y_sends == 1:
        yq = [swapped(yq[0], "gy")]
    else:
        n = d.n_gy
        yq = [
            lax.ppermute(yq[0], "gy", [(i, i + 1) for i in range(n - 1)]),
            lax.ppermute(yq[1], "gy", [(i + 1, i) for i in range(n - 1)]),
        ]
    zface = swapped(zface, "gz")
    return [in_vmem(a) for a in (xa, xb, zface, *yq)]


def body(fields, parent_wind, diffusivity, wall_type, building_count, slot_of, parent_of):
    _, levels, tiles, columns = fields.shape
    d = Dims(levels, tiles, columns, slot_of.shape[0], lax.axis_size("gx"), lax.axis_size("gy"))
    assert columns == LANES and lax.axis_size("gz") == 2 and d.n_gx % 2 == 0
    params = pltpu.CompilerParams(vmem_limit_bytes=24 << 20)
    rows = FIELDS * levels * tiles
    pad_t = pltpu.VMEM((d.pad_rows, LANES), F32)
    x_t = pltpu.VMEM((FIELDS * levels, LANES), F32)
    z_t = pltpu.VMEM((FIELDS * tiles, LANES), F32)
    y_ts = [pltpu.VMEM((tiles, d.groups * LANES), F32)] * d.y_sends
    stress_t = pltpu.VMEM((d.capacity * levels, LANES), F32)

    pad, xa, xb, zface, *yq = pl.pallas_call(
        functools.partial(pack_kernel, d),
        out_shape=[pad_t, x_t, x_t, z_t, *y_ts],
        in_specs=[VM],
        out_specs=[VM] * (4 + d.y_sends),
        compiler_params=params,
        name="pack",
    )(fields.reshape(rows, LANES))
    faces = faces_swapped(d, xa, xb, zface, yq)

    n_out = 6 + d.y_sends + d.n_gx
    _, new_pad, factor, xa, xb, zface, *rest = pl.pallas_call(
        functools.partial(step_one_kernel, d),
        out_shape=[pad_t, pad_t, pltpu.VMEM(((levels + 1) * tiles, LANES), F32), x_t, x_t, z_t, *y_ts]
        + [stress_t] * d.n_gx,
        in_specs=[VM] * (5 + d.y_sends) + [SM] * 4,
        out_specs=[VM] * n_out,
        scratch_shapes=[pltpu.SMEM((d.n_gx * d.capacity,), jnp.int32), pltpu.SMEM((d.n_gx,), jnp.int32)],
        input_output_aliases={0: 0},
        compiler_params=params,
        name="step_one",
    )(in_vmem(pad), *faces, wall_type, parent_wind, diffusivity, building_count, slot_of)
    yq, stress = rest[: d.y_sends], rest[d.y_sends :]
    faces = faces_swapped(d, xa, xb, zface, yq)
    stress = [stress[0]] + [rotated(stress[k], "gx", k) for k in range(1, d.n_gx)]

    per_parent = -(-FIELDS * (levels // RATIO) // 8) * 8
    _, new_fields, own_sums, sent_sums = pl.pallas_call(
        functools.partial(step_two_kernel, d),
        out_shape=[
            pad_t,
            jax.ShapeDtypeStruct((rows, LANES), F32),
            pltpu.VMEM((d.parents * per_parent, LANES), F32),
            pltpu.VMEM((per_parent, LANES), F32),
        ],
        in_specs=[VM] * (5 + d.y_sends) + [SM] * 3,
        out_specs=[VM] * 4,
        scratch_shapes=[pltpu.VMEM(((d.parents + 1) * per_parent, LANES), F32)],
        input_output_aliases={0: 0},
        compiler_params=params,
        name="step_two",
    )(in_vmem(new_pad), in_vmem(factor), *faces, parent_wind, diffusivity, parent_of)
    got_sums = rotated(sent_sums, "gx", 1)

    wall_stress, parent_mean = pl.pallas_call(
        functools.partial(place_kernel, d),
        out_shape=[
            jax.ShapeDtypeStruct((levels * SLOTS, LANES), F32),
            jax.ShapeDtypeStruct((d.parents, FIELDS, levels // RATIO, columns // RATIO), F32),
        ],
        in_specs=[VM, VM, SM, SM] + [VM] * d.n_gx,
        out_specs=[VM, VM],
        scratch_shapes=[
            pltpu.VMEM((d.n_gx * d.capacity * levels, LANES), F32),
            pltpu.SMEM((SLOTS + 1,), jnp.int32),
        ],
        compiler_params=params,
        name="place",
    )(in_vmem(own_sums), in_vmem(got_sums), slot_of, parent_of, *[in_vmem(s) for s in stress])
    return (
        new_fields.reshape(fields.shape),
        wall_stress.reshape(levels, SLOTS, columns),
        parent_mean,
    )


def solution(mesh):
    in_specs = (
        P(None, "gz", ("groups", "gx"), "gy"),
        P(None, ("groups", "gz")),
        P(),
        P(("groups", "gx"), "gy"),
        P(("groups", "gx")),
        P("groups"),
        P("groups"),
    )
    out_specs = (
        P(None, "gz", ("groups", "gx"), "gy"),
        P("gz", ("groups", "gx"), "gy"),
        P(("groups", "gx"), None, "gz", "gy"),
    )
    return jax.shard_map(body, mesh=mesh, in_specs=in_specs, out_specs=out_specs, check_vma=False)
```

time: 140 us -> 41.9 us (0.30)
  local copies, waits for them, and re-layouts: 48.7 us -> 4.66 us
  other arithmetic: 33.8 us -> 0 us
  starting transfers between devices: 43 us -> 14.5 us
  Pallas kernels: 0 us -> 11.4 us
  matrix products: 3.68 us -> 0 us
  waiting for transfers between devices: 8.84 us -> 10.3 us
    ppermute x13 -> x12, starting transfers between devices: 38.7 us -> 14.5 us  [the longest x6 6.57 us: swapped(): lax.ppermute(block, axis, [(i, i ^ 1) for i in range(lax.axis_size(axis))])]
    ppermute x8 -> x0, local copies, waits for them, and re-layouts: 18.4 us -> none  [the longest x4 9.21 us: padded_2(): lax.ppermute(head, axis, [((i + 1) % count, i) for i in range(ends)])]
    slice x12 -> x0, local copies, waits for them, and re-layouts: 17.7 us -> none  [the longest x6 12.1 us: padded_2(): lax.slice_in_dim(cells, cells.shape[dim] - width, cells.shape[dim], axis=...]
    pallas_call x0 -> x4, Pallas kernels: none -> 11.4 us  [the longest x1 4.3 us: body(): pl.pallas_call(functools.partial(step_one_kernel, d), out_shape=[pad_t, p...]
    ppermute x13 -> x12, waiting for transfers between devices: 1.48 us -> 10.3 us  [the longest x4 5.48 us: rotated(): lax.ppermute(block, axis, [(i, (i + distance) % n) for i in range(n)])]
    add x9 -> x0, other arithmetic: 8.3 us -> none  [the longest x2 7.16 us: tendency(): return -advect + diffusivity[:, None, None, None] * (beside - 6.0 * fields)]
    all_to_all x1 -> x0, waiting for transfers between devices: 7.36 us -> none  [body(): lax.all_to_all(sent_factor, 'gx', split_axis=0, concat_axis=0, tiled=True)]
    concatenate x4 -> x0, other arithmetic: 7.1 us -> none  [padded_2(): jnp.concatenate([lax.ppermute(tail, axis, [(i, (i + 1) % count) for i in...]
  transfers between devices with their start and end apart: 14 -> 12, of which waited for: 2 -> 4; matrix products, arithmetic and copies ran while one was open for 22% -> 0% of each run, Pallas kernels for 0% -> 10%
where the time goes in v1:
time: 41.9 us; the launch traced here: 41.6 us
  starting transfers between devices  14.5 us (35%)
  Pallas kernels  11.4 us (27%)
  waiting for transfers between devices  10.3 us (25%)
  local copies, waits for them, and re-layouts  4.66 us (11%)
  between operations  0.7 us (2%)
    ppermute x6, starting transfers between devices, swapped(): lax.ppermute(block, axis, [(i, i ^ 1) for i in range(lax.axis_size(axis))])  6.57 us
    ppermute x4, waiting for transfers between devices, rotated(): lax.ppermute(block, axis, [(i, (i + distance) % n) for i in range(n)])  5.48 us
    ppermute x2, starting transfers between devices, swapped_between(): return lax.ppermute(block, axis, [(i, other(i)) for i in range(n)])  5.19 us
    unnamed x14, local copies, waits for them, and re-layouts  4.66 us
    ppermute x6, waiting for transfers between devices, swapped(): lax.ppermute(block, axis, [(i, i ^ 1) for i in range(lax.axis_size(axis))])  4.49 us
    pallas_call x1, Pallas kernels, body(): pl.pallas_call(functools.partial(step_one_kernel, d), out_shape=[pad_t, p...  4.3 us
    pallas_call x1, Pallas kernels, body(): pl.pallas_call(functools.partial(step_two_kernel, d), out_shape=[pad_t, j...  3.96 us
    ppermute x4, starting transfers between devices, rotated(): lax.ppermute(block, axis, [(i, (i + distance) % n) for i in range(n)])  2.75 us
  transfers between devices with their start and end apart: 12, of which 4 were waited for; matrix products, arithmetic and copies ran while one was open for 0% of the time, Pallas kernels for 10%

profile of v1, /device:TPU:0, one launch (start us, length us, event | category | flops | bytes accessed | tf_op | source)
XLA Modules:
  0.0 41.6 jit_solution(10098310939456408774)
XLA Ops:
  0.6 0.0 copy-start.4
  0.6 0.0 copy-start
  0.6 1.3 %copy-done = f32[5,32,16,128]{3,2,1,0:T(8,128)S(1)} copy-done((f32[5,32,16,128]{3,2,1,0:T(8,128)S(1)}, f32[5,32,16,128]{3,2,1,0:T(8,128)}, u32[]{:S(2)}) %copy-start) | copy-done | bytes 1310744
  2.0 1.6 %pack.1 = (f32[4088,128]{1,0:T(8,128)S(1)}, f32[160,128]{1,0:T(8,128)S(1)}, f32[160,128]{1,0:T(8,128)S(1)}, f32[80,128]{1,0:T(8,128)S(1)}, f32[16,384]{1,0:T(8,128)S(1)}) custom-call(f32[2560,128]{1,0:T(8,128)S(1)} %bitcast.3), custom_call_target="tpu_custom_call" | custom-call | tf_op jit(solution)/shard_map/pack/pallas_call | solution.py:359
  3.6 3.1 %collective-permute-start = (f32[160,128]{1,0:T(8,128)S(1)}, f32[160,128]{1,0:T(8,128)S(1)}, u32[]{:S(2)}, u32[]{:S(2)}) collective-permute-start(f32[160,128]{1,0:T(8,128)S(1)} %get-tuple-element.24), channel_id=1, source_target_pairs={{0,4},{4,0},{8,12},{12,8},{1,5},{5,1},{9,13},{13,9},{2,6},{6,2},{1... | collective-permute-start | bytes 245768 | tf_op jit(solution)/shard_map/ppermute | solution.py:318
  6.7 2.5 %collective-permute-start.1 = (f32[160,128]{1,0:T(8,128)S(1)}, f32[160,128]{1,0:T(8,128)S(1)}, u32[]{:S(2)}, u32[]{:S(2)}) collective-permute-start(f32[160,128]{1,0:T(8,128)S(1)} %get-tuple-element.25), channel_id=1, source_target_pairs={{0,12},{4,8},{8,4},{12,0},{1,13},{5,9},{9,5},{13,1},{2,14},{6,10},... | collective-permute-start | bytes 245768 | tf_op jit(solution)/shard_map/ppermute | solution.py:324
  9.1 0.0 collective-permute-start.2
  9.1 1.5 %collective-permute-start.3 = (f32[16,384]{1,0:T(8,128)S(1)}, f32[16,384]{1,0:T(8,128)S(1)}, u32[]{:S(2)}, u32[]{:S(2)}) collective-permute-start(f32[16,384]{1,0:T(8,128)S(1)} %get-tuple-element.27), channel_id=1, source_target_pairs={{0,2},{2,0},{1,3},{3,1},{4,6},{6,4},{5,7},{7,5},{8,10},{10,8},{9,1... | collective-permute-start | bytes 73736 | tf_op jit(solution)/shard_map/ppermute | solution.py:318
  10.6 2.3 %collective-permute-done.3.refs_0_ = f32[16,384]{1,0:T(8,128)S(1)} collective-permute-done((f32[16,384]{1,0:T(8,128)S(1)}, f32[16,384]{1,0:T(8,128)S(1)}, u32[]{:S(2)}, u32[]{:S(2)}) %collective-permute-start.3) | collective-permute-done | bytes 24608 | tf_op jit(solution)/shard_map/ppermute | solution.py:318
  13.0 0.0 collective-permute-done.2.zface
  13.0 0.0 collective-permute-done.xa
  13.0 0.3 collective-permute-done.1.xb
  13.3 0.0 copy-start.1
  13.3 0.7 %copy-done.1 = s32[16,128]{1,0:T(8,128)S(1)} copy-done((s32[16,128]{1,0:T(8,128)S(1)}, s32[16,128]{1,0:T(8,128)}, u32[]{:S(2)}) %copy-start.1) | copy-done | bytes 8216
  14.0 0.0 copy-start.2
  14.0 0.7 %copy-done.2 = f32[3,32]{1,0:T(4,128)S(1)} copy-done((f32[3,32]{1,0:T(4,128)S(1)}, f32[3,32]{1,0:T(4,128)}, u32[]{:S(2)}) %copy-start.2) | copy-done | bytes 408
  14.7 0.0 copy-start.3
  14.7 0.7 %copy-done.3 = s32[64]{0:T(128)S(1)} copy-done((s32[64]{0:T(128)S(1)}, s32[64]{0:T(128)}, u32[]{:S(2)}) %copy-start.3) | copy-done | bytes 280
  15.3 0.0 copy-start.5
  15.3 0.7 %copy-done.5 = f32[5]{0:T(128)S(1)} copy-done((f32[5]{0:T(128)S(1)}, f32[5]{0:T(128)}, u32[]{:S(2)}) %copy-start.5) | copy-done | bytes 44
  16.0 0.0 copy-start.6
  16.0 0.7 %copy-done.6 = s32[16]{0:T(128)S(1)} copy-done((s32[16]{0:T(128)S(1)}, s32[16]{0:T(128)}, u32[]{:S(2)}) %copy-start.6) | copy-done | bytes 88
  16.6 4.3 %step_one.1 = (f32[4088,128]{1,0:T(8,128)S(1)}, f32[4088,128]{1,0:T(8,128)S(1)}, f32[528,128]{1,0:T(8,128)S(1)}, f32[160,128]{1,0:T(8,128)S(1)}, f32[160,128]{1,...) custom-call(f32[4088,128]{1,0:T(8,128)S(1)} %get-tuple-element.23.pa, ...), custom_call_target="tpu_custom_call", output_to_operand_aliasing={{0}: (0, {})} | custom-call | tf_op jit(solution)/shard_map/step_one/pallas_call | solution.py:370
  20.9 0.1 collective-permute-start.6
  21.0 0.4 %collective-permute-start.4 = (f32[160,128]{1,0:T(8,128)S(1)}, f32[160,128]{1,0:T(8,128)S(1)}, u32[]{:S(2)}, u32[]{:S(2)}) collective-permute-start(f32[160,128]{1,0:T(8,128)S(1)} %get-tuple-element.30), channel_id=1, source_target_pairs={{0,4},{4,0},{8,12},{12,8},{1,5},{5,1},{9,13},{13,9},{2,6},{6,2},{1... | collective-permute-start | bytes 245768 | tf_op jit(solution)/shard_map/ppermute | solution.py:318
  21.5 2.7 %collective-permute-start.5 = (f32[160,128]{1,0:T(8,128)S(1)}, f32[160,128]{1,0:T(8,128)S(1)}, u32[]{:S(2)}, u32[]{:S(2)}) collective-permute-start(f32[160,128]{1,0:T(8,128)S(1)} %get-tuple-element.31), channel_id=1, source_target_pairs={{0,12},{4,8},{8,4},{12,0},{1,13},{5,9},{9,5},{13,1},{2,14},{6,10},... | collective-permute-start | bytes 245768 | tf_op jit(solution)/shard_map/ppermute | solution.py:324
  24.2 1.5 %collective-permute-start.7 = (f32[16,384]{1,0:T(8,128)S(1)}, f32[16,384]{1,0:T(8,128)S(1)}, u32[]{:S(2)}, u32[]{:S(2)}) collective-permute-start(f32[16,384]{1,0:T(8,128)S(1)} %get-tuple-element.33), channel_id=1, source_target_pairs={{0,2},{2,0},{1,3},{3,1},{4,6},{6,4},{5,7},{7,5},{8,10},{10,8},{9,1... | collective-permute-start | bytes 73736 | tf_op jit(solution)/shard_map/ppermute | solution.py:318
  25.7 0.2 collective-permute-start.9
  25.8 2.1 %collective-permute-done.7.refs_0_ = f32[16,384]{1,0:T(8,128)S(1)} collective-permute-done((f32[16,384]{1,0:T(8,128)S(1)}, f32[16,384]{1,0:T(8,128)S(1)}, u32[]{:S(2)}, u32[]{:S(2)}) %collective-permute-start.7) | collective-permute-done | bytes 24608 | tf_op jit(solution)/shard_map/ppermute | solution.py:318
  28.0 0.4 %collective-permute-start.10 = (f32[128,128]{1,0:T(8,128)S(1)}, f32[128,128]{1,0:T(8,128)S(1)}, u32[]{:S(2)}, u32[]{:S(2)}) collective-permute-start(f32[128,128]{1,0:T(8,128)S(1)} %get-tuple-element.39), channel_id=1, source_target_pairs={{0,8},{4,12},{8,0},{12,4},{1,9},{5,13},{9,1},{13,5},{2,10},{6,14},... | collective-permute-start | bytes 196616 | tf_op jit(solution)/shard_map/ppermute | solution.py:329
  28.4 0.0 collective-permute-done.6.zface
  28.4 2.1 %collective-permute-start.11 = (f32[128,128]{1,0:T(8,128)S(1)}, f32[128,128]{1,0:T(8,128)S(1)}, u32[]{:S(2)}, u32[]{:S(2)}) collective-permute-start(f32[128,128]{1,0:T(8,128)S(1)} %get-tuple-element.40), channel_id=1, source_target_pairs={{0,12},{4,0},{8,4},{12,8},{1,13},{5,1},{9,5},{13,9},{2,14},{6,2},{... | collective-permute-start | bytes 196616 | tf_op jit(solution)/shard_map/ppermute | solution.py:329
  30.5 0.0 collective-permute-done.4.xa
  30.6 0.0 collective-permute-done.5.xb
  30.6 0.0 copy-done.4
  30.6 4.0 %step_two.1 = (f32[4088,128]{1,0:T(8,128)S(1)}, f32[2560,128]{1,0:T(8,128)}, f32[48,128]{1,0:T(8,128)S(1)}, f32[24,128]{1,0:T(8,128)S(1)}) custom-call(f32[4088,128]{1,0:T(8,128)S(1)} %get-tuple-element.28.pad_in, f32[528,128]{1,0:T(8,128)S(1)} %get-tuple-element.29.factor, ...), custom_call_target="tpu_custom_call", output_to_operand_aliasing={{0}: (0, {})} | custom-call | tf_op jit(solution)/shard_map/step_two/pallas_call | solution.py:386
  34.5 0.0 collective-permute-start.8
  34.5 0.0 collective-permute-done.9.refs_1_
  34.5 0.0 collective-permute-done.10.refs_2_
  34.5 0.0 collective-permute-done.11.refs_3_
  34.5 5.5 %collective-permute-done.8.got_sums = f32[24,128]{1,0:T(8,128)S(1)} collective-permute-done((f32[24,128]{1,0:T(8,128)S(1)}, f32[24,128]{1,0:T(8,128)S(1)}, u32[]{:S(2)}, u32[]{:S(2)}) %collective-permute-start.8) | collective-permute-done | bytes 12320 | tf_op jit(solution)/shard_map/ppermute | solution.py:329
  40.0 1.6 %place.1 = (f32[256,128]{1,0:T(8,128)}, f32[2,5,4,16]{3,2,1,0:T(4,128)}) custom-call(f32[48,128]{1,0:T(8,128)S(1)} %get-tuple-element.35.own_sums, f32[24,128]{1,0:T(8,128)S(1)} %collective-permute-done.8.got_sums, s32[64]{0:T(128)S(1)} %copy-done.3, s32[64]{0:T(128)S(1)} %copy-done.4, f32[128,128]{1,0:T(8,128)S(1)} %get-tuple-element.37.refs_0_, ...), custom_call_target="tpu_custom_call" | custom-call | tf_op jit(solution)/shard_map/place/pallas_call | solution.py:403
Async XLA Ops:
  0.6 29.9 %copy-start.4 = (s32[64]{0:T(128)S(1)}, s32[64]{0:T(128)}, u32[]{:S(2)}) copy-start(s32[64]{0:T(128)} %parent_of.1) | copy-start | bytes 772
  0.6 1.3 %copy-start = (f32[5,32,16,128]{3,2,1,0:T(8,128)S(1)}, f32[5,32,16,128]{3,2,1,0:T(8,128)}, u32[]{:S(2)}) copy-start(f32[5,32,16,128]{3,2,1,0:T(8,128)} %param.7) | copy-start | bytes 3932164
  3.6 9.4 %collective-permute-start = (f32[160,128]{1,0:T(8,128)S(1)}, f32[160,128]{1,0:T(8,128)S(1)}, u32[]{:S(2)}, u32[]{:S(2)}) collective-permute-start(f32[160,128]{1,0:T(8,128)S(1)} %get-tuple-element.24), channel_id=1, source_target_pairs={{0,4},{4,0},{8,12},{12,8},{1,5},{5,1},{9,13},{13,9},{2,6},{6,2},{1... | collective-permute-start | bytes 245768 | tf_op jit(solution)/shard_map/ppermute | solution.py:318
  6.7 6.6 %collective-permute-start.1 = (f32[160,128]{1,0:T(8,128)S(1)}, f32[160,128]{1,0:T(8,128)S(1)}, u32[]{:S(2)}, u32[]{:S(2)}) collective-permute-start(f32[160,128]{1,0:T(8,128)S(1)} %get-tuple-element.25), channel_id=1, source_target_pairs={{0,12},{4,8},{8,4},{12,0},{1,13},{5,9},{9,5},{13,1},{2,14},{6,10},... | collective-permute-start | bytes 245768 | tf_op jit(solution)/shard_map/ppermute | solution.py:324
  9.1 3.8 %collective-permute-start.2 = (f32[80,128]{1,0:T(8,128)S(1)}, f32[80,128]{1,0:T(8,128)S(1)}, u32[]{:S(2)}, u32[]{:S(2)}) collective-permute-start(f32[80,128]{1,0:T(8,128)S(1)} %get-tuple-element.26), channel_id=1, source_target_pairs={{0,1},{1,0},{2,3},{3,2},{4,5},{5,4},{6,7},{7,6},{8,9},{9,8},{10,11... | collective-permute-start | bytes 122888 | tf_op jit(solution)/shard_map/ppermute | solution.py:318
  9.1 3.8 %collective-permute-start.3 = (f32[16,384]{1,0:T(8,128)S(1)}, f32[16,384]{1,0:T(8,128)S(1)}, u32[]{:S(2)}, u32[]{:S(2)}) collective-permute-start(f32[16,384]{1,0:T(8,128)S(1)} %get-tuple-element.27), channel_id=1, source_target_pairs={{0,2},{2,0},{1,3},{3,1},{4,6},{6,4},{5,7},{7,5},{8,10},{10,8},{9,1... | collective-permute-start | bytes 73736 | tf_op jit(solution)/shard_map/ppermute | solution.py:318
  13.3 0.7 %copy-start.1 = (s32[16,128]{1,0:T(8,128)S(1)}, s32[16,128]{1,0:T(8,128)}, u32[]{:S(2)}) copy-start(s32[16,128]{1,0:T(8,128)} %refs_1_.2) | copy-start | bytes 24580
  14.0 0.7 %copy-start.2 = (f32[3,32]{1,0:T(4,128)S(1)}, f32[3,32]{1,0:T(4,128)}, u32[]{:S(2)}) copy-start(f32[3,32]{1,0:T(4,128)} %refs_1_.3) | copy-start | bytes 1156
  14.7 0.7 %copy-start.3 = (s32[64]{0:T(128)S(1)}, s32[64]{0:T(128)}, u32[]{:S(2)}) copy-start(s32[64]{0:T(128)} %slot_of.1) | copy-start | bytes 772
  15.3 0.7 %copy-start.5 = (f32[5]{0:T(128)S(1)}, f32[5]{0:T(128)}, u32[]{:S(2)}) copy-start(f32[5]{0:T(128)} %refs_2_.3) | copy-start | bytes 64
  16.0 0.7 %copy-start.6 = (s32[16]{0:T(128)S(1)}, s32[16]{0:T(128)}, u32[]{:S(2)}) copy-start(s32[16]{0:T(128)} %refs_4_.1) | copy-start | bytes 196
  20.9 7.5 %collective-permute-start.6 = (f32[80,128]{1,0:T(8,128)S(1)}, f32[80,128]{1,0:T(8,128)S(1)}, u32[]{:S(2)}, u32[]{:S(2)}) collective-permute-start(f32[80,128]{1,0:T(8,128)S(1)} %get-tuple-element.32), channel_id=1, source_target_pairs={{0,1},{1,0},{2,3},{3,2},{4,5},{5,4},{6,7},{7,6},{8,9},{9,8},{10,11... | collective-permute-start | bytes 122888 | tf_op jit(solution)/shard_map/ppermute | solution.py:318
  21.0 9.5 %collective-permute-start.4 = (f32[160,128]{1,0:T(8,128)S(1)}, f32[160,128]{1,0:T(8,128)S(1)}, u32[]{:S(2)}, u32[]{:S(2)}) collective-permute-start(f32[160,128]{1,0:T(8,128)S(1)} %get-tuple-element.30), channel_id=1, source_target_pairs={{0,4},{4,0},{8,12},{12,8},{1,5},{5,1},{9,13},{13,9},{2,6},{6,2},{1... | collective-permute-start | bytes 245768 | tf_op jit(solution)/shard_map/ppermute | solution.py:318
  21.5 9.1 %collective-permute-start.5 = (f32[160,128]{1,0:T(8,128)S(1)}, f32[160,128]{1,0:T(8,128)S(1)}, u32[]{:S(2)}, u32[]{:S(2)}) collective-permute-start(f32[160,128]{1,0:T(8,128)S(1)} %get-tuple-element.31), channel_id=1, source_target_pairs={{0,12},{4,8},{8,4},{12,0},{1,13},{5,9},{9,5},{13,1},{2,14},{6,10},... | collective-permute-start | bytes 245768 | tf_op jit(solution)/shard_map/ppermute | solution.py:324
  24.2 3.8 %collective-permute-start.7 = (f32[16,384]{1,0:T(8,128)S(1)}, f32[16,384]{1,0:T(8,128)S(1)}, u32[]{:S(2)}, u32[]{:S(2)}) collective-permute-start(f32[16,384]{1,0:T(8,128)S(1)} %get-tuple-element.33), channel_id=1, source_target_pairs={{0,2},{2,0},{1,3},{3,1},{4,6},{6,4},{5,7},{7,5},{8,10},{10,8},{9,1... | collective-permute-start | bytes 73736 | tf_op jit(solution)/shard_map/ppermute | solution.py:318
  25.7 8.9 %collective-permute-start.9 = (f32[128,128]{1,0:T(8,128)S(1)}, f32[128,128]{1,0:T(8,128)S(1)}, u32[]{:S(2)}, u32[]{:S(2)}) collective-permute-start(f32[128,128]{1,0:T(8,128)S(1)} %get-tuple-element.38), channel_id=1, source_target_pairs={{0,4},{4,8},{8,12},{12,0},{1,5},{5,9},{9,13},{13,1},{2,6},{6,10},{... | collective-permute-start | bytes 196616 | tf_op jit(solution)/shard_map/ppermute | solution.py:329
  28.0 6.5 %collective-permute-start.10 = (f32[128,128]{1,0:T(8,128)S(1)}, f32[128,128]{1,0:T(8,128)S(1)}, u32[]{:S(2)}, u32[]{:S(2)}) collective-permute-start(f32[128,128]{1,0:T(8,128)S(1)} %get-tuple-element.39), channel_id=1, source_target_pairs={{0,8},{4,12},{8,0},{12,4},{1,9},{5,13},{9,1},{13,5},{2,10},{6,14},... | collective-permute-start | bytes 196616 | tf_op jit(solution)/shard_map/ppermute | solution.py:329
  28.4 6.1 %collective-permute-start.11 = (f32[128,128]{1,0:T(8,128)S(1)}, f32[128,128]{1,0:T(8,128)S(1)}, u32[]{:S(2)}, u32[]{:S(2)}) collective-permute-start(f32[128,128]{1,0:T(8,128)S(1)} %get-tuple-element.40), channel_id=1, source_target_pairs={{0,12},{4,0},{8,4},{12,8},{1,13},{5,1},{9,5},{13,9},{2,14},{6,2},{... | collective-permute-start | bytes 196616 | tf_op jit(solution)/shard_map/ppermute | solution.py:329
  34.5 5.5 %collective-permute-start.8 = (f32[24,128]{1,0:T(8,128)S(1)}, f32[24,128]{1,0:T(8,128)S(1)}, u32[]{:S(2)}, u32[]{:S(2)}) collective-permute-start(f32[24,128]{1,0:T(8,128)S(1)} %get-tuple-element.36), channel_id=1, source_target_pairs={{0,4},{4,8},{8,12},{12,0},{1,5},{5,9},{9,13},{13,1},{2,6},{6,10},{... | collective-permute-start | bytes 36872 | tf_op jit(solution)/shard_map/ppermute | solution.py:329

commit v2 on v1

--- a/solution.py
+++ b/solution.py
@@ -21,6 +21,10 @@
 
 VM = pl.BlockSpec(memory_space=pltpu.VMEM)
 SM = pl.BlockSpec(memory_space=pltpu.SMEM)
+
+
+def in_hbm(array):
+    return pltpu.with_memory_space_constraint(array, pltpu.HBM)
 
 
 def in_vmem(array):
@@ -48,56 +52,64 @@
     return 2 * ((f % d.per_group) * d.levels + z)
 
 
-def y_choices(d):
-    if d.n_gy == 2:
-        first = lax.axis_index("gy") == 0
-        return [(jnp.where(first, d.columns - 1, 0), jnp.where(first, 1, 0))]
-    return [(d.columns - 1, 1), (0, 0)]
-
-
 def x_choices(d):
     even = lax.rem(lax.axis_index("gx"), 2) == 0
     return [jnp.where(even, d.tiles - 1, 0), jnp.where(even, 0, d.tiles - 1)]
 
 
-def gather_y(d, accs, f, z, cells, lane):
+def add_edges(d, packed, pad, f, lane):
+    pair = lax.rem(lax.shift_right_logical(lane + 1, 1), LANES // 2)
     g = f // d.per_group
-    for i, (column, side) in enumerate(y_choices(d)):
-        place = lane_of(d, f, z) + side
-        moved = pltpu.roll(cells, lax.rem(place - column + 2 * LANES, LANES), 1)
-        accs[i][g] = jnp.where(lane == place, moved, accs[i][g])
-    return accs
-
-
-def pack_kernel(d, fields, pad, xa, xb, zface, *yq):
+    for z in range(d.levels):
+        cells = pad[pl.ds(base_row(d, f, z) + FRONT, d.tiles), :]
+        place = lane_of(d, f, z)
+        moved = pltpu.roll(cells, place, 1) if place else cells
+        packed[g] = jnp.where(pair == place // 2, moved, packed[g])
+    return packed
+
+
+def write_y(d, outs, packed, lane):
+    odd = lax.rem(lane, 2) == 1
+    first = lax.axis_index("gy") == 0
+    for g in range(d.groups):
+        tail = pltpu.roll(jnp.where(odd, packed[g], 0.0), 2, 1)
+        head = jnp.where(odd, 0.0, packed[g])
+        messages = [jnp.where(first, tail, head)] if d.y_sends == 1 else [tail, head]
+        for out, message in zip(outs, messages):
+            out[:, g * LANES : (g + 1) * LANES] = message
+
+
+def pack_kernel(d, fields, *refs):
+    n_small = len(refs[: (len(refs) - 5 - d.y_sends) // 2])
+    small, refs = refs[:n_small], refs[n_small:]
+    small_out, (pad, xa, xb, zface), yq = refs[:n_small], refs[n_small : n_small + 4], refs[n_small + 4 : -1]
+    sems = refs[-1]
     lane = lax.broadcasted_iota(jnp.int32, (d.tiles, LANES), 1)
-    zeros = jnp.zeros((d.tiles, LANES), F32)
-    rows = d.levels * d.tiles
-
-    def level(z, accs):
-        accs = [list(a) for a in accs]
-        for f in range(FIELDS):
-            cells = fields[pl.ds(pl.multiple_of(f * rows + z * d.tiles, 8), d.tiles), :]
-            pad[pl.ds(pl.multiple_of(base_row(d, f, z) + FRONT, 8), d.tiles), :] = cells
-            accs = gather_y(d, accs, f, z, cells, lane)
-        return tuple(tuple(a) for a in accs)
-
-    accs = lax.fori_loop(
-        0, d.levels, level, tuple(tuple(zeros for _ in range(d.groups)) for _ in range(d.y_sends)), unroll=2
-    )
-    for i in range(d.y_sends):
-        for g in range(d.groups):
-            yq[i][:, g * LANES : (g + 1) * LANES] = accs[i][g]
-    for out, tile in zip((xa, xb), x_choices(d)):
-        for f in range(FIELDS):
+    copies = []
+    for f in range(FIELDS):
+        blocks = pad.at[pl.ds(base_row(d, f, 0), d.levels * d.block), :].reshape(d.levels, d.block, LANES)
+        copies.append(pltpu.make_async_copy(fields.at[f], blocks.at[:, pl.ds(FRONT, d.tiles), :], sems.at[f]))
+    moves = [
+        pltpu.make_async_copy(source, target, sems.at[FIELDS + i])
+        for i, (source, target) in enumerate(zip(small, small_out))
+    ]
+    for copy in copies + moves:
+        copy.start()
+    z_out = jnp.where(lax.axis_index("gz") == 0, d.levels - 1, 0)
+    packed = [jnp.zeros((d.tiles, LANES), F32)] * d.groups
+    for f in range(FIELDS):
+        copies[f].wait()
+        packed = add_edges(d, packed, pad, f, lane)
+        for out, tile in zip((xa, xb), x_choices(d)):
             out[f * d.levels : (f + 1) * d.levels, :] = pad[
                 pl.ds(base_row(d, f, 0) + FRONT + tile, d.levels, stride=d.block), :
             ]
-    z_out = jnp.where(lax.axis_index("gz") == 0, d.levels - 1, 0)
-    for f in range(FIELDS):
-        zface[f * d.tiles : (f + 1) * d.tiles, :] = fields[
-            pl.ds(pl.multiple_of(f * rows + z_out * d.tiles, 8), d.tiles), :
+        zface[f * d.tiles : (f + 1) * d.tiles, :] = pad[
+            pl.ds(pl.multiple_of(base_row(d, f, z_out) + FRONT, 8), d.tiles), :
         ]
+    write_y(d, yq, packed, lane)
+    for copy in moves:
+        copy.wait()
 
 
 def set_halos(d, pad, xa, xb, zface):
@@ -175,23 +187,20 @@
     zeros = jnp.zeros((d.tiles, LANES), F32)
     coef = wall_coefficients(d, wall_type, count, slot_of)
 
-    def level(z, accs):
-        accs = [list(a) for a in accs]
+    def level(z, carry):
         both = [stencil(d, pad, yq, wind, diff, f, z, lane) for f in range(FIELDS)]
         drag = STEP * (coef * speed(*(both[f][0] for f in range(3))))
         news = [both[f][1] - drag * both[f][0] if f < 3 else both[f][1] for f in range(FIELDS)]
         for f in range(FIELDS):
             new_pad[pl.ds(pl.multiple_of(base_row(d, f, z) + FRONT, 8), d.tiles), :] = news[f]
-            accs = gather_y(d, accs, f, z, news[f], lane)
         factor[pl.ds(pl.multiple_of(z * d.tiles, 8), d.tiles), :] = coef * speed(*news[:3])
-        return tuple(tuple(a) for a in accs)
-
-    accs = lax.fori_loop(
-        0, d.levels, level, tuple(tuple(zeros for _ in range(d.groups)) for _ in range(d.y_sends)), unroll=2
-    )
-    for i in range(d.y_sends):
-        for g in range(d.groups):
-            yq_out[i][:, g * LANES : (g + 1) * LANES] = accs[i][g]
+        return carry
+
+    lax.fori_loop(0, d.levels, level, 0, unroll=8)
+    packed = [zeros] * d.groups
+    for f in range(FIELDS):
+        packed = add_edges(d, packed, new_pad, f, lane)
+    write_y(d, yq_out, packed, lane)
     for out, tile in zip((xa_out, xb_out), x_choices(d)):
         for f in range(FIELDS):
             out[f * d.levels : (f + 1) * d.levels, :] = new_pad[
@@ -254,7 +263,7 @@
                 added.append(sums[f] + new)
             return tuple(added)
 
-        sums = lax.fori_loop(0, RATIO, level, (zeros,) * FIELDS, unroll=2)
+        sums = lax.fori_loop(0, RATIO, level, (zeros,) * FIELDS, unroll=8)
         for p in range(d.parents + 1):
             for f in range(FIELDS):
                 line = jnp.sum(sums[f] * masks[p], axis=0, keepdims=True)
@@ -349,6 +358,7 @@
     d = Dims(levels, tiles, columns, slot_of.shape[0], lax.axis_size("gx"), lax.axis_size("gy"))
     assert columns == LANES and lax.axis_size("gz") == 2 and d.n_gx % 2 == 0
     params = pltpu.CompilerParams(vmem_limit_bytes=24 << 20)
+    small = [in_hbm(a) for a in (wall_type, parent_wind, diffusivity, building_count, slot_of, parent_of)]
     rows = FIELDS * levels * tiles
     pad_t = pltpu.VMEM((d.pad_rows, LANES), F32)
     x_t = pltpu.VMEM((FIELDS * levels, LANES), F32)
@@ -356,14 +366,18 @@
     y_ts = [pltpu.VMEM((tiles, d.groups * LANES), F32)] * d.y_sends
     stress_t = pltpu.VMEM((d.capacity * levels, LANES), F32)
 
-    pad, xa, xb, zface, *yq = pl.pallas_call(
+    n_small = len(small)
+    *small, pad, xa, xb, zface = (packed := pl.pallas_call(
         functools.partial(pack_kernel, d),
-        out_shape=[pad_t, x_t, x_t, z_t, *y_ts],
-        in_specs=[VM],
-        out_specs=[VM] * (4 + d.y_sends),
+        out_shape=[pltpu.SMEM(a.shape, a.dtype) if a.shape != wall_type.shape else pltpu.VMEM(a.shape, a.dtype) for a in small]
+        + [pad_t, x_t, x_t, z_t, *y_ts],
+        in_specs=[pl.BlockSpec(memory_space=pltpu.HBM)] * (1 + n_small),
+        out_specs=[VM] + [SM] * (n_small - 1) + [VM] * (4 + d.y_sends),
+        scratch_shapes=[pltpu.SemaphoreType.DMA((FIELDS + n_small,))],
         compiler_params=params,
         name="pack",
-    )(fields.reshape(rows, LANES))
+    )(in_hbm(fields), *small))[: n_small + 4]
+    yq = packed[n_small + 4 :]
     faces = faces_swapped(d, xa, xb, zface, yq)
 
     n_out = 6 + d.y_sends + d.n_gx
@@ -377,7 +391,7 @@
         input_output_aliases={0: 0},
         compiler_params=params,
         name="step_one",
-    )(in_vmem(pad), *faces, wall_type, parent_wind, diffusivity, building_count, slot_of)
+    )(in_vmem(pad), *faces, *small[:5])
     yq, stress = rest[: d.y_sends], rest[d.y_sends :]
     faces = faces_swapped(d, xa, xb, zface, yq)
     stress = [stress[0]] + [rotated(stress[k], "gx", k) for k in range(1, d.n_gx)]
@@ -397,7 +411,7 @@
         input_output_aliases={0: 0},
         compiler_params=params,
         name="step_two",
-    )(in_vmem(new_pad), in_vmem(factor), *faces, parent_wind, diffusivity, parent_of)
+    )(in_vmem(new_pad), in_vmem(factor), *faces, small[1], small[2], small[5])
     got_sums = rotated(sent_sums, "gx", 1)
 
     wall_stress, parent_mean = pl.pallas_call(
@@ -414,7 +428,7 @@
         ],
         compiler_params=params,
         name="place",
-    )(in_vmem(own_sums), in_vmem(got_sums), slot_of, parent_of, *[in_vmem(s) for s in stress])
+    )(in_vmem(own_sums), in_vmem(got_sums), small[4], small[5], *[in_vmem(s) for s in stress])
     return (
         new_fields.reshape(fields.shape),
         wall_stress.reshape(levels, SLOTS, columns),

time: 41.9 us -> 33 us (0.79)
  local copies, waits for them, and re-layouts: 4.66 us -> 0 us
  Pallas kernels: 11.4 us -> 7.4 us
    unnamed x14 -> x0, local copies, waits for them, and re-layouts: 4.66 us -> none
    pallas_call x1, Pallas kernels: 4.3 us -> 2.04 us  [body(): pl.pallas_call(functools.partial(step_one_kernel, d), out_shape=[pad_t, p...]
    pallas_call x1, Pallas kernels: 3.96 us -> 2.45 us  [body(): pl.pallas_call(functools.partial(step_two_kernel, d), out_shape=[pad_t, j...]
    pallas_call x1, Pallas kernels: 1.57 us -> 1.02 us  [body(): pl.pallas_call(functools.partial(place_kernel, d), out_shape=[jax.ShapeDt...]
  transfers between devices with their start and end apart: 12 -> 12, of which waited for: 4 -> 5; matrix products, arithmetic and copies ran while one was open for 0% -> 0% of each run, Pallas kernels for 10% -> 7%
where the time goes in v2:
time: 33 us; the launch traced here: 32.9 us
  starting transfers between devices  14.5 us (44%)
  waiting for transfers between devices  10.3 us (31%)
  Pallas kernels  7.4 us (22%)
  between operations  0.67 us (2%)
    ppermute x6, starting transfers between devices, swapped(): lax.ppermute(block, axis, [(i, i ^ 1) for i in range(lax.axis_size(axis))])  6.59 us
    ppermute x4, waiting for transfers between devices, rotated(): lax.ppermute(block, axis, [(i, (i + distance) % n) for i in range(n)])  5.49 us
    ppermute x2, starting transfers between devices, swapped_between(): return lax.ppermute(block, axis, [(i, other(i)) for i in range(n)])  5.17 us
    ppermute x6, waiting for transfers between devices, swapped(): lax.ppermute(block, axis, [(i, i ^ 1) for i in range(lax.axis_size(axis))])  4.49 us
    ppermute x4, starting transfers between devices, rotated(): lax.ppermute(block, axis, [(i, (i + distance) % n) for i in range(n)])  2.75 us
    pallas_call x1, Pallas kernels, body(): pl.pallas_call(functools.partial(step_two_kernel, d), out_shape=[pad_t, j...  2.45 us
    pallas_call x1, Pallas kernels, body(): pl.pallas_call(functools.partial(step_one_kernel, d), out_shape=[pad_t, p...  2.04 us
    pallas_call x1, Pallas kernels, body(): pl.pallas_call(functools.partial(pack_kernel, d), out_shape=[pltpu.SMEM(a...  1.87 us
  transfers between devices with their start and end apart: 12, of which 5 were waited for; matrix products, arithmetic and copies ran while one was open for 0% of the time, Pallas kernels for 7%

profile of v2, /device:TPU:0, one launch (start us, length us, event | category | flops | bytes accessed | tf_op | source)
XLA Modules:
  0.0 32.9 jit_solution(13141071390438626425)
XLA Ops:
  0.6 1.9 %pack.1 = (s32[16,128]{1,0:T(8,128)S(1)}, f32[3,32]{1,0:T(4,128)S(4)}, f32[5]{0:T(128)S(4)}, s32[16]{0:T(128)S(4)}, s32[64]{0:T(128)S(4)}, /*index=5*/s32[64]{0:...) custom-call(f32[5,32,16,128]{3,2,1,0:T(8,128)} %fields.1, ...), custom_call_target="tpu_custom_call" | custom-call | tf_op jit(solution)/shard_map/pack/pallas_call | solution.py:370
  2.5 3.1 %collective-permute-start = (f32[160,128]{1,0:T(8,128)S(1)}, f32[160,128]{1,0:T(8,128)S(1)}, u32[]{:S(2)}, u32[]{:S(2)}) collective-permute-start(f32[160,128]{1,0:T(8,128)S(1)} %get-tuple-element.30), channel_id=1, source_target_pairs={{0,4},{4,0},{8,12},{12,8},{1,5},{5,1},{9,13},{13,9},{2,6},{6,2},{1... | collective-permute-start | bytes 245768 | tf_op jit(solution)/shard_map/ppermute | solution.py:327
  5.6 2.5 %collective-permute-start.1 = (f32[160,128]{1,0:T(8,128)S(1)}, f32[160,128]{1,0:T(8,128)S(1)}, u32[]{:S(2)}, u32[]{:S(2)}) collective-permute-start(f32[160,128]{1,0:T(8,128)S(1)} %get-tuple-element.31), channel_id=1, source_target_pairs={{0,12},{4,8},{8,4},{12,0},{1,13},{5,9},{9,5},{13,1},{2,14},{6,10},... | collective-permute-start | bytes 245768 | tf_op jit(solution)/shard_map/ppermute | solution.py:333
  8.1 0.0 collective-permute-start.2
  8.1 1.5 %collective-permute-start.3 = (f32[16,384]{1,0:T(8,128)S(1)}, f32[16,384]{1,0:T(8,128)S(1)}, u32[]{:S(2)}, u32[]{:S(2)}) collective-permute-start(f32[16,384]{1,0:T(8,128)S(1)} %get-tuple-element.33), channel_id=1, source_target_pairs={{0,2},{2,0},{1,3},{3,1},{4,6},{6,4},{5,7},{7,5},{8,10},{10,8},{9,1... | collective-permute-start | bytes 73736 | tf_op jit(solution)/shard_map/ppermute | solution.py:327
  9.6 2.3 %collective-permute-done.3.refs_0_ = f32[16,384]{1,0:T(8,128)S(1)} collective-permute-done((f32[16,384]{1,0:T(8,128)S(1)}, f32[16,384]{1,0:T(8,128)S(1)}, u32[]{:S(2)}, u32[]{:S(2)}) %collective-permute-start.3) | collective-permute-done | bytes 24608 | tf_op jit(solution)/shard_map/ppermute | solution.py:327
  11.9 0.0 collective-permute-done.2.zface
  11.9 0.0 collective-permute-done.xa
  11.9 0.3 collective-permute-done.1.xb
  12.2 2.0 %step_one.1 = (f32[4088,128]{1,0:T(8,128)S(1)}, f32[4088,128]{1,0:T(8,128)S(1)}, f32[528,128]{1,0:T(8,128)S(1)}, f32[160,128]{1,0:T(8,128)S(1)}, f32[160,128]{1,...) custom-call(f32[4088,128]{1,0:T(8,128)S(1)} %get-tuple-element.29.pa, ...), custom_call_target="tpu_custom_call", output_to_operand_aliasing={{0}: (0, {})} | custom-call | tf_op jit(solution)/shard_map/step_one/pallas_call | solution.py:384
  14.3 0.1 collective-permute-start.6
  14.4 0.4 %collective-permute-start.4 = (f32[160,128]{1,0:T(8,128)S(1)}, f32[160,128]{1,0:T(8,128)S(1)}, u32[]{:S(2)}, u32[]{:S(2)}) collective-permute-start(f32[160,128]{1,0:T(8,128)S(1)} %get-tuple-element.41), channel_id=1, source_target_pairs={{0,4},{4,0},{8,12},{12,8},{1,5},{5,1},{9,13},{13,9},{2,6},{6,2},{1... | collective-permute-start | bytes 245768 | tf_op jit(solution)/shard_map/ppermute | solution.py:327
  14.8 2.7 %collective-permute-start.5 = (f32[160,128]{1,0:T(8,128)S(1)}, f32[160,128]{1,0:T(8,128)S(1)}, u32[]{:S(2)}, u32[]{:S(2)}) collective-permute-start(f32[160,128]{1,0:T(8,128)S(1)} %get-tuple-element.42), channel_id=1, source_target_pairs={{0,12},{4,8},{8,4},{12,0},{1,13},{5,9},{9,5},{13,1},{2,14},{6,10},... | collective-permute-start | bytes 245768 | tf_op jit(solution)/shard_map/ppermute | solution.py:333
  17.5 1.5 %collective-permute-start.7 = (f32[16,384]{1,0:T(8,128)S(1)}, f32[16,384]{1,0:T(8,128)S(1)}, u32[]{:S(2)}, u32[]{:S(2)}) collective-permute-start(f32[16,384]{1,0:T(8,128)S(1)} %get-tuple-element.44), channel_id=1, source_target_pairs={{0,2},{2,0},{1,3},{3,1},{4,6},{6,4},{5,7},{7,5},{8,10},{10,8},{9,1... | collective-permute-start | bytes 73736 | tf_op jit(solution)/shard_map/ppermute | solution.py:327
  19.0 0.2 collective-permute-start.9
  19.2 2.1 %collective-permute-done.7.refs_0_ = f32[16,384]{1,0:T(8,128)S(1)} collective-permute-done((f32[16,384]{1,0:T(8,128)S(1)}, f32[16,384]{1,0:T(8,128)S(1)}, u32[]{:S(2)}, u32[]{:S(2)}) %collective-permute-start.7) | collective-permute-done | bytes 24608 | tf_op jit(solution)/shard_map/ppermute | solution.py:327
  21.3 0.4 %collective-permute-start.10 = (f32[128,128]{1,0:T(8,128)S(1)}, f32[128,128]{1,0:T(8,128)S(1)}, u32[]{:S(2)}, u32[]{:S(2)}) collective-permute-start(f32[128,128]{1,0:T(8,128)S(1)} %get-tuple-element.51), channel_id=1, source_target_pairs={{0,8},{4,12},{8,0},{12,4},{1,9},{5,13},{9,1},{13,5},{2,10},{6,14},... | collective-permute-start | bytes 196616 | tf_op jit(solution)/shard_map/ppermute | solution.py:338
  21.8 0.0 collective-permute-done.6.zface
  21.8 2.1 %collective-permute-start.11 = (f32[128,128]{1,0:T(8,128)S(1)}, f32[128,128]{1,0:T(8,128)S(1)}, u32[]{:S(2)}, u32[]{:S(2)}) collective-permute-start(f32[128,128]{1,0:T(8,128)S(1)} %get-tuple-element.52), channel_id=1, source_target_pairs={{0,12},{4,0},{8,4},{12,8},{1,13},{5,1},{9,5},{13,9},{2,14},{6,2},{... | collective-permute-start | bytes 196616 | tf_op jit(solution)/shard_map/ppermute | solution.py:338
  23.9 0.0 collective-permute-done.4.xa
  23.9 0.0 collective-permute-done.5.xb
  23.9 2.5 %step_two.1 = (f32[4088,128]{1,0:T(8,128)S(1)}, f32[2560,128]{1,0:T(8,128)}, f32[48,128]{1,0:T(8,128)S(1)}, f32[24,128]{1,0:T(8,128)S(1)}) custom-call(f32[4088,128]{1,0:T(8,128)S(1)} %get-tuple-element.39.pad_in, f32[528,128]{1,0:T(8,128)S(1)} %get-tuple-element.40.factor, ...), custom_call_target="tpu_custom_call", output_to_operand_aliasing={{0}: (0, {})} | custom-call | tf_op jit(solution)/shard_map/step_two/pallas_call | solution.py:400
  26.4 0.0 collective-permute-start.8
  26.4 0.0 collective-permute-done.9.refs_1_
  26.4 1.5 %collective-permute-done.10.refs_2_ = f32[128,128]{1,0:T(8,128)S(1)} collective-permute-done((f32[128,128]{1,0:T(8,128)S(1)}, f32[128,128]{1,0:T(8,128)S(1)}, u32[]{:S(2)}, u32[]{:S(2)}) %collective-permute-start.10) | collective-permute-done | bytes 65568 | tf_op jit(solution)/shard_map/ppermute | solution.py:338
  27.8 0.0 collective-permute-done.11.refs_3_
  27.8 4.0 %collective-permute-done.8.got_sums = f32[24,128]{1,0:T(8,128)S(1)} collective-permute-done((f32[24,128]{1,0:T(8,128)S(1)}, f32[24,128]{1,0:T(8,128)S(1)}, u32[]{:S(2)}, u32[]{:S(2)}) %collective-permute-start.8) | collective-permute-done | bytes 12320 | tf_op jit(solution)/shard_map/ppermute | solution.py:338
  31.8 1.0 %place.1 = (f32[256,128]{1,0:T(8,128)}, f32[2,5,4,16]{3,2,1,0:T(4,128)}) custom-call(f32[48,128]{1,0:T(8,128)S(1)} %get-tuple-element.47.own_sums, f32[24,128]{1,0:T(8,128)S(1)} %collective-permute-done.8.got_sums, s32[64]{0:T(128)S(4)} %get-tuple-element.38.refs_5_.slot_of, s32[64]{0:T(128)S(4)} %get-tuple-element.45.refs_3_.parent_of, ...), custom_call_target="tpu_custom_call" | custom-call | tf_op jit(solution)/shard_map/place/pallas_call | solution.py:417
Async XLA Ops:
  2.5 9.4 %collective-permute-start = (f32[160,128]{1,0:T(8,128)S(1)}, f32[160,128]{1,0:T(8,128)S(1)}, u32[]{:S(2)}, u32[]{:S(2)}) collective-permute-start(f32[160,128]{1,0:T(8,128)S(1)} %get-tuple-element.30), channel_id=1, source_target_pairs={{0,4},{4,0},{8,12},{12,8},{1,5},{5,1},{9,13},{13,9},{2,6},{6,2},{1... | collective-permute-start | bytes 245768 | tf_op jit(solution)/shard_map/ppermute | solution.py:327
  5.6 6.6 %collective-permute-start.1 = (f32[160,128]{1,0:T(8,128)S(1)}, f32[160,128]{1,0:T(8,128)S(1)}, u32[]{:S(2)}, u32[]{:S(2)}) collective-permute-start(f32[160,128]{1,0:T(8,128)S(1)} %get-tuple-element.31), channel_id=1, source_target_pairs={{0,12},{4,8},{8,4},{12,0},{1,13},{5,9},{9,5},{13,1},{2,14},{6,10},... | collective-permute-start | bytes 245768 | tf_op jit(solution)/shard_map/ppermute | solution.py:333
  8.1 3.8 %collective-permute-start.2 = (f32[80,128]{1,0:T(8,128)S(1)}, f32[80,128]{1,0:T(8,128)S(1)}, u32[]{:S(2)}, u32[]{:S(2)}) collective-permute-start(f32[80,128]{1,0:T(8,128)S(1)} %get-tuple-element.32), channel_id=1, source_target_pairs={{0,1},{1,0},{2,3},{3,2},{4,5},{5,4},{6,7},{7,6},{8,9},{9,8},{10,11... | collective-permute-start | bytes 122888 | tf_op jit(solution)/shard_map/ppermute | solution.py:327
  8.1 3.8 %collective-permute-start.3 = (f32[16,384]{1,0:T(8,128)S(1)}, f32[16,384]{1,0:T(8,128)S(1)}, u32[]{:S(2)}, u32[]{:S(2)}) collective-permute-start(f32[16,384]{1,0:T(8,128)S(1)} %get-tuple-element.33), channel_id=1, source_target_pairs={{0,2},{2,0},{1,3},{3,1},{4,6},{6,4},{5,7},{7,5},{8,10},{10,8},{9,1... | collective-permute-start | bytes 73736 | tf_op jit(solution)/shard_map/ppermute | solution.py:327
  14.3 7.5 %collective-permute-start.6 = (f32[80,128]{1,0:T(8,128)S(1)}, f32[80,128]{1,0:T(8,128)S(1)}, u32[]{:S(2)}, u32[]{:S(2)}) collective-permute-start(f32[80,128]{1,0:T(8,128)S(1)} %get-tuple-element.43), channel_id=1, source_target_pairs={{0,1},{1,0},{2,3},{3,2},{4,5},{5,4},{6,7},{7,6},{8,9},{9,8},{10,11... | collective-permute-start | bytes 122888 | tf_op jit(solution)/shard_map/ppermute | solution.py:327
  14.4 9.5 %collective-permute-start.4 = (f32[160,128]{1,0:T(8,128)S(1)}, f32[160,128]{1,0:T(8,128)S(1)}, u32[]{:S(2)}, u32[]{:S(2)}) collective-permute-start(f32[160,128]{1,0:T(8,128)S(1)} %get-tuple-element.41), channel_id=1, source_target_pairs={{0,4},{4,0},{8,12},{12,8},{1,5},{5,1},{9,13},{13,9},{2,6},{6,2},{1... | collective-permute-start | bytes 245768 | tf_op jit(solution)/shard_map/ppermute | solution.py:327
  14.8 9.1 %collective-permute-start.5 = (f32[160,128]{1,0:T(8,128)S(1)}, f32[160,128]{1,0:T(8,128)S(1)}, u32[]{:S(2)}, u32[]{:S(2)}) collective-permute-start(f32[160,128]{1,0:T(8,128)S(1)} %get-tuple-element.42), channel_id=1, source_target_pairs={{0,12},{4,8},{8,4},{12,0},{1,13},{5,9},{9,5},{13,1},{2,14},{6,10},... | collective-permute-start | bytes 245768 | tf_op jit(solution)/shard_map/ppermute | solution.py:333
  17.5 3.8 %collective-permute-start.7 = (f32[16,384]{1,0:T(8,128)S(1)}, f32[16,384]{1,0:T(8,128)S(1)}, u32[]{:S(2)}, u32[]{:S(2)}) collective-permute-start(f32[16,384]{1,0:T(8,128)S(1)} %get-tuple-element.44), channel_id=1, source_target_pairs={{0,2},{2,0},{1,3},{3,1},{4,6},{6,4},{5,7},{7,5},{8,10},{10,8},{9,1... | collective-permute-start | bytes 73736 | tf_op jit(solution)/shard_map/ppermute | solution.py:327
  19.0 7.4 %collective-permute-start.9 = (f32[128,128]{1,0:T(8,128)S(1)}, f32[128,128]{1,0:T(8,128)S(1)}, u32[]{:S(2)}, u32[]{:S(2)}) collective-permute-start(f32[128,128]{1,0:T(8,128)S(1)} %get-tuple-element.50), channel_id=1, source_target_pairs={{0,4},{4,8},{8,12},{12,0},{1,5},{5,9},{9,13},{13,1},{2,6},{6,10},{... | collective-permute-start | bytes 196616 | tf_op jit(solution)/shard_map/ppermute | solution.py:338
  21.3 6.5 %collective-permute-start.10 = (f32[128,128]{1,0:T(8,128)S(1)}, f32[128,128]{1,0:T(8,128)S(1)}, u32[]{:S(2)}, u32[]{:S(2)}) collective-permute-start(f32[128,128]{1,0:T(8,128)S(1)} %get-tuple-element.51), channel_id=1, source_target_pairs={{0,8},{4,12},{8,0},{12,4},{1,9},{5,13},{9,1},{13,5},{2,10},{6,14},... | collective-permute-start | bytes 196616 | tf_op jit(solution)/shard_map/ppermute | solution.py:338
  21.8 6.1 %collective-permute-start.11 = (f32[128,128]{1,0:T(8,128)S(1)}, f32[128,128]{1,0:T(8,128)S(1)}, u32[]{:S(2)}, u32[]{:S(2)}) collective-permute-start(f32[128,128]{1,0:T(8,128)S(1)} %get-tuple-element.52), channel_id=1, source_target_pairs={{0,12},{4,0},{8,4},{12,8},{1,13},{5,1},{9,5},{13,9},{2,14},{6,2},{... | collective-permute-start | bytes 196616 | tf_op jit(solution)/shard_map/ppermute | solution.py:338
  26.4 5.5 %collective-permute-start.8 = (f32[24,128]{1,0:T(8,128)S(1)}, f32[24,128]{1,0:T(8,128)S(1)}, u32[]{:S(2)}, u32[]{:S(2)}) collective-permute-start(f32[24,128]{1,0:T(8,128)S(1)} %get-tuple-element.48), channel_id=1, source_target_pairs={{0,4},{4,8},{8,12},{12,0},{1,5},{5,9},{9,13},{13,1},{2,6},{6,10},{... | collective-permute-start | bytes 36872 | tf_op jit(solution)/shard_map/ppermute | solution.py:338

commit v3 on v2

--- a/solution.py
+++ b/solution.py
@@ -112,23 +112,26 @@
         copy.wait()
 
 
-def set_halos(d, pad, xa, xb, zface):
+def x_halos(d, xa, xb, rows):
     me = lax.axis_index("gx")
     even = lax.rem(me, 2) == 0
-    zero_x = jnp.zeros((d.levels, LANES), F32)
-    for f in range(FIELDS):
-        a = xa[f * d.levels : (f + 1) * d.levels, :]
-        b = xb[f * d.levels : (f + 1) * d.levels, :]
-        left = jnp.where(me == 0, zero_x, jnp.where(even, b, a))
-        right = jnp.where(me == d.n_gx - 1, zero_x, jnp.where(even, a, b))
-        pad[pl.ds(base_row(d, f, 0) + FRONT - 1, d.levels, stride=d.block), :] = left
-        pad[pl.ds(base_row(d, f, 0) + d.block, d.levels, stride=d.block), :] = right
+    a, b = xa[rows, :], xb[rows, :]
+    left = jnp.where(me == 0, 0.0, jnp.where(even, b, a))
+    right = jnp.where(me == d.n_gx - 1, 0.0, jnp.where(even, a, b))
+    return left, right
+
+
+def set_x_halos(d, pad, f, left, right):
+    pad[pl.ds(base_row(d, f, 0) + FRONT - 1, d.levels, stride=d.block), :] = left
+    pad[pl.ds(base_row(d, f, 0) + d.block, d.levels, stride=d.block), :] = right
+
+
+def set_z_halos(d, pad, zface):
     low = lax.axis_index("gz") == 0
-    zero_z = jnp.zeros((d.tiles, LANES), F32)
     for f in range(FIELDS):
         face = zface[f * d.tiles : (f + 1) * d.tiles, :]
-        pad[pl.ds(base_row(d, f, -1) + FRONT, d.tiles), :] = jnp.where(low, zero_z, face)
-        pad[pl.ds(base_row(d, f, d.levels) + FRONT, d.tiles), :] = jnp.where(low, face, zero_z)
+        pad[pl.ds(base_row(d, f, -1) + FRONT, d.tiles), :] = jnp.where(low, 0.0, face)
+        pad[pl.ds(base_row(d, f, d.levels) + FRONT, d.tiles), :] = jnp.where(low, face, 0.0)
 
 
 def stencil(d, pad, yq, wind, diff, f, z, lane):
@@ -160,32 +163,82 @@
     return jnp.sqrt(u * u + v * v + w * w + 1.0)
 
 
-def wall_coefficients(d, wall_type, count, slot_of):
-    first_tile = lax.axis_index("gx") * d.tiles
+def prepare_kernel(d, wall_type, wind, diff, count, slot_of, parent_of, *outs):
+    wall_coef, from_left, from_right, masks, send_table, place_table, counts, tally = outs
+    me = lax.axis_index("gx")
+    first_tile = me * d.tiles
     row = lax.broadcasted_iota(jnp.int32, (d.tiles, LANES), 0)
     strength = jnp.zeros((d.tiles, LANES), F32)
+    owner = jnp.full((d.tiles, LANES), -1, jnp.int32)
     for x in range(d.tiles):
         held = jnp.where(slot_of[first_tile + x] >= 0, count[x], 0).astype(F32) * (1.0 / BMAX)
         strength = jnp.where(row == x, held, strength)
+        owner = jnp.where(row == x, parent_of[first_tile + x] - me * d.parents, owner)
     kind = wall_type[...]
     value = jnp.zeros((d.tiles, LANES), F32)
     for code, entry in enumerate(TABLE):
         value = jnp.where(kind == code, entry, value)
-    return value * strength
+    wall_coef[...] = value * strength
+    for p in range(d.parents + 1):
+        masks[p * d.tiles : (p + 1) * d.tiles, :] = jnp.where(owner == p, 1.0, 0.0)
+    for z in range(d.levels):
+        wx = (0.5 * STEP) * wind[0, z]
+        for f in range(FIELDS):
+            spread = STEP * diff[f]
+            from_left[f * d.levels + z : f * d.levels + z + 1, :] = jnp.full((1, LANES), spread + wx, F32)
+            from_right[f * d.levels + z : f * d.levels + z + 1, :] = jnp.full((1, LANES), spread - wx, F32)
+    for k in range(d.n_gx):
+        tally[k] = 0
+    for i in range(d.n_gx * d.capacity):
+        send_table[i] = 0
+    for x in range(d.tiles):
+        slot = slot_of[first_tile + x]
+
+        @pl.when(slot >= 0)
+        def _():
+            away = lax.bitwise_xor(lax.shift_right_logical(slot, 3), me)
+            rank = tally[away]
+            send_table[away * d.capacity + rank] = x
+            tally[away] = rank + 1
+
+    def source(s, carry):
+        away = lax.bitwise_xor(s, me)
+
+        def tile(x, rank):
+            slot = slot_of[s * d.tiles + x]
+            mine = (slot >= 0) & (lax.shift_right_logical(slot, 3) == me)
+            place = jnp.where(mine, slot - me * SLOTS, SLOTS)
+            place_table[place] = away * d.capacity + rank
+            return rank + mine.astype(jnp.int32)
+
+        lax.fori_loop(0, d.tiles, tile, 0, unroll=True)
+        return carry
+
+    lax.fori_loop(0, d.n_gx, source, 0)
+    before = jnp.maximum(first_tile - d.tiles, 0)
+    for p in range(d.parents):
+        total = jnp.int32(0)
+        for x in range(d.tiles):
+            total = total + (parent_of[first_tile + x] == me * d.parents + p).astype(jnp.int32)
+            if p == 0:
+                earlier = parent_of[before + x] == me * d.parents
+                total = total + ((me > 0) & earlier).astype(jnp.int32)
+        counts[p] = total
 
 
 def step_one_kernel(d, pad_in, xa, xb, zface, *refs):
     yq = refs[: d.y_sends]
-    wall_type, wind, diff, count, slot_of = refs[d.y_sends : d.y_sends + 5]
-    outs = refs[d.y_sends + 5 :]
-    pad, new_pad, factor, xa_out, xb_out, z_out = outs[:6]
-    yq_out = outs[6 : 6 + d.y_sends]
-    stress = outs[6 + d.y_sends : 6 + d.y_sends + d.n_gx]
-    table, tally = outs[6 + d.y_sends + d.n_gx :]
-    set_halos(d, pad, xa, xb, zface)
+    wall_coef, wind, diff, send_table = refs[d.y_sends : d.y_sends + 4]
+    outs = refs[d.y_sends + 4 :]
+    pad, new_pad, factor, z_out = outs[:4]
+    yq_out = outs[4 : 4 + d.y_sends]
+    stress = outs[4 + d.y_sends :]
+    for f in range(FIELDS):
+        set_x_halos(d, pad, f, *x_halos(d, xa, xb, slice(f * d.levels, (f + 1) * d.levels)))
+    set_z_halos(d, pad, zface)
     lane = lax.broadcasted_iota(jnp.int32, (d.tiles, LANES), 1)
     zeros = jnp.zeros((d.tiles, LANES), F32)
-    coef = wall_coefficients(d, wall_type, count, slot_of)
+    coef = wall_coef[...]
 
     def level(z, carry):
         both = [stencil(d, pad, yq, wind, diff, f, z, lane) for f in range(FIELDS)]
@@ -201,54 +254,32 @@
     for f in range(FIELDS):
         packed = add_edges(d, packed, new_pad, f, lane)
     write_y(d, yq_out, packed, lane)
-    for out, tile in zip((xa_out, xb_out), x_choices(d)):
-        for f in range(FIELDS):
-            out[f * d.levels : (f + 1) * d.levels, :] = new_pad[
-                pl.ds(base_row(d, f, 0) + FRONT + tile, d.levels, stride=d.block), :
-            ]
     z_level = jnp.where(lax.axis_index("gz") == 0, d.levels - 1, 0)
     for f in range(FIELDS):
         z_out[f * d.tiles : (f + 1) * d.tiles, :] = new_pad[
             pl.ds(pl.multiple_of(base_row(d, f, z_level) + FRONT, 8), d.tiles), :
         ]
-    me = lax.axis_index("gx")
-    for k in range(d.n_gx):
-        tally[k] = 0
-    for i in range(d.n_gx * d.capacity):
-        table[i] = 0
-    for x in range(d.tiles):
-        slot = slot_of[me * d.tiles + x]
-
-        @pl.when(slot >= 0)
-        def _():
-            away = lax.rem(lax.shift_right_logical(slot, 3) - me + d.n_gx, d.n_gx)
-            rank = tally[away]
-            table[away * d.capacity + rank] = x
-            tally[away] = rank + 1
-
     for k in range(d.n_gx):
         for c in range(d.capacity):
-            tile = table[k * d.capacity + c]
+            tile = send_table[k * d.capacity + c]
             stress[k][c * d.levels : (c + 1) * d.levels, :] = factor[pl.ds(tile, d.levels, stride=d.tiles), :]
 
 
-def step_two_kernel(d, pad_in, factor, xa, xb, zface, *refs):
+def step_two_kernel(d, pad_in, factor, zface, *refs):
     yq = refs[: d.y_sends]
-    wind, diff, parent_of = refs[d.y_sends : d.y_sends + 3]
-    pad, new_fields, own_sums, sent_sums, coarse = refs[d.y_sends + 3 :]
-    set_halos(d, pad, xa, xb, zface)
+    masks_in, wind, diff = refs[d.y_sends : d.y_sends + 3]
+    pad, new_fields, coarse, xa_out, xb_out = refs[-5:]
+    zero_x = jnp.zeros((d.levels, LANES), F32)
+    for f in range(FIELDS):
+        set_x_halos(d, pad, f, zero_x, zero_x)
+    set_z_halos(d, pad, zface)
     lane = lax.broadcasted_iota(jnp.int32, (d.tiles, LANES), 1)
-    row = lax.broadcasted_iota(jnp.int32, (d.tiles, LANES), 0)
     zeros = jnp.zeros((d.tiles, LANES), F32)
-    me = lax.axis_index("gx")
-    held = jnp.full((d.tiles, LANES), -1, jnp.int32)
-    for x in range(d.tiles):
-        held = jnp.where(row == x, parent_of[me * d.tiles + x] - me * d.parents, held)
-    masks = [jnp.where(held == p, 1.0, 0.0) for p in range(d.parents + 1)]
+    masks = [masks_in[p * d.tiles : (p + 1) * d.tiles, :] for p in range(d.parents + 1)]
     coarse_levels = d.levels // RATIO
     coarse[...] = jnp.zeros_like(coarse)
     rows = d.levels * d.tiles
-    per_parent = own_sums.shape[0] // d.parents
+    per_parent = coarse.shape[0] // (d.parents + 1)
 
     def coarse_level(k, carry):
         def level(i, sums):
@@ -271,76 +302,102 @@
         return carry
 
     lax.fori_loop(0, coarse_levels, coarse_level, 0)
+    edge = FIELDS * d.levels
+    for out, tile in zip((xa_out, xb_out), x_choices(d)):
+        for f in range(FIELDS):
+            out[f * d.levels : (f + 1) * d.levels, :] = pad[
+                pl.ds(base_row(d, f, 0) + FRONT + tile, d.levels, stride=d.block), :
+            ]
+        out[edge : edge + per_parent, :] = coarse[d.parents * per_parent :, :]
+
+
+def finish_kernel(d, from_left, from_right, state_in, xa, xb, own_a, own_b, coarse, parent_of, place_table, counts, *refs):
+    stress = refs[: d.n_gx]
+    state, new_fields, wall_stress, parent_mean, terms, gathered, placed, sems = refs[d.n_gx :]
+    me = lax.axis_index("gx")
+    even = lax.rem(me, 2) == 0
+    rows = d.levels * d.tiles
+    coarse_levels = d.levels // RATIO
+    per_parent = coarse.shape[0] // (d.parents + 1)
+    copies = []
+    for f in range(FIELDS):
+        cut = slice(f * d.levels, (f + 1) * d.levels)
+        left, right = x_halos(d, xa, xb, cut)
+        left, right = from_left[cut, :] * left, from_right[cut, :] * right
+        ahead = from_right[cut, :] * jnp.where(even, own_b[cut, :], own_a[cut, :])
+        for tile, added in ((0, left), (d.tiles - 1, right)):
+            place = pl.ds(f * rows + tile, d.levels, stride=d.tiles)
+            state[place, :] = state[place, :] + added
+        copies.append(
+            pltpu.make_async_copy(
+                state.at[pl.ds(f * rows, rows), :], new_fields.at[pl.ds(f * rows, rows), :], sems.at[f]
+            )
+        )
+        copies[-1].start()
+        for i, term in enumerate((left, right, ahead)):
+            terms[i * per_parent + f * coarse_levels : i * per_parent + (f + 1) * coarse_levels, :] = jnp.sum(
+                term.reshape(coarse_levels, RATIO, LANES), axis=1
+            )
+    part = d.capacity * d.levels
+    for k in range(d.n_gx):
+        gathered[k * part : (k + 1) * part, :] = stress[k][...]
+    for s in range(SLOTS):
+        start = pl.multiple_of(place_table[s] * d.levels, 8)
+        placed[pl.ds(s, d.levels, stride=SLOTS), :] = gathered[pl.ds(start, d.levels), :]
+    copies.append(pltpu.make_async_copy(placed.at[pl.ds(0, d.levels * SLOTS), :], wall_stress, sems.at[FIELDS]))
+    copies[-1].start()
+    filled = FIELDS * coarse_levels
+    if filled < per_parent:
+        for i in range(3):
+            terms[i * per_parent + filled : (i + 1) * per_parent, :] = jnp.zeros((per_parent - filled, LANES), F32)
+    edge = FIELDS * d.levels
+    got = jnp.where(even, xb[edge : edge + per_parent, :], xa[edge : edge + per_parent, :])
+    first_tile = me * d.tiles
+    first_parent = parent_of[first_tile] - me * d.parents
+    last_parent = parent_of[first_tile + d.tiles - 1] - me * d.parents
+    before = jnp.maximum(first_tile - 1, 0)
+    ahead_counts = (me > 0) & (parent_of[before] == me * d.parents)
     pick_row = lax.broadcasted_iota(jnp.int32, (LANES, LANES), 0)
     pick_lane = lax.broadcasted_iota(jnp.int32, (LANES, LANES), 1)
     pick = jnp.where(pick_row // RATIO == pick_lane, 1.0, 0.0)
-    summed = jnp.dot(coarse[...], pick, precision=lax.Precision.HIGHEST, preferred_element_type=F32)
-    own_sums[...] = summed[: d.parents * per_parent, :]
-    sent_sums[...] = summed[d.parents * per_parent :, :]
-
-
-def place_kernel(d, own_sums, got_sums, slot_of, parent_of, *refs):
-    stress = refs[: d.n_gx]
-    wall_stress, parent_mean, gathered, table = refs[d.n_gx :]
-    me = lax.axis_index("gx")
-    part = d.capacity * d.levels
-    for k in range(d.n_gx):
-        gathered[k * part : (k + 1) * part, :] = stress[k][...]
-
-    def source(s, carry):
-        away = lax.rem(me - s + d.n_gx, d.n_gx)
-
-        def tile(x, rank):
-            slot = slot_of[s * d.tiles + x]
-            mine = (slot >= 0) & (lax.shift_right_logical(slot, 3) == me)
-            place = jnp.where(mine, slot - me * SLOTS, SLOTS)
-            table[place] = away * d.capacity + rank
-            return rank + mine.astype(jnp.int32)
-
-        lax.fori_loop(0, d.tiles, tile, 0, unroll=True)
-        return carry
-
-    lax.fori_loop(0, d.n_gx, source, 0)
-    for s in range(SLOTS):
-        start = pl.multiple_of(table[s] * d.levels, 8)
-        wall_stress[pl.ds(s, d.levels, stride=SLOTS), :] = gathered[pl.ds(start, d.levels), :]
-    before = jnp.maximum(me - 1, 0) * d.tiles
-    per_parent = own_sums.shape[0] // d.parents
-    coarse_levels = d.levels // RATIO
-    cells = d.columns // RATIO
     for p in range(d.parents):
-        count = jnp.int32(0)
-        for x in range(d.tiles):
-            count = count + (parent_of[me * d.tiles + x] == me * d.parents + p).astype(jnp.int32)
-            if p == 0:
-                earlier = parent_of[before + x] == me * d.parents + p
-                count = count + ((me > 0) & earlier).astype(jnp.int32)
-        total = own_sums[p * per_parent : (p + 1) * per_parent, :]
+        total = coarse[p * per_parent : (p + 1) * per_parent, :]
+        total = total + jnp.where(first_parent == p, terms[:per_parent, :], 0.0)
+        total = total + jnp.where(last_parent == p, terms[per_parent : 2 * per_parent, :], 0.0)
         if p == 0:
-            total = jnp.where(me == 0, total, total + got_sums[...])
-        mean = total / (jnp.full(total.shape, count, jnp.int32).astype(F32) * (RATIO * RATIO))
+            total = total + jnp.where(me == 0, 0.0, got)
+            total = total + jnp.where(ahead_counts, terms[2 * per_parent :, :], 0.0)
+        total = jnp.dot(total, pick, precision=lax.Precision.HIGHEST, preferred_element_type=F32)
+        mean = total / (jnp.full(total.shape, counts[p], jnp.int32).astype(F32) * (RATIO * RATIO))
         for f in range(FIELDS):
-            parent_mean[p, f] = mean[f * coarse_levels : (f + 1) * coarse_levels, :cells]
+            parent_mean[p, f] = mean[f * coarse_levels : (f + 1) * coarse_levels, : d.columns // RATIO]
+    for copy in copies:
+        copy.wait()
 
 
 def swapped(block, axis):
     return lax.ppermute(block, axis, [(i, i ^ 1) for i in range(lax.axis_size(axis))])
 
 
-def swapped_between(block, axis):
+def swapped_between(block, axis, inner):
     n = lax.axis_size(axis)
-    other = lambda i: (i + 1) % n if i % 2 else (i - 1) % n
-    return lax.ppermute(block, axis, [(i, other(i)) for i in range(n)])
-
-
-def rotated(block, axis, distance):
-    n = lax.axis_size(axis)
-    return lax.ppermute(block, axis, [(i, (i + distance) % n) for i in range(n)])
-
-
-def faces_swapped(d, xa, xb, zface, yq):
-    xa = swapped(xa, "gx")
-    xb = swapped_between(xb, "gx")
+    route = []
+    for i in range(n):
+        for k in range(2):
+            other = (i, 1 - k) if i in (0, n - 1) else (i + 1 if i % 2 else i - 1, k)
+            route.append((2 * i + k, 2 * other[0] + other[1]))
+    return lax.ppermute(block, (axis, inner), route)
+
+
+def crossed(block, axis, distance):
+    return lax.ppermute(block, axis, [(i, i ^ distance) for i in range(lax.axis_size(axis))])
+
+
+def x_swapped(xa, xb):
+    return [in_vmem(swapped(xa, "gx")), in_vmem(swapped_between(xb, "gx", "gz"))]
+
+
+def zy_swapped(d, zface, yq):
     if d.y_sends == 1:
         yq = [swapped(yq[0], "gy")]
     else:
@@ -349,14 +406,13 @@
             lax.ppermute(yq[0], "gy", [(i, i + 1) for i in range(n - 1)]),
             lax.ppermute(yq[1], "gy", [(i + 1, i) for i in range(n - 1)]),
         ]
-    zface = swapped(zface, "gz")
-    return [in_vmem(a) for a in (xa, xb, zface, *yq)]
+    return [in_vmem(a) for a in (swapped(zface, "gz"), *yq)]
 
 
 def body(fields, parent_wind, diffusivity, wall_type, building_count, slot_of, parent_of):
     _, levels, tiles, columns = fields.shape
     d = Dims(levels, tiles, columns, slot_of.shape[0], lax.axis_size("gx"), lax.axis_size("gy"))
-    assert columns == LANES and lax.axis_size("gz") == 2 and d.n_gx % 2 == 0
+    assert columns == LANES and lax.axis_size("gz") == 2 and d.n_gx & (d.n_gx - 1) == 0
     params = pltpu.CompilerParams(vmem_limit_bytes=24 << 20)
     small = [in_hbm(a) for a in (wall_type, parent_wind, diffusivity, building_count, slot_of, parent_of)]
     rows = FIELDS * levels * tiles
@@ -378,57 +434,78 @@
         name="pack",
     )(in_hbm(fields), *small))[: n_small + 4]
     yq = packed[n_small + 4 :]
-    faces = faces_swapped(d, xa, xb, zface, yq)
-
-    n_out = 6 + d.y_sends + d.n_gx
-    _, new_pad, factor, xa, xb, zface, *rest = pl.pallas_call(
+    faces = x_swapped(xa, xb) + zy_swapped(d, zface, yq)
+    hbm = pl.BlockSpec(memory_space=pltpu.HBM)
+
+    def ints(n):
+        return pltpu.SMEM((n,), jnp.int32)
+
+    wall_coef, from_left, from_right, masks, send_table, place_table, counts = pl.pallas_call(
+        functools.partial(prepare_kernel, d),
+        out_shape=[pltpu.VMEM((tiles, LANES), F32), x_t, x_t, pltpu.VMEM(((d.parents + 1) * tiles, LANES), F32)]
+        + [ints(d.n_gx * d.capacity), ints(SLOTS + 1), ints(d.parents)],
+        in_specs=[VM] + [SM] * 5,
+        out_specs=[VM] * 4 + [SM] * 3,
+        scratch_shapes=[ints(d.n_gx)],
+        compiler_params=params,
+        name="prepare",
+    )(in_vmem(small[0]), *small[1:])
+
+    _, new_pad, factor, zface, *rest = pl.pallas_call(
         functools.partial(step_one_kernel, d),
-        out_shape=[pad_t, pad_t, pltpu.VMEM(((levels + 1) * tiles, LANES), F32), x_t, x_t, z_t, *y_ts]
-        + [stress_t] * d.n_gx,
-        in_specs=[VM] * (5 + d.y_sends) + [SM] * 4,
-        out_specs=[VM] * n_out,
-        scratch_shapes=[pltpu.SMEM((d.n_gx * d.capacity,), jnp.int32), pltpu.SMEM((d.n_gx,), jnp.int32)],
+        out_shape=[pad_t, pad_t, pltpu.VMEM(((levels + 1) * tiles, LANES), F32), z_t, *y_ts] + [stress_t] * d.n_gx,
+        in_specs=[VM] * (5 + d.y_sends) + [SM] * 3,
+        out_specs=[VM] * (4 + d.y_sends + d.n_gx),
         input_output_aliases={0: 0},
         compiler_params=params,
         name="step_one",
-    )(in_vmem(pad), *faces, *small[:5])
+    )(in_vmem(pad), *faces, in_vmem(wall_coef), small[1], small[2], send_table)
     yq, stress = rest[: d.y_sends], rest[d.y_sends :]
-    faces = faces_swapped(d, xa, xb, zface, yq)
-    stress = [stress[0]] + [rotated(stress[k], "gx", k) for k in range(1, d.n_gx)]
-
+    faces = zy_swapped(d, zface, yq)
+    stress = [stress[0]] + [in_vmem(crossed(stress[k], "gx", k)) for k in range(1, d.n_gx)]
+
+    early = stress[1:]
     per_parent = -(-FIELDS * (levels // RATIO) // 8) * 8
-    _, new_fields, own_sums, sent_sums = pl.pallas_call(
+    state_t = pltpu.VMEM((rows + tiles, LANES), F32)
+    message_t = pltpu.VMEM((FIELDS * levels + per_parent, LANES), F32)
+    _, state, coarse, own_a, own_b = pl.pallas_call(
         functools.partial(step_two_kernel, d),
-        out_shape=[
-            pad_t,
-            jax.ShapeDtypeStruct((rows, LANES), F32),
-            pltpu.VMEM((d.parents * per_parent, LANES), F32),
-            pltpu.VMEM((per_parent, LANES), F32),
-        ],
-        in_specs=[VM] * (5 + d.y_sends) + [SM] * 3,
-        out_specs=[VM] * 4,
-        scratch_shapes=[pltpu.VMEM(((d.parents + 1) * per_parent, LANES), F32)],
+        out_shape=[pad_t, state_t, pltpu.VMEM(((d.parents + 1) * per_parent, LANES), F32), message_t, message_t],
+        in_specs=[VM] * (4 + d.y_sends) + [SM] * 2 + [VM] * len(early),
+        out_specs=[VM] * 5,
         input_output_aliases={0: 0},
         compiler_params=params,
         name="step_two",
-    )(in_vmem(new_pad), in_vmem(factor), *faces, small[1], small[2], small[5])
-    got_sums = rotated(sent_sums, "gx", 1)
-
-    wall_stress, parent_mean = pl.pallas_call(
-        functools.partial(place_kernel, d),
+    )(in_vmem(new_pad), in_vmem(factor), *faces, in_vmem(masks), small[1], small[2], *early)
+    xs = x_swapped(own_a, own_b)
+
+    _, new_fields, wall_stress, parent_mean = pl.pallas_call(
+        functools.partial(finish_kernel, d),
         out_shape=[
+            state_t,
+            jax.ShapeDtypeStruct((rows, LANES), F32),
             jax.ShapeDtypeStruct((levels * SLOTS, LANES), F32),
             jax.ShapeDtypeStruct((d.parents, FIELDS, levels // RATIO, columns // RATIO), F32),
         ],
-        in_specs=[VM, VM, SM, SM] + [VM] * d.n_gx,
-        out_specs=[VM, VM],
+        in_specs=[VM] * 8 + [SM] * 3 + [VM] * d.n_gx,
+        out_specs=[VM, hbm, hbm, VM],
         scratch_shapes=[
+            pltpu.VMEM((3 * per_parent, LANES), F32),
             pltpu.VMEM((d.n_gx * d.capacity * levels, LANES), F32),
-            pltpu.SMEM((SLOTS + 1,), jnp.int32),
+            pltpu.VMEM(((levels + 1) * SLOTS, LANES), F32),
+            pltpu.SemaphoreType.DMA((FIELDS + 1,)),
         ],
+        input_output_aliases={2: 0},
         compiler_params=params,
-        name="place",
-    )(in_vmem(own_sums), in_vmem(got_sums), small[4], small[5], *[in_vmem(s) for s in stress])
+        name="finish",
+    )(
+        *[in_vmem(a) for a in (from_left, from_right, state, *xs, own_a, own_b, coarse)],
+        small[5],
+        place_table,
+        counts,
+        *[in_vmem(stress[0])],
+        *stress[1:],
+    )
     return (
         new_fields.reshape(fields.shape),
         wall_stress.reshape(levels, SLOTS, columns),

time: 33 us -> 30.1 us (0.912)
  waiting for transfers between devices: 10.3 us -> 8.28 us
  starting transfers between devices: 14.5 us -> 13.1 us
  Pallas kernels: 7.4 us -> 7.9 us
    ppermute x6 -> x5, waiting for transfers between devices: 5.82 us -> 1.01 us  [the longest x3 1.01 us: crossed(): lax.ppermute(block, axis, [(i, i ^ distance) for i in range(lax.axis_size...]
    ppermute x6, waiting for transfers between devices: 4.49 us -> 7.26 us  [swapped(): lax.ppermute(block, axis, [(i, i ^ 1) for i in range(lax.axis_size(axis))])]
    ppermute x6 -> x5, starting transfers between devices: 7.91 us -> 5.15 us  [the longest x3 5.14 us: crossed(): lax.ppermute(block, axis, [(i, i ^ distance) for i in range(lax.axis_size...]
    ppermute x6, starting transfers between devices: 6.59 us -> 7.91 us  [swapped(): lax.ppermute(block, axis, [(i, i ^ 1) for i in range(lax.axis_size(axis))])]
    pallas_call x2 -> x3, Pallas kernels: 3.48 us -> 4.1 us  [the longest x1 1.93 us: body(): pl.pallas_call(functools.partial(finish_kernel, d), out_shape=[state_t, j...]
  transfers between devices with their start and end apart: 12 -> 11, of which waited for: 5 -> 4; matrix products, arithmetic and copies ran while one was open for 0% -> 0% of each run, Pallas kernels for 7% -> 2%
where the time goes in v3:
time: 30.1 us; the launch traced here: 29.9 us
  starting transfers between devices  13.1 us (44%)
  waiting for transfers between devices  8.28 us (28%)
  Pallas kernels  7.9 us (26%)
  between operations  0.68 us (2%)
    ppermute x6, starting transfers between devices, swapped(): lax.ppermute(block, axis, [(i, i ^ 1) for i in range(lax.axis_size(axis))])  7.91 us
    ppermute x6, waiting for transfers between devices, swapped(): lax.ppermute(block, axis, [(i, i ^ 1) for i in range(lax.axis_size(axis))])  7.26 us
    ppermute x3, starting transfers between devices, crossed(): lax.ppermute(block, axis, [(i, i ^ distance) for i in range(lax.axis_size...  5.14 us
    pallas_call x1, Pallas kernels, body(): pl.pallas_call(functools.partial(step_one_kernel, d), out_shape=[pad_t, p...  1.93 us
    pallas_call x1, Pallas kernels, body(): pl.pallas_call(functools.partial(finish_kernel, d), out_shape=[state_t, j...  1.93 us
    pallas_call x1, Pallas kernels, body(): pl.pallas_call(functools.partial(pack_kernel, d), out_shape=[pltpu.SMEM(a...  1.87 us
    pallas_call x1, Pallas kernels, body(): pl.pallas_call(functools.partial(step_two_kernel, d), out_shape=[pad_t, s...  1.45 us
    ppermute x3, waiting for transfers between devices, crossed(): lax.ppermute(block, axis, [(i, i ^ distance) for i in range(lax.axis_size...  1.01 us
  transfers between devices with their start and end apart: 11, of which 4 were waited for; matrix products, arithmetic and copies ran while one was open for 0% of the time, Pallas kernels for 2%

profile of v3, /device:TPU:0, one launch (start us, length us, event | category | flops | bytes accessed | tf_op | source)
XLA Modules:
  0.0 29.9 jit_solution(6135151796632186803)
XLA Ops:
  0.6 1.9 %pack.1 = (s32[16,128]{1,0:T(8,128)S(1)}, f32[3,32]{1,0:T(4,128)S(4)}, f32[5]{0:T(128)S(4)}, s32[16]{0:T(128)S(4)}, s32[64]{0:T(128)S(4)}, /*index=5*/s32[64]{0:...) custom-call(f32[5,32,16,128]{3,2,1,0:T(8,128)} %fields.1, ...), custom_call_target="tpu_custom_call" | custom-call | tf_op jit(solution)/shard_map/pack/pallas_call | solution.py:426
  2.5 3.1 %collective-permute-start = (f32[160,128]{1,0:T(8,128)S(1)}, f32[160,128]{1,0:T(8,128)S(1)}, u32[]{:S(2)}, u32[]{:S(2)}) collective-permute-start(f32[160,128]{1,0:T(8,128)S(1)} %get-tuple-element.45), channel_id=1, source_target_pairs={{0,4},{4,0},{8,12},{12,8},{1,5},{5,1},{9,13},{13,9},{2,6},{6,2},{1... | collective-permute-start | bytes 245768 | tf_op jit(solution)/shard_map/ppermute | solution.py:379
  5.6 0.0 collective-permute-start.1
  5.6 0.5 %collective-permute-start.2 = (f32[80,128]{1,0:T(8,128)S(1)}, f32[80,128]{1,0:T(8,128)S(1)}, u32[]{:S(2)}, u32[]{:S(2)}) collective-permute-start(f32[80,128]{1,0:T(8,128)S(1)} %get-tuple-element.47), channel_id=1, source_target_pairs={{0,1},{1,0},{2,3},{3,2},{4,5},{5,4},{6,7},{7,6},{8,9},{9,8},{10,11... | collective-permute-start | bytes 122888 | tf_op jit(solution)/shard_map/ppermute | solution.py:379
  6.1 1.5 %collective-permute-start.3 = (f32[16,384]{1,0:T(8,128)S(1)}, f32[16,384]{1,0:T(8,128)S(1)}, u32[]{:S(2)}, u32[]{:S(2)}) collective-permute-start(f32[16,384]{1,0:T(8,128)S(1)} %get-tuple-element.48), channel_id=1, source_target_pairs={{0,2},{2,0},{1,3},{3,1},{4,6},{6,4},{5,7},{7,5},{8,10},{10,8},{9,1... | collective-permute-start | bytes 73736 | tf_op jit(solution)/shard_map/ppermute | solution.py:379
  7.6 0.7 %prepare.1 = (f32[16,128]{1,0:T(8,128)S(1)}, f32[160,128]{1,0:T(8,128)S(1)}, f32[160,128]{1,0:T(8,128)S(1)}, f32[48,128]{1,0:T(8,128)S(1)}, s32[16]{0:T(128)S(4)}, /*index=5*/s32[9]{0:T(128)S(4)}, s32[2]{0:T(128)S(4)}) custom-call(s32[16,128]{1,0:T(8,128)S(1)} %get-tuple-element.36.wall_type, f32[3,32]{1,0:T(4,128)S(4)} %get-tuple-element.37.wind.refs_2_, ...), custom_call_target="tpu_custom_call" | custom-call | tf_op jit(solution)/shard_map/prepare/pallas_call | solution.py:443
  8.3 1.6 %collective-permute-done.3.refs_0_ = f32[16,384]{1,0:T(8,128)S(1)} collective-permute-done((f32[16,384]{1,0:T(8,128)S(1)}, f32[16,384]{1,0:T(8,128)S(1)}, u32[]{:S(2)}, u32[]{:S(2)}) %collective-permute-start.3) | collective-permute-done | bytes 24608 | tf_op jit(solution)/shard_map/ppermute | solution.py:379
  9.9 0.0 collective-permute-done.2.zface
  9.9 0.0 collective-permute-done.xa
  9.9 0.0 collective-permute-done.1.xb
  10.0 1.9 %step_one.1 = (f32[4088,128]{1,0:T(8,128)S(1)}, f32[4088,128]{1,0:T(8,128)S(1)}, f32[528,128]{1,0:T(8,128)S(1)}, f32[80,128]{1,0:T(8,128)S(1)}, f32[16,384]{1,0:...) custom-call(f32[4088,128]{1,0:T(8,128)S(1)} %get-tuple-element.44.pa, ...), custom_call_target="tpu_custom_call", output_to_operand_aliasing={{0}: (0, {})} | custom-call | tf_op jit(solution)/shard_map/step_one/pallas_call | solution.py:454
  11.9 2.7 %collective-permute-start.6 = (f32[128,128]{1,0:T(8,128)S(1)}, f32[128,128]{1,0:T(8,128)S(1)}, u32[]{:S(2)}, u32[]{:S(2)}) collective-permute-start(f32[128,128]{1,0:T(8,128)S(1)} %get-tuple-element.56), channel_id=1, source_target_pairs={{0,4},{4,0},{8,12},{12,8},{1,5},{5,1},{9,13},{13,9},{2,6},{6,2},{1... | collective-permute-start | bytes 196616 | tf_op jit(solution)/shard_map/ppermute | solution.py:393
  14.6 0.4 %collective-permute-start.7 = (f32[128,128]{1,0:T(8,128)S(1)}, f32[128,128]{1,0:T(8,128)S(1)}, u32[]{:S(2)}, u32[]{:S(2)}) collective-permute-start(f32[128,128]{1,0:T(8,128)S(1)} %get-tuple-element.57), channel_id=1, source_target_pairs={{0,8},{4,12},{8,0},{12,4},{1,9},{5,13},{9,1},{13,5},{2,10},{6,14},... | collective-permute-start | bytes 196616 | tf_op jit(solution)/shard_map/ppermute | solution.py:393
  15.0 2.0 %collective-permute-start.8 = (f32[128,128]{1,0:T(8,128)S(1)}, f32[128,128]{1,0:T(8,128)S(1)}, u32[]{:S(2)}, u32[]{:S(2)}) collective-permute-start(f32[128,128]{1,0:T(8,128)S(1)} %get-tuple-element.58), channel_id=1, source_target_pairs={{0,12},{4,8},{8,4},{12,0},{1,13},{5,9},{9,5},{13,1},{2,14},{6,10},... | collective-permute-start | bytes 196616 | tf_op jit(solution)/shard_map/ppermute | solution.py:393
  17.0 0.0 collective-permute-start.4
  17.0 1.5 %collective-permute-start.5 = (f32[16,384]{1,0:T(8,128)S(1)}, f32[16,384]{1,0:T(8,128)S(1)}, u32[]{:S(2)}, u32[]{:S(2)}) collective-permute-start(f32[16,384]{1,0:T(8,128)S(1)} %get-tuple-element.54), channel_id=1, source_target_pairs={{0,2},{2,0},{1,3},{3,1},{4,6},{6,4},{5,7},{7,5},{8,10},{10,8},{9,1... | collective-permute-start | bytes 73736 | tf_op jit(solution)/shard_map/ppermute | solution.py:379
  18.5 2.3 %collective-permute-done.5.refs_0_ = f32[16,384]{1,0:T(8,128)S(1)} collective-permute-done((f32[16,384]{1,0:T(8,128)S(1)}, f32[16,384]{1,0:T(8,128)S(1)}, u32[]{:S(2)}, u32[]{:S(2)}) %collective-permute-start.5) | collective-permute-done | bytes 24608 | tf_op jit(solution)/shard_map/ppermute | solution.py:379
  20.9 0.0 collective-permute-done.4.zface
  20.9 0.0 collective-permute-done.6.refs_4_.refs_1_
  20.9 1.0 %collective-permute-done.7.refs_5_.refs_2_ = f32[128,128]{1,0:T(8,128)S(1)} collective-permute-done((f32[128,128]{1,0:T(8,128)S(1)}, f32[128,128]{1,0:T(8,128)S(1)}, u32[]{:S(2)}, u32[]{:S(2)}) %collective-permute-start.7) | collective-permute-done | bytes 65568 | tf_op jit(solution)/shard_map/ppermute | solution.py:393
  21.9 0.0 collective-permute-done.8.refs_6_.refs_3_
  21.9 1.5 %step_two.1 = (f32[4088,128]{1,0:T(8,128)S(1)}, f32[2576,128]{1,0:T(8,128)S(1)}, f32[72,128]{1,0:T(8,128)S(1)}, f32[184,128]{1,0:T(8,128)S(1)}, f32[184,128]{1,0:T(8,128)S(1)}) custom-call(f32[4088,128]{1,0:T(8,128)S(1)} %get-tuple-element.51.pad_in, f32[528,128]{1,0:T(8,128)S(1)} %get-tuple-element.52.factor, ...), custom_call_target="tpu_custom_call", output_to_operand_aliasing={{0}: (0, {})} | custom-call | tf_op jit(solution)/shard_map/step_two/pallas_call | solution.py:471
  23.3 1.3 %collective-permute-start.9 = (f32[184,128]{1,0:T(8,128)S(1)}, f32[184,128]{1,0:T(8,128)S(1)}, u32[]{:S(2)}, u32[]{:S(2)}) collective-permute-start(f32[184,128]{1,0:T(8,128)S(1)} %get-tuple-element.60.own_a), channel_id=1, source_target_pairs={{0,4},{4,0},{8,12},{12,8},{1,5},{5,1},{9,13},{13,9},{2,6},{6,2},{1... | collective-permute-start | bytes 282632 | tf_op jit(solution)/shard_map/ppermute | solution.py:379
  24.7 0.0 collective-permute-start.10
  24.7 3.3 %collective-permute-done.9.xa = f32[184,128]{1,0:T(8,128)S(1)} collective-permute-done((f32[184,128]{1,0:T(8,128)S(1)}, f32[184,128]{1,0:T(8,128)S(1)}, u32[]{:S(2)}, u32[]{:S(2)}) %collective-permute-start.9) | collective-permute-done | bytes 94240 | tf_op jit(solution)/shard_map/ppermute | solution.py:379
  28.0 0.0 collective-permute-done.10.xb
  28.0 1.9 %finish.1 = (f32[2576,128]{1,0:T(8,128)S(1)}, f32[2560,128]{1,0:T(8,128)}, f32[256,128]{1,0:T(8,128)}, f32[2,5,4,16]{3,2,1,0:T(4,128)}) custom-call(f32[160,128]{1,0:T(8,128)S(1)} %get-tuple-element.42.from_left, f32[160,128]{1,0:T(8,128)S(1)} %get-tuple-element.43.from_right, ...), custom_call_target="tpu_custom_call", output_to_operand_aliasing={{0}: (2, {})} | custom-call | tf_op jit(solution)/shard_map/finish/pallas_call | solution.py:482
Async XLA Ops:
  2.5 7.4 %collective-permute-start = (f32[160,128]{1,0:T(8,128)S(1)}, f32[160,128]{1,0:T(8,128)S(1)}, u32[]{:S(2)}, u32[]{:S(2)}) collective-permute-start(f32[160,128]{1,0:T(8,128)S(1)} %get-tuple-element.45), channel_id=1, source_target_pairs={{0,4},{4,0},{8,12},{12,8},{1,5},{5,1},{9,13},{13,9},{2,6},{6,2},{1... | collective-permute-start | bytes 245768 | tf_op jit(solution)/shard_map/ppermute | solution.py:379
  5.6 4.3 %collective-permute-start.1 = (f32[160,128]{1,0:T(8,128)S(1)}, f32[160,128]{1,0:T(8,128)S(1)}, u32[]{:S(2)}, u32[]{:S(2)}) collective-permute-start(f32[160,128]{1,0:T(8,128)S(1)} %get-tuple-element.46), channel_id=1, source_target_pairs={{0,1},{1,0},{4,8},{5,9},{8,4},{9,5},{12,13},{13,12},{2,3},{3,2},{6... | collective-permute-start | bytes 245768 | tf_op jit(solution)/shard_map/ppermute | solution.py:389
  5.6 4.3 %collective-permute-start.2 = (f32[80,128]{1,0:T(8,128)S(1)}, f32[80,128]{1,0:T(8,128)S(1)}, u32[]{:S(2)}, u32[]{:S(2)}) collective-permute-start(f32[80,128]{1,0:T(8,128)S(1)} %get-tuple-element.47), channel_id=1, source_target_pairs={{0,1},{1,0},{2,3},{3,2},{4,5},{5,4},{6,7},{7,6},{8,9},{9,8},{10,11... | collective-permute-start | bytes 122888 | tf_op jit(solution)/shard_map/ppermute | solution.py:379
  6.1 3.8 %collective-permute-start.3 = (f32[16,384]{1,0:T(8,128)S(1)}, f32[16,384]{1,0:T(8,128)S(1)}, u32[]{:S(2)}, u32[]{:S(2)}) collective-permute-start(f32[16,384]{1,0:T(8,128)S(1)} %get-tuple-element.48), channel_id=1, source_target_pairs={{0,2},{2,0},{1,3},{3,1},{4,6},{6,4},{5,7},{7,5},{8,10},{10,8},{9,1... | collective-permute-start | bytes 73736 | tf_op jit(solution)/shard_map/ppermute | solution.py:379
  11.9 9.0 %collective-permute-start.6 = (f32[128,128]{1,0:T(8,128)S(1)}, f32[128,128]{1,0:T(8,128)S(1)}, u32[]{:S(2)}, u32[]{:S(2)}) collective-permute-start(f32[128,128]{1,0:T(8,128)S(1)} %get-tuple-element.56), channel_id=1, source_target_pairs={{0,4},{4,0},{8,12},{12,8},{1,5},{5,1},{9,13},{13,9},{2,6},{6,2},{1... | collective-permute-start | bytes 196616 | tf_op jit(solution)/shard_map/ppermute | solution.py:393
  14.6 7.3 %collective-permute-start.7 = (f32[128,128]{1,0:T(8,128)S(1)}, f32[128,128]{1,0:T(8,128)S(1)}, u32[]{:S(2)}, u32[]{:S(2)}) collective-permute-start(f32[128,128]{1,0:T(8,128)S(1)} %get-tuple-element.57), channel_id=1, source_target_pairs={{0,8},{4,12},{8,0},{12,4},{1,9},{5,13},{9,1},{13,5},{2,10},{6,14},... | collective-permute-start | bytes 196616 | tf_op jit(solution)/shard_map/ppermute | solution.py:393
  15.0 6.9 %collective-permute-start.8 = (f32[128,128]{1,0:T(8,128)S(1)}, f32[128,128]{1,0:T(8,128)S(1)}, u32[]{:S(2)}, u32[]{:S(2)}) collective-permute-start(f32[128,128]{1,0:T(8,128)S(1)} %get-tuple-element.58), channel_id=1, source_target_pairs={{0,12},{4,8},{8,4},{12,0},{1,13},{5,9},{9,5},{13,1},{2,14},{6,10},... | collective-permute-start | bytes 196616 | tf_op jit(solution)/shard_map/ppermute | solution.py:393
  17.0 3.8 %collective-permute-start.4 = (f32[80,128]{1,0:T(8,128)S(1)}, f32[80,128]{1,0:T(8,128)S(1)}, u32[]{:S(2)}, u32[]{:S(2)}) collective-permute-start(f32[80,128]{1,0:T(8,128)S(1)} %get-tuple-element.53), channel_id=1, source_target_pairs={{0,1},{1,0},{2,3},{3,2},{4,5},{5,4},{6,7},{7,6},{8,9},{9,8},{10,11... | collective-permute-start | bytes 122888 | tf_op jit(solution)/shard_map/ppermute | solution.py:379
  17.0 3.8 %collective-permute-start.5 = (f32[16,384]{1,0:T(8,128)S(1)}, f32[16,384]{1,0:T(8,128)S(1)}, u32[]{:S(2)}, u32[]{:S(2)}) collective-permute-start(f32[16,384]{1,0:T(8,128)S(1)} %get-tuple-element.54), channel_id=1, source_target_pairs={{0,2},{2,0},{1,3},{3,1},{4,6},{6,4},{5,7},{7,5},{8,10},{10,8},{9,1... | collective-permute-start | bytes 73736 | tf_op jit(solution)/shard_map/ppermute | solution.py:379
  23.3 4.6 %collective-permute-start.9 = (f32[184,128]{1,0:T(8,128)S(1)}, f32[184,128]{1,0:T(8,128)S(1)}, u32[]{:S(2)}, u32[]{:S(2)}) collective-permute-start(f32[184,128]{1,0:T(8,128)S(1)} %get-tuple-element.60.own_a), channel_id=1, source_target_pairs={{0,4},{4,0},{8,12},{12,8},{1,5},{5,1},{9,13},{13,9},{2,6},{6,2},{1... | collective-permute-start | bytes 282632 | tf_op jit(solution)/shard_map/ppermute | solution.py:379
  24.7 3.3 %collective-permute-start.10 = (f32[184,128]{1,0:T(8,128)S(1)}, f32[184,128]{1,0:T(8,128)S(1)}, u32[]{:S(2)}, u32[]{:S(2)}) collective-permute-start(f32[184,128]{1,0:T(8,128)S(1)} %get-tuple-element.61.own_b), channel_id=1, source_target_pairs={{0,1},{1,0},{4,8},{5,9},{8,4},{9,5},{12,13},{13,12},{2,3},{3,2},{6... | collective-permute-start | bytes 282632 | tf_op jit(solution)/shard_map/ppermute | solution.py:389

commit v4 on v3

--- a/solution.py
+++ b/solution.py
@@ -42,6 +42,12 @@
         self.groups = -(-FIELDS // self.per_group)
         self.parents = tiles // RATIO
         self.y_sends = 1 if n_gy == 2 else 2
+        self.part = self.capacity * levels
+        self.early = 2 if n_gx == 4 else 0
+        self.late = FIELDS - self.early
+
+    def riders(self, k):
+        return self.levels * (FIELDS if k == 1 else self.early if k == 3 else 0)
 
 
 def base_row(d, f, z):
@@ -113,9 +119,13 @@
 
 
 def x_halos(d, xa, xb, rows):
+    a, b = xa[rows, :], xb[rows, :]
+    return left_right(d, a, b)
+
+
+def left_right(d, a, b):
     me = lax.axis_index("gx")
     even = lax.rem(me, 2) == 0
-    a, b = xa[rows, :], xb[rows, :]
     left = jnp.where(me == 0, 0.0, jnp.where(even, b, a))
     right = jnp.where(me == d.n_gx - 1, 0.0, jnp.where(even, a, b))
     return left, right
@@ -230,9 +240,9 @@
     yq = refs[: d.y_sends]
     wall_coef, wind, diff, send_table = refs[d.y_sends : d.y_sends + 4]
     outs = refs[d.y_sends + 4 :]
-    pad, new_pad, factor, z_out = outs[:4]
-    yq_out = outs[4 : 4 + d.y_sends]
-    stress = outs[4 + d.y_sends :]
+    pad, new_pad, factor, z_out, head = outs[:5]
+    yq_out = outs[5 : 5 + d.y_sends]
+    stress = outs[5 + d.y_sends :]
     for f in range(FIELDS):
         set_x_halos(d, pad, f, *x_halos(d, xa, xb, slice(f * d.levels, (f + 1) * d.levels)))
     set_z_halos(d, pad, zface)
@@ -254,6 +264,14 @@
     for f in range(FIELDS):
         packed = add_edges(d, packed, new_pad, f, lane)
     write_y(d, yq_out, packed, lane)
+    first, second = x_choices(d)
+    targets = [(head, f * d.levels, f, 0) for f in range(FIELDS)]
+    targets += [(stress[1], d.part + f * d.levels, f, first) for f in range(FIELDS)]
+    targets += [(stress[3], d.part + i * d.levels, d.late + i, second) for i in range(d.early)]
+    for out, start, f, tile in targets:
+        out[start : start + d.levels, :] = new_pad[
+            pl.ds(base_row(d, f, 0) + FRONT + tile, d.levels, stride=d.block), :
+        ]
     z_level = jnp.where(lax.axis_index("gz") == 0, d.levels - 1, 0)
     for f in range(FIELDS):
         z_out[f * d.tiles : (f + 1) * d.tiles, :] = new_pad[
@@ -268,7 +286,7 @@
 def step_two_kernel(d, pad_in, factor, zface, *refs):
     yq = refs[: d.y_sends]
     masks_in, wind, diff = refs[d.y_sends : d.y_sends + 3]
-    pad, new_fields, coarse, xa_out, xb_out = refs[-5:]
+    pad, new_fields, own_sums, sent_sums, sent_b, coarse = refs[-6:]
     zero_x = jnp.zeros((d.levels, LANES), F32)
     for f in range(FIELDS):
         set_x_halos(d, pad, f, zero_x, zero_x)
@@ -302,29 +320,36 @@
         return carry
 
     lax.fori_loop(0, coarse_levels, coarse_level, 0)
-    edge = FIELDS * d.levels
-    for out, tile in zip((xa_out, xb_out), x_choices(d)):
-        for f in range(FIELDS):
-            out[f * d.levels : (f + 1) * d.levels, :] = pad[
-                pl.ds(base_row(d, f, 0) + FRONT + tile, d.levels, stride=d.block), :
-            ]
-        out[edge : edge + per_parent, :] = coarse[d.parents * per_parent :, :]
-
-
-def finish_kernel(d, from_left, from_right, state_in, xa, xb, own_a, own_b, coarse, parent_of, place_table, counts, *refs):
-    stress = refs[: d.n_gx]
+    own_sums[...] = coarse[: d.parents * per_parent, :]
+    sent_sums[...] = coarse[d.parents * per_parent :, :]
+    second = x_choices(d)[1]
+    for f in range(d.late):
+        sent_b[f * d.levels : (f + 1) * d.levels, :] = pad[
+            pl.ds(base_row(d, f, 0) + FRONT + second, d.levels, stride=d.block), :
+        ]
+    sent_b[d.late * d.levels :, :] = coarse[d.parents * per_parent :, :]
+
+
+def finish_kernel(d, from_left, from_right, state_in, head, coarse, *refs):
+    got_a, got_b, parent_of, place_table, counts = refs[:5]
+    stress, refs = refs[5 : 5 + d.n_gx], refs[5:]
     state, new_fields, wall_stress, parent_mean, terms, gathered, placed, sems = refs[d.n_gx :]
     me = lax.axis_index("gx")
     even = lax.rem(me, 2) == 0
     rows = d.levels * d.tiles
     coarse_levels = d.levels // RATIO
-    per_parent = coarse.shape[0] // (d.parents + 1)
+    per_parent = coarse.shape[0] // d.parents
     copies = []
     for f in range(FIELDS):
         cut = slice(f * d.levels, (f + 1) * d.levels)
-        left, right = x_halos(d, xa, xb, cut)
+        a = stress[1][d.part + f * d.levels : d.part + (f + 1) * d.levels, :]
+        if f < d.late:
+            b = got_b[cut, :]
+        else:
+            b = stress[3][d.part + (f - d.late) * d.levels : d.part + (f - d.late + 1) * d.levels, :]
+        left, right = left_right(d, a, b)
         left, right = from_left[cut, :] * left, from_right[cut, :] * right
-        ahead = from_right[cut, :] * jnp.where(even, own_b[cut, :], own_a[cut, :])
+        ahead = from_right[cut, :] * head[cut, :]
         for tile, added in ((0, left), (d.tiles - 1, right)):
             place = pl.ds(f * rows + tile, d.levels, stride=d.tiles)
             state[place, :] = state[place, :] + added
@@ -338,9 +363,9 @@
             terms[i * per_parent + f * coarse_levels : i * per_parent + (f + 1) * coarse_levels, :] = jnp.sum(
                 term.reshape(coarse_levels, RATIO, LANES), axis=1
             )
-    part = d.capacity * d.levels
+    part = d.part
     for k in range(d.n_gx):
-        gathered[k * part : (k + 1) * part, :] = stress[k][...]
+        gathered[k * part : (k + 1) * part, :] = stress[k][:part, :]
     for s in range(SLOTS):
         start = pl.multiple_of(place_table[s] * d.levels, 8)
         placed[pl.ds(s, d.levels, stride=SLOTS), :] = gathered[pl.ds(start, d.levels), :]
@@ -350,8 +375,7 @@
     if filled < per_parent:
         for i in range(3):
             terms[i * per_parent + filled : (i + 1) * per_parent, :] = jnp.zeros((per_parent - filled, LANES), F32)
-    edge = FIELDS * d.levels
-    got = jnp.where(even, xb[edge : edge + per_parent, :], xa[edge : edge + per_parent, :])
+    got = jnp.where(even, got_b[d.late * d.levels :, :], got_a[...])
     first_tile = me * d.tiles
     first_parent = parent_of[first_tile] - me * d.parents
     last_parent = parent_of[first_tile + d.tiles - 1] - me * d.parents
@@ -420,7 +444,6 @@
     x_t = pltpu.VMEM((FIELDS * levels, LANES), F32)
     z_t = pltpu.VMEM((FIELDS * tiles, LANES), F32)
     y_ts = [pltpu.VMEM((tiles, d.groups * LANES), F32)] * d.y_sends
-    stress_t = pltpu.VMEM((d.capacity * levels, LANES), F32)
 
     n_small = len(small)
     *small, pad, xa, xb, zface = (packed := pl.pallas_call(
@@ -451,11 +474,12 @@
         name="prepare",
     )(in_vmem(small[0]), *small[1:])
 
-    _, new_pad, factor, zface, *rest = pl.pallas_call(
+    _, new_pad, factor, zface, head, *rest = pl.pallas_call(
         functools.partial(step_one_kernel, d),
-        out_shape=[pad_t, pad_t, pltpu.VMEM(((levels + 1) * tiles, LANES), F32), z_t, *y_ts] + [stress_t] * d.n_gx,
+        out_shape=[pad_t, pad_t, pltpu.VMEM(((levels + 1) * tiles, LANES), F32), z_t, x_t, *y_ts]
+        + [pltpu.VMEM((d.part + d.riders(k), LANES), F32) for k in range(d.n_gx)],
         in_specs=[VM] * (5 + d.y_sends) + [SM] * 3,
-        out_specs=[VM] * (4 + d.y_sends + d.n_gx),
+        out_specs=[VM] * (5 + d.y_sends + d.n_gx),
         input_output_aliases={0: 0},
         compiler_params=params,
         name="step_one",
@@ -464,20 +488,25 @@
     faces = zy_swapped(d, zface, yq)
     stress = [stress[0]] + [in_vmem(crossed(stress[k], "gx", k)) for k in range(1, d.n_gx)]
 
-    early = stress[1:]
     per_parent = -(-FIELDS * (levels // RATIO) // 8) * 8
     state_t = pltpu.VMEM((rows + tiles, LANES), F32)
-    message_t = pltpu.VMEM((FIELDS * levels + per_parent, LANES), F32)
-    _, state, coarse, own_a, own_b = pl.pallas_call(
+    _, state, own_sums, sent_sums, sent_b = pl.pallas_call(
         functools.partial(step_two_kernel, d),
-        out_shape=[pad_t, state_t, pltpu.VMEM(((d.parents + 1) * per_parent, LANES), F32), message_t, message_t],
-        in_specs=[VM] * (4 + d.y_sends) + [SM] * 2 + [VM] * len(early),
+        out_shape=[
+            pad_t,
+            state_t,
+            pltpu.VMEM((d.parents * per_parent, LANES), F32),
+            pltpu.VMEM((per_parent, LANES), F32),
+            pltpu.VMEM((d.late * levels + per_parent, LANES), F32),
+        ],
+        in_specs=[VM] * (4 + d.y_sends) + [SM] * 2,
         out_specs=[VM] * 5,
+        scratch_shapes=[pltpu.VMEM(((d.parents + 1) * per_parent, LANES), F32)],
         input_output_aliases={0: 0},
         compiler_params=params,
         name="step_two",
-    )(in_vmem(new_pad), in_vmem(factor), *faces, in_vmem(masks), small[1], small[2], *early)
-    xs = x_swapped(own_a, own_b)
+    )(in_vmem(new_pad), in_vmem(factor), *faces, in_vmem(masks), small[1], small[2])
+    got = x_swapped(sent_sums, sent_b)
 
     _, new_fields, wall_stress, parent_mean = pl.pallas_call(
         functools.partial(finish_kernel, d),
@@ -487,7 +516,7 @@
             jax.ShapeDtypeStruct((levels * SLOTS, LANES), F32),
             jax.ShapeDtypeStruct((d.parents, FIELDS, levels // RATIO, columns // RATIO), F32),
         ],
-        in_specs=[VM] * 8 + [SM] * 3 + [VM] * d.n_gx,
+        in_specs=[VM] * 7 + [SM] * 3 + [VM] * d.n_gx,
         out_specs=[VM, hbm, hbm, VM],
         scratch_shapes=[
             pltpu.VMEM((3 * per_parent, LANES), F32),
@@ -499,7 +528,8 @@
         compiler_params=params,
         name="finish",
     )(
-        *[in_vmem(a) for a in (from_left, from_right, state, *xs, own_a, own_b, coarse)],
+        *[in_vmem(a) for a in (from_left, from_right, state, head, own_sums)],
+        *got,
         small[5],
         place_table,
         counts,

time: 30.1 us -> 27.3 us (0.907)
  waiting for transfers between devices: 8.28 us -> 6.46 us
  starting transfers between devices: 13.1 us -> 12.1 us
    ppermute x3, waiting for transfers between devices: 1.01 us -> 0.01 us  [crossed(): lax.ppermute(block, axis, [(i, i ^ distance) for i in range(lax.axis_size...]
    ppermute x3, starting transfers between devices: 5.14 us -> 4.33 us  [crossed(): lax.ppermute(block, axis, [(i, i ^ distance) for i in range(lax.axis_size...]
    ppermute x6, waiting for transfers between devices: 7.26 us -> 6.45 us  [swapped(): lax.ppermute(block, axis, [(i, i ^ 1) for i in range(lax.axis_size(axis))])]
  transfers between devices with their start and end apart: 11 -> 11, of which waited for: 4 -> 3; matrix products, arithmetic and copies ran while one was open for 0% -> 0% of each run, Pallas kernels for 2% -> 8%
where the time goes in v4:
time: 27.3 us; the launch traced here: 27.2 us
  starting transfers between devices  12.1 us (44%)
  Pallas kernels  7.9 us (29%)
  waiting for transfers between devices  6.46 us (24%)
  between operations  0.7 us (3%)
    ppermute x6, starting transfers between devices, swapped(): lax.ppermute(block, axis, [(i, i ^ 1) for i in range(lax.axis_size(axis))])  7.72 us
    ppermute x6, waiting for transfers between devices, swapped(): lax.ppermute(block, axis, [(i, i ^ 1) for i in range(lax.axis_size(axis))])  6.45 us
    ppermute x3, starting transfers between devices, crossed(): lax.ppermute(block, axis, [(i, i ^ distance) for i in range(lax.axis_size...  4.33 us
    pallas_call x1, Pallas kernels, body(): pl.pallas_call(functools.partial(step_one_kernel, d), out_shape=[pad_t, p...  1.96 us
    pallas_call x1, Pallas kernels, body(): pl.pallas_call(functools.partial(finish_kernel, d), out_shape=[state_t, j...  1.92 us
    pallas_call x1, Pallas kernels, body(): pl.pallas_call(functools.partial(pack_kernel, d), out_shape=[pltpu.SMEM(a...  1.87 us
    pallas_call x1, Pallas kernels, body(): pl.pallas_call(functools.partial(step_two_kernel, d), out_shape=[pad_t, s...  1.42 us
    pallas_call x1, Pallas kernels, body(): pl.pallas_call(functools.partial(prepare_kernel, d), out_shape=[pltpu.VME...  0.71 us
  transfers between devices with their start and end apart: 11, of which 3 were waited for; matrix products, arithmetic and copies ran while one was open for 0% of the time, Pallas kernels for 8%

profile of v4, /device:TPU:0, one launch (start us, length us, event | category | flops | bytes accessed | tf_op | source)
XLA Modules:
  0.0 27.2 jit_solution(18116627280334711551)
XLA Ops:
  0.6 1.9 %pack.1 = (s32[16,128]{1,0:T(8,128)S(1)}, f32[3,32]{1,0:T(4,128)S(4)}, f32[5]{0:T(128)S(4)}, s32[16]{0:T(128)S(4)}, s32[64]{0:T(128)S(4)}, /*index=5*/s32[64]{0:...) custom-call(f32[5,32,16,128]{3,2,1,0:T(8,128)} %fields.1, ...), custom_call_target="tpu_custom_call" | custom-call | tf_op jit(solution)/shard_map/pack/pallas_call | solution.py:449
  2.5 3.1 %collective-permute-start = (f32[160,128]{1,0:T(8,128)S(1)}, f32[160,128]{1,0:T(8,128)S(1)}, u32[]{:S(2)}, u32[]{:S(2)}) collective-permute-start(f32[160,128]{1,0:T(8,128)S(1)} %get-tuple-element.46), channel_id=1, source_target_pairs={{0,4},{4,0},{8,12},{12,8},{1,5},{5,1},{9,13},{13,9},{2,6},{6,2},{1... | collective-permute-start | bytes 245768 | tf_op jit(solution)/shard_map/ppermute | solution.py:403
  5.6 0.0 collective-permute-start.1
  5.6 0.5 %collective-permute-start.2 = (f32[80,128]{1,0:T(8,128)S(1)}, f32[80,128]{1,0:T(8,128)S(1)}, u32[]{:S(2)}, u32[]{:S(2)}) collective-permute-start(f32[80,128]{1,0:T(8,128)S(1)} %get-tuple-element.48), channel_id=1, source_target_pairs={{0,1},{1,0},{2,3},{3,2},{4,5},{5,4},{6,7},{7,6},{8,9},{9,8},{10,11... | collective-permute-start | bytes 122888 | tf_op jit(solution)/shard_map/ppermute | solution.py:403
  6.1 1.5 %collective-permute-start.3 = (f32[16,384]{1,0:T(8,128)S(1)}, f32[16,384]{1,0:T(8,128)S(1)}, u32[]{:S(2)}, u32[]{:S(2)}) collective-permute-start(f32[16,384]{1,0:T(8,128)S(1)} %get-tuple-element.49), channel_id=1, source_target_pairs={{0,2},{2,0},{1,3},{3,1},{4,6},{6,4},{5,7},{7,5},{8,10},{10,8},{9,1... | collective-permute-start | bytes 73736 | tf_op jit(solution)/shard_map/ppermute | solution.py:403
  7.6 0.7 %prepare.1 = (f32[16,128]{1,0:T(8,128)S(1)}, f32[160,128]{1,0:T(8,128)S(1)}, f32[160,128]{1,0:T(8,128)S(1)}, f32[48,128]{1,0:T(8,128)S(1)}, s32[16]{0:T(128)S(4)}, /*index=5*/s32[9]{0:T(128)S(4)}, s32[2]{0:T(128)S(4)}) custom-call(s32[16,128]{1,0:T(8,128)S(1)} %get-tuple-element.37.wall_type, f32[3,32]{1,0:T(4,128)S(4)} %get-tuple-element.38.wind.refs_2_, ...), custom_call_target="tpu_custom_call" | custom-call | tf_op jit(solution)/shard_map/prepare/pallas_call | solution.py:466
  8.3 1.6 %collective-permute-done.3.refs_0_ = f32[16,384]{1,0:T(8,128)S(1)} collective-permute-done((f32[16,384]{1,0:T(8,128)S(1)}, f32[16,384]{1,0:T(8,128)S(1)}, u32[]{:S(2)}, u32[]{:S(2)}) %collective-permute-start.3) | collective-permute-done | bytes 24608 | tf_op jit(solution)/shard_map/ppermute | solution.py:403
  9.9 0.0 collective-permute-done.2.zface
  9.9 0.0 collective-permute-done.xa
  9.9 0.0 collective-permute-done.1.xb
  10.0 2.0 %step_one.1 = (f32[4088,128]{1,0:T(8,128)S(1)}, f32[4088,128]{1,0:T(8,128)S(1)}, f32[528,128]{1,0:T(8,128)S(1)}, f32[80,128]{1,0:T(8,128)S(1)}, f32[160,128]{1,0...) custom-call(f32[4088,128]{1,0:T(8,128)S(1)} %get-tuple-element.45.pa, ...), custom_call_target="tpu_custom_call", output_to_operand_aliasing={{0}: (0, {})} | custom-call | tf_op jit(solution)/shard_map/step_one/pallas_call | solution.py:477
  11.9 2.7 %collective-permute-start.8 = (f32[288,128]{1,0:T(8,128)S(1)}, f32[288,128]{1,0:T(8,128)S(1)}, u32[]{:S(2)}, u32[]{:S(2)}) collective-permute-start(f32[288,128]{1,0:T(8,128)S(1)} %get-tuple-element.65), channel_id=1, source_target_pairs={{0,4},{4,0},{8,12},{12,8},{1,5},{5,1},{9,13},{13,9},{2,6},{6,2},{1... | collective-permute-start | bytes 442376 | tf_op jit(solution)/shard_map/ppermute | solution.py:417
  14.6 0.0 collective-permute-start.4
  14.6 1.5 %collective-permute-start.10 = (f32[192,128]{1,0:T(8,128)S(1)}, f32[192,128]{1,0:T(8,128)S(1)}, u32[]{:S(2)}, u32[]{:S(2)}) collective-permute-start(f32[192,128]{1,0:T(8,128)S(1)} %get-tuple-element.67), channel_id=1, source_target_pairs={{0,12},{4,8},{8,4},{12,0},{1,13},{5,9},{9,5},{13,1},{2,14},{6,10},... | collective-permute-start | bytes 294920 | tf_op jit(solution)/shard_map/ppermute | solution.py:417
  16.1 1.5 %collective-permute-start.5 = (f32[16,384]{1,0:T(8,128)S(1)}, f32[16,384]{1,0:T(8,128)S(1)}, u32[]{:S(2)}, u32[]{:S(2)}) collective-permute-start(f32[16,384]{1,0:T(8,128)S(1)} %get-tuple-element.55), channel_id=1, source_target_pairs={{0,2},{2,0},{1,3},{3,1},{4,6},{6,4},{5,7},{7,5},{8,10},{10,8},{9,1... | collective-permute-start | bytes 73736 | tf_op jit(solution)/shard_map/ppermute | solution.py:403
  17.6 0.1 collective-permute-start.9
  17.7 2.2 %collective-permute-done.5.refs_0_ = f32[16,384]{1,0:T(8,128)S(1)} collective-permute-done((f32[16,384]{1,0:T(8,128)S(1)}, f32[16,384]{1,0:T(8,128)S(1)}, u32[]{:S(2)}, u32[]{:S(2)}) %collective-permute-start.5) | collective-permute-done | bytes 24608 | tf_op jit(solution)/shard_map/ppermute | solution.py:403
  20.0 0.0 collective-permute-done.4.zface
  20.0 1.4 %step_two.1 = (f32[4088,128]{1,0:T(8,128)S(1)}, f32[2576,128]{1,0:T(8,128)S(1)}, f32[48,128]{1,0:T(8,128)S(1)}, f32[24,128]{1,0:T(8,128)S(1)}, f32[120,128]{1,0:T(8,128)S(1)}) custom-call(f32[4088,128]{1,0:T(8,128)S(1)} %get-tuple-element.52.pad_in, f32[528,128]{1,0:T(8,128)S(1)} %get-tuple-element.53.factor, ...), custom_call_target="tpu_custom_call", output_to_operand_aliasing={{0}: (0, {})} | custom-call | tf_op jit(solution)/shard_map/step_two/pallas_call | solution.py:493
  21.4 0.1 collective-permute-start.7
  21.5 1.1 %collective-permute-start.6 = (f32[24,128]{1,0:T(8,128)S(1)}, f32[24,128]{1,0:T(8,128)S(1)}, u32[]{:S(2)}, u32[]{:S(2)}) collective-permute-start(f32[24,128]{1,0:T(8,128)S(1)} %get-tuple-element.60), channel_id=1, source_target_pairs={{0,4},{4,0},{8,12},{12,8},{1,5},{5,1},{9,13},{13,9},{2,6},{6,2},{1... | collective-permute-start | bytes 36872 | tf_op jit(solution)/shard_map/ppermute | solution.py:403
  22.6 2.6 %collective-permute-done.6.refs_0_ = f32[24,128]{1,0:T(8,128)S(1)} collective-permute-done((f32[24,128]{1,0:T(8,128)S(1)}, f32[24,128]{1,0:T(8,128)S(1)}, u32[]{:S(2)}, u32[]{:S(2)}) %collective-permute-start.6) | collective-permute-done | bytes 12320 | tf_op jit(solution)/shard_map/ppermute | solution.py:403
  25.2 0.0 collective-permute-done.9.refs_7_
  25.2 0.0 collective-permute-done.10.refs_8_
  25.2 0.0 collective-permute-done.7.refs_1_
  25.2 0.0 collective-permute-done.8.refs_6_
  25.3 1.9 %finish.1 = (f32[2576,128]{1,0:T(8,128)S(1)}, f32[2560,128]{1,0:T(8,128)}, f32[256,128]{1,0:T(8,128)}, f32[2,5,4,16]{3,2,1,0:T(4,128)}) custom-call(f32[160,128]{1,0:T(8,128)S(1)} %get-tuple-element.43.from_left, f32[160,128]{1,0:T(8,128)S(1)} %get-tuple-element.44.from_right, ...), custom_call_target="tpu_custom_call", output_to_operand_aliasing={{0}: (2, {})} | custom-call | tf_op jit(solution)/shard_map/finish/pallas_call | solution.py:511
Async XLA Ops:
  2.5 7.4 %collective-permute-start = (f32[160,128]{1,0:T(8,128)S(1)}, f32[160,128]{1,0:T(8,128)S(1)}, u32[]{:S(2)}, u32[]{:S(2)}) collective-permute-start(f32[160,128]{1,0:T(8,128)S(1)} %get-tuple-element.46), channel_id=1, source_target_pairs={{0,4},{4,0},{8,12},{12,8},{1,5},{5,1},{9,13},{13,9},{2,6},{6,2},{1... | collective-permute-start | bytes 245768 | tf_op jit(solution)/shard_map/ppermute | solution.py:403
  5.6 4.3 %collective-permute-start.1 = (f32[160,128]{1,0:T(8,128)S(1)}, f32[160,128]{1,0:T(8,128)S(1)}, u32[]{:S(2)}, u32[]{:S(2)}) collective-permute-start(f32[160,128]{1,0:T(8,128)S(1)} %get-tuple-element.47), channel_id=1, source_target_pairs={{0,1},{1,0},{4,8},{5,9},{8,4},{9,5},{12,13},{13,12},{2,3},{3,2},{6... | collective-permute-start | bytes 245768 | tf_op jit(solution)/shard_map/ppermute | solution.py:413
  5.6 4.3 %collective-permute-start.2 = (f32[80,128]{1,0:T(8,128)S(1)}, f32[80,128]{1,0:T(8,128)S(1)}, u32[]{:S(2)}, u32[]{:S(2)}) collective-permute-start(f32[80,128]{1,0:T(8,128)S(1)} %get-tuple-element.48), channel_id=1, source_target_pairs={{0,1},{1,0},{2,3},{3,2},{4,5},{5,4},{6,7},{7,6},{8,9},{9,8},{10,11... | collective-permute-start | bytes 122888 | tf_op jit(solution)/shard_map/ppermute | solution.py:403
  6.1 3.8 %collective-permute-start.3 = (f32[16,384]{1,0:T(8,128)S(1)}, f32[16,384]{1,0:T(8,128)S(1)}, u32[]{:S(2)}, u32[]{:S(2)}) collective-permute-start(f32[16,384]{1,0:T(8,128)S(1)} %get-tuple-element.49), channel_id=1, source_target_pairs={{0,2},{2,0},{1,3},{3,1},{4,6},{6,4},{5,7},{7,5},{8,10},{10,8},{9,1... | collective-permute-start | bytes 73736 | tf_op jit(solution)/shard_map/ppermute | solution.py:403
  11.9 13.3 %collective-permute-start.8 = (f32[288,128]{1,0:T(8,128)S(1)}, f32[288,128]{1,0:T(8,128)S(1)}, u32[]{:S(2)}, u32[]{:S(2)}) collective-permute-start(f32[288,128]{1,0:T(8,128)S(1)} %get-tuple-element.65), channel_id=1, source_target_pairs={{0,4},{4,0},{8,12},{12,8},{1,5},{5,1},{9,13},{13,9},{2,6},{6,2},{1... | collective-permute-start | bytes 442376 | tf_op jit(solution)/shard_map/ppermute | solution.py:417
  14.6 5.3 %collective-permute-start.4 = (f32[80,128]{1,0:T(8,128)S(1)}, f32[80,128]{1,0:T(8,128)S(1)}, u32[]{:S(2)}, u32[]{:S(2)}) collective-permute-start(f32[80,128]{1,0:T(8,128)S(1)} %get-tuple-element.54), channel_id=1, source_target_pairs={{0,1},{1,0},{2,3},{3,2},{4,5},{5,4},{6,7},{7,6},{8,9},{9,8},{10,11... | collective-permute-start | bytes 122888 | tf_op jit(solution)/shard_map/ppermute | solution.py:403
  14.6 10.6 %collective-permute-start.10 = (f32[192,128]{1,0:T(8,128)S(1)}, f32[192,128]{1,0:T(8,128)S(1)}, u32[]{:S(2)}, u32[]{:S(2)}) collective-permute-start(f32[192,128]{1,0:T(8,128)S(1)} %get-tuple-element.67), channel_id=1, source_target_pairs={{0,12},{4,8},{8,4},{12,0},{1,13},{5,9},{9,5},{13,1},{2,14},{6,10},... | collective-permute-start | bytes 294920 | tf_op jit(solution)/shard_map/ppermute | solution.py:417
  16.1 3.8 %collective-permute-start.5 = (f32[16,384]{1,0:T(8,128)S(1)}, f32[16,384]{1,0:T(8,128)S(1)}, u32[]{:S(2)}, u32[]{:S(2)}) collective-permute-start(f32[16,384]{1,0:T(8,128)S(1)} %get-tuple-element.55), channel_id=1, source_target_pairs={{0,2},{2,0},{1,3},{3,1},{4,6},{6,4},{5,7},{7,5},{8,10},{10,8},{9,1... | collective-permute-start | bytes 73736 | tf_op jit(solution)/shard_map/ppermute | solution.py:403
  17.6 7.6 %collective-permute-start.9 = (f32[128,128]{1,0:T(8,128)S(1)}, f32[128,128]{1,0:T(8,128)S(1)}, u32[]{:S(2)}, u32[]{:S(2)}) collective-permute-start(f32[128,128]{1,0:T(8,128)S(1)} %get-tuple-element.66), channel_id=1, source_target_pairs={{0,8},{4,12},{8,0},{12,4},{1,9},{5,13},{9,1},{13,5},{2,10},{6,14},... | collective-permute-start | bytes 196616 | tf_op jit(solution)/shard_map/ppermute | solution.py:417
  21.4 3.8 %collective-permute-start.7 = (f32[120,128]{1,0:T(8,128)S(1)}, f32[120,128]{1,0:T(8,128)S(1)}, u32[]{:S(2)}, u32[]{:S(2)}) collective-permute-start(f32[120,128]{1,0:T(8,128)S(1)} %get-tuple-element.61), channel_id=1, source_target_pairs={{0,1},{1,0},{4,8},{5,9},{8,4},{9,5},{12,13},{13,12},{2,3},{3,2},{6... | collective-permute-start | bytes 184328 | tf_op jit(solution)/shard_map/ppermute | solution.py:413
  21.5 3.8 %collective-permute-start.6 = (f32[24,128]{1,0:T(8,128)S(1)}, f32[24,128]{1,0:T(8,128)S(1)}, u32[]{:S(2)}, u32[]{:S(2)}) collective-permute-start(f32[24,128]{1,0:T(8,128)S(1)} %get-tuple-element.60), channel_id=1, source_target_pairs={{0,4},{4,0},{8,12},{12,8},{1,5},{5,1},{9,13},{13,9},{2,6},{6,2},{1... | collective-permute-start | bytes 36872 | tf_op jit(solution)/shard_map/ppermute | solution.py:403

commit v5 on v4

--- a/solution.py
+++ b/solution.py
@@ -173,8 +173,8 @@
     return jnp.sqrt(u * u + v * v + w * w + 1.0)
 
 
-def prepare_kernel(d, wall_type, wind, diff, count, slot_of, parent_of, *outs):
-    wall_coef, from_left, from_right, masks, send_table, place_table, counts, tally = outs
+def prepare_kernel(d, pad, wall_type, wind, diff, count, slot_of, parent_of, *outs):
+    wall_coef, drag, from_left, from_right, masks, send_table, place_table, counts, tally = outs
     me = lax.axis_index("gx")
     first_tile = me * d.tiles
     row = lax.broadcasted_iota(jnp.int32, (d.tiles, LANES), 0)
@@ -188,7 +188,15 @@
     value = jnp.zeros((d.tiles, LANES), F32)
     for code, entry in enumerate(TABLE):
         value = jnp.where(kind == code, entry, value)
-    wall_coef[...] = value * strength
+    coef = value * strength
+    wall_coef[...] = coef
+
+    def level(z, carry):
+        at = [pl.ds(pl.multiple_of(base_row(d, f, z) + FRONT, 8), d.tiles) for f in range(3)]
+        drag[pl.ds(pl.multiple_of(z * d.tiles, 8), d.tiles), :] = STEP * (coef * speed(*(pad[a, :] for a in at)))
+        return carry
+
+    lax.fori_loop(0, d.levels, level, 0, unroll=8)
     for p in range(d.parents + 1):
         masks[p * d.tiles : (p + 1) * d.tiles, :] = jnp.where(owner == p, 1.0, 0.0)
     for z in range(d.levels):
@@ -238,8 +246,8 @@
 
 def step_one_kernel(d, pad_in, xa, xb, zface, *refs):
     yq = refs[: d.y_sends]
-    wall_coef, wind, diff, send_table = refs[d.y_sends : d.y_sends + 4]
-    outs = refs[d.y_sends + 4 :]
+    wall_coef, first_drag, wind, diff, send_table = refs[d.y_sends : d.y_sends + 5]
+    outs = refs[d.y_sends + 5 :]
     pad, new_pad, factor, z_out, head = outs[:5]
     yq_out = outs[5 : 5 + d.y_sends]
     stress = outs[5 + d.y_sends :]
@@ -252,7 +260,7 @@
 
     def level(z, carry):
         both = [stencil(d, pad, yq, wind, diff, f, z, lane) for f in range(FIELDS)]
-        drag = STEP * (coef * speed(*(both[f][0] for f in range(3))))
+        drag = first_drag[pl.ds(pl.multiple_of(z * d.tiles, 8), d.tiles), :]
         news = [both[f][1] - drag * both[f][0] if f < 3 else both[f][1] for f in range(FIELDS)]
         for f in range(FIELDS):
             new_pad[pl.ds(pl.multiple_of(base_row(d, f, z) + FRONT, 8), d.tiles), :] = news[f]
@@ -330,16 +338,30 @@
     sent_b[d.late * d.levels :, :] = coarse[d.parents * per_parent :, :]
 
 
-def finish_kernel(d, from_left, from_right, state_in, head, coarse, *refs):
+def flush_kernel(d, state, new_fields, sem):
+    copy = pltpu.make_async_copy(state.at[pl.ds(0, new_fields.shape[0]), :], new_fields, sem.at[0])
+    copy.start()
+    copy.wait()
+
+
+def finish_kernel(d, from_left, from_right, flushed, state_in, head, coarse, *refs):
     got_a, got_b, parent_of, place_table, counts = refs[:5]
     stress, refs = refs[5 : 5 + d.n_gx], refs[5:]
-    state, new_fields, wall_stress, parent_mean, terms, gathered, placed, sems = refs[d.n_gx :]
+    new_fields, state, wall_stress, parent_mean, terms, gathered, placed, mean_out, sems = refs[d.n_gx :]
     me = lax.axis_index("gx")
     even = lax.rem(me, 2) == 0
     rows = d.levels * d.tiles
     coarse_levels = d.levels // RATIO
     per_parent = coarse.shape[0] // d.parents
     copies = []
+    part = d.part
+    for k in range(d.n_gx):
+        gathered[k * part : (k + 1) * part, :] = stress[k][:part, :]
+    for s in range(SLOTS):
+        start = pl.multiple_of(place_table[s] * d.levels, 8)
+        placed[pl.ds(s, d.levels, stride=SLOTS), :] = gathered[pl.ds(start, d.levels), :]
+    copies.append(pltpu.make_async_copy(placed.at[pl.ds(0, d.levels * SLOTS), :], wall_stress, sems.at[2 * FIELDS]))
+    copies[-1].start()
     for f in range(FIELDS):
         cut = slice(f * d.levels, (f + 1) * d.levels)
         a = stress[1][d.part + f * d.levels : d.part + (f + 1) * d.levels, :]
@@ -353,24 +375,17 @@
         for tile, added in ((0, left), (d.tiles - 1, right)):
             place = pl.ds(f * rows + tile, d.levels, stride=d.tiles)
             state[place, :] = state[place, :] + added
-        copies.append(
-            pltpu.make_async_copy(
-                state.at[pl.ds(f * rows, rows), :], new_fields.at[pl.ds(f * rows, rows), :], sems.at[f]
-            )
-        )
-        copies[-1].start()
+        for i, tile in enumerate((0, d.tiles - 1)):
+            ends = [
+                array.at[pl.ds(f * rows, rows), :].reshape(d.levels, d.tiles, LANES).at[:, pl.ds(tile, 1), :]
+                for array in (state, new_fields)
+            ]
+            copies.append(pltpu.make_async_copy(*ends, sems.at[2 * f + i]))
+            copies[-1].start()
         for i, term in enumerate((left, right, ahead)):
             terms[i * per_parent + f * coarse_levels : i * per_parent + (f + 1) * coarse_levels, :] = jnp.sum(
                 term.reshape(coarse_levels, RATIO, LANES), axis=1
             )
-    part = d.part
-    for k in range(d.n_gx):
-        gathered[k * part : (k + 1) * part, :] = stress[k][:part, :]
-    for s in range(SLOTS):
-        start = pl.multiple_of(place_table[s] * d.levels, 8)
-        placed[pl.ds(s, d.levels, stride=SLOTS), :] = gathered[pl.ds(start, d.levels), :]
-    copies.append(pltpu.make_async_copy(placed.at[pl.ds(0, d.levels * SLOTS), :], wall_stress, sems.at[FIELDS]))
-    copies[-1].start()
     filled = FIELDS * coarse_levels
     if filled < per_parent:
         for i in range(3):
@@ -394,7 +409,9 @@
         total = jnp.dot(total, pick, precision=lax.Precision.HIGHEST, preferred_element_type=F32)
         mean = total / (jnp.full(total.shape, counts[p], jnp.int32).astype(F32) * (RATIO * RATIO))
         for f in range(FIELDS):
-            parent_mean[p, f] = mean[f * coarse_levels : (f + 1) * coarse_levels, : d.columns // RATIO]
+            mean_out[p, f] = mean[f * coarse_levels : (f + 1) * coarse_levels, : d.columns // RATIO]
+    copies.append(pltpu.make_async_copy(mean_out, parent_mean, sems.at[2 * FIELDS + 1]))
+    copies[-1].start()
     for copy in copies:
         copy.wait()
 
@@ -463,27 +480,28 @@
     def ints(n):
         return pltpu.SMEM((n,), jnp.int32)
 
-    wall_coef, from_left, from_right, masks, send_table, place_table, counts = pl.pallas_call(
+    wall_coef, drag, from_left, from_right, masks, send_table, place_table, counts = pl.pallas_call(
         functools.partial(prepare_kernel, d),
-        out_shape=[pltpu.VMEM((tiles, LANES), F32), x_t, x_t, pltpu.VMEM(((d.parents + 1) * tiles, LANES), F32)]
+        out_shape=[pltpu.VMEM((tiles, LANES), F32), pltpu.VMEM((levels * tiles, LANES), F32), x_t, x_t]
+        + [pltpu.VMEM(((d.parents + 1) * tiles, LANES), F32)]
         + [ints(d.n_gx * d.capacity), ints(SLOTS + 1), ints(d.parents)],
-        in_specs=[VM] + [SM] * 5,
-        out_specs=[VM] * 4 + [SM] * 3,
+        in_specs=[VM] * 2 + [SM] * 5,
+        out_specs=[VM] * 5 + [SM] * 3,
         scratch_shapes=[ints(d.n_gx)],
         compiler_params=params,
         name="prepare",
-    )(in_vmem(small[0]), *small[1:])
+    )(in_vmem(pad), in_vmem(small[0]), *small[1:])
 
     _, new_pad, factor, zface, head, *rest = pl.pallas_call(
         functools.partial(step_one_kernel, d),
         out_shape=[pad_t, pad_t, pltpu.VMEM(((levels + 1) * tiles, LANES), F32), z_t, x_t, *y_ts]
         + [pltpu.VMEM((d.part + d.riders(k), LANES), F32) for k in range(d.n_gx)],
-        in_specs=[VM] * (5 + d.y_sends) + [SM] * 3,
+        in_specs=[VM] * (6 + d.y_sends) + [SM] * 3,
         out_specs=[VM] * (5 + d.y_sends + d.n_gx),
         input_output_aliases={0: 0},
         compiler_params=params,
         name="step_one",
-    )(in_vmem(pad), *faces, in_vmem(wall_coef), small[1], small[2], send_table)
+    )(in_vmem(pad), *faces, in_vmem(wall_coef), in_vmem(drag), small[1], small[2], send_table)
     yq, stress = rest[: d.y_sends], rest[d.y_sends :]
     faces = zy_swapped(d, zface, yq)
     stress = [stress[0]] + [in_vmem(crossed(stress[k], "gx", k)) for k in range(1, d.n_gx)]
@@ -508,27 +526,41 @@
     )(in_vmem(new_pad), in_vmem(factor), *faces, in_vmem(masks), small[1], small[2])
     got = x_swapped(sent_sums, sent_b)
 
-    _, new_fields, wall_stress, parent_mean = pl.pallas_call(
+    flushed = pl.pallas_call(
+        functools.partial(flush_kernel, d),
+        out_shape=jax.ShapeDtypeStruct((rows, LANES), F32),
+        in_specs=[VM],
+        out_specs=hbm,
+        scratch_shapes=[pltpu.SemaphoreType.DMA((1,))],
+        compiler_params=params,
+        name="flush",
+    )(in_vmem(state))
+
+    new_fields, _, wall_stress, parent_mean = pl.pallas_call(
         functools.partial(finish_kernel, d),
         out_shape=[
+            jax.ShapeDtypeStruct((rows, LANES), F32),
             state_t,
-            jax.ShapeDtypeStruct((rows, LANES), F32),
             jax.ShapeDtypeStruct((levels * SLOTS, LANES), F32),
             jax.ShapeDtypeStruct((d.parents, FIELDS, levels // RATIO, columns // RATIO), F32),
         ],
-        in_specs=[VM] * 7 + [SM] * 3 + [VM] * d.n_gx,
-        out_specs=[VM, hbm, hbm, VM],
+        in_specs=[VM] * 2 + [hbm] + [VM] * 5 + [SM] * 3 + [VM] * d.n_gx,
+        out_specs=[hbm, VM, hbm, hbm],
         scratch_shapes=[
             pltpu.VMEM((3 * per_parent, LANES), F32),
             pltpu.VMEM((d.n_gx * d.capacity * levels, LANES), F32),
             pltpu.VMEM(((levels + 1) * SLOTS, LANES), F32),
-            pltpu.SemaphoreType.DMA((FIELDS + 1,)),
+            pltpu.VMEM((d.parents, FIELDS, levels // RATIO, columns // RATIO), F32),
+            pltpu.SemaphoreType.DMA((2 * FIELDS + 2,)),
         ],
-        input_output_aliases={2: 0},
+        input_output_aliases={2: 0, 3: 1},
         compiler_params=params,
         name="finish",
     )(
-        *[in_vmem(a) for a in (from_left, from_right, state, head, own_sums)],
+        in_vmem(from_left),
+        in_vmem(from_right),
+        flushed,
+        *[in_vmem(a) for a in (state, head, own_sums)],
         *got,
         small[5],
         place_table,

time: 27.3 us -> 26.5 us (0.971)
  waiting for transfers between devices: 6.46 us -> 5.25 us
  Pallas kernels: 7.9 us -> 8.25 us
    ppermute x6, waiting for transfers between devices: 6.45 us -> 5.23 us  [swapped(): lax.ppermute(block, axis, [(i, i ^ 1) for i in range(lax.axis_size(axis))])]
    pallas_call x1 -> x2, Pallas kernels: 1.92 us -> 2.16 us  [the longest x1 1.1 us: body(): pl.pallas_call(functools.partial(finish_kernel, d), out_shape=[jax.ShapeD...]
  transfers between devices with their start and end apart: 11 -> 11, of which waited for: 3 -> 3; matrix products, arithmetic and copies ran while one was open for 0% -> 0% of each run, Pallas kernels for 8% -> 13%
where the time goes in v5:
time: 26.5 us; the launch traced here: 26.3 us
  starting transfers between devices  12.1 us (46%)
  Pallas kernels  8.25 us (31%)
  waiting for transfers between devices  5.25 us (20%)
  between operations  0.7 us (3%)
    ppermute x6, starting transfers between devices, swapped(): lax.ppermute(block, axis, [(i, i ^ 1) for i in range(lax.axis_size(axis))])  7.72 us
    ppermute x6, waiting for transfers between devices, swapped(): lax.ppermute(block, axis, [(i, i ^ 1) for i in range(lax.axis_size(axis))])  5.23 us
    ppermute x3, starting transfers between devices, crossed(): lax.ppermute(block, axis, [(i, i ^ distance) for i in range(lax.axis_size...  4.33 us
    pallas_call x1, Pallas kernels, body(): pl.pallas_call(functools.partial(step_one_kernel, d), out_shape=[pad_t, p...  1.94 us
    pallas_call x1, Pallas kernels, body(): pl.pallas_call(functools.partial(pack_kernel, d), out_shape=[pltpu.SMEM(a...  1.87 us
    pallas_call x1, Pallas kernels, body(): pl.pallas_call(functools.partial(step_two_kernel, d), out_shape=[pad_t, s...  1.42 us
    pallas_call x1, Pallas kernels, body(): pl.pallas_call(functools.partial(finish_kernel, d), out_shape=[jax.ShapeD...  1.1 us
    pallas_call x1, Pallas kernels, body(): pl.pallas_call(functools.partial(flush_kernel, d), out_shape=jax.ShapeDty...  1.06 us
  transfers between devices with their start and end apart: 11, of which 3 were waited for; matrix products, arithmetic and copies ran while one was open for 0% of the time, Pallas kernels for 13%

profile of v5, /device:TPU:0, one launch (start us, length us, event | category | flops | bytes accessed | tf_op | source)
XLA Modules:
  0.0 26.3 jit_solution(6938476881733661238)
XLA Ops:
  0.6 1.9 %pack.1 = (s32[16,128]{1,0:T(8,128)S(1)}, f32[3,32]{1,0:T(4,128)S(4)}, f32[5]{0:T(128)S(4)}, s32[16]{0:T(128)S(4)}, s32[64]{0:T(128)S(4)}, /*index=5*/s32[64]{0:...) custom-call(f32[5,32,16,128]{3,2,1,0:T(8,128)} %fields.1, ...), custom_call_target="tpu_custom_call" | custom-call | tf_op jit(solution)/shard_map/pack/pallas_call | solution.py:466
  2.5 3.1 %collective-permute-start = (f32[160,128]{1,0:T(8,128)S(1)}, f32[160,128]{1,0:T(8,128)S(1)}, u32[]{:S(2)}, u32[]{:S(2)}) collective-permute-start(f32[160,128]{1,0:T(8,128)S(1)} %get-tuple-element.47), channel_id=1, source_target_pairs={{0,4},{4,0},{8,12},{12,8},{1,5},{5,1},{9,13},{13,9},{2,6},{6,2},{1... | collective-permute-start | bytes 245768 | tf_op jit(solution)/shard_map/ppermute | solution.py:420
  5.6 0.0 collective-permute-start.1
  5.6 0.5 %collective-permute-start.2 = (f32[80,128]{1,0:T(8,128)S(1)}, f32[80,128]{1,0:T(8,128)S(1)}, u32[]{:S(2)}, u32[]{:S(2)}) collective-permute-start(f32[80,128]{1,0:T(8,128)S(1)} %get-tuple-element.49), channel_id=1, source_target_pairs={{0,1},{1,0},{2,3},{3,2},{4,5},{5,4},{6,7},{7,6},{8,9},{9,8},{10,11... | collective-permute-start | bytes 122888 | tf_op jit(solution)/shard_map/ppermute | solution.py:420
  6.1 1.5 %collective-permute-start.3 = (f32[16,384]{1,0:T(8,128)S(1)}, f32[16,384]{1,0:T(8,128)S(1)}, u32[]{:S(2)}, u32[]{:S(2)}) collective-permute-start(f32[16,384]{1,0:T(8,128)S(1)} %get-tuple-element.50), channel_id=1, source_target_pairs={{0,2},{2,0},{1,3},{3,1},{4,6},{6,4},{5,7},{7,5},{8,10},{10,8},{9,1... | collective-permute-start | bytes 73736 | tf_op jit(solution)/shard_map/ppermute | solution.py:420
  7.6 0.9 %prepare.1 = (f32[16,128]{1,0:T(8,128)S(1)}, f32[512,128]{1,0:T(8,128)S(1)}, f32[160,128]{1,0:T(8,128)S(1)}, f32[160,128]{1,0:T(8,128)S(1)}, f32[48,128]{1,0:T(8...) custom-call(f32[4088,128]{1,0:T(8,128)S(1)} %get-tuple-element.38.pad.pad_in, ...), custom_call_target="tpu_custom_call" | custom-call | tf_op jit(solution)/shard_map/prepare/pallas_call | solution.py:483
  8.5 1.5 %collective-permute-done.3.refs_0_ = f32[16,384]{1,0:T(8,128)S(1)} collective-permute-done((f32[16,384]{1,0:T(8,128)S(1)}, f32[16,384]{1,0:T(8,128)S(1)}, u32[]{:S(2)}, u32[]{:S(2)}) %collective-permute-start.3) | collective-permute-done | bytes 24608 | tf_op jit(solution)/shard_map/ppermute | solution.py:420
  9.9 0.0 collective-permute-done.2.zface
  9.9 0.0 collective-permute-done.xa
  9.9 0.0 collective-permute-done.1.xb
  10.0 1.9 %step_one.1 = (f32[4088,128]{1,0:T(8,128)S(1)}, f32[4088,128]{1,0:T(8,128)S(1)}, f32[528,128]{1,0:T(8,128)S(1)}, f32[80,128]{1,0:T(8,128)S(1)}, f32[160,128]{1,0...) custom-call(f32[4088,128]{1,0:T(8,128)S(1)} %get-tuple-element.38.pa, ...), custom_call_target="tpu_custom_call", output_to_operand_aliasing={{0}: (0, {})} | custom-call | tf_op jit(solution)/shard_map/step_one/pallas_call | solution.py:495
  11.9 2.7 %collective-permute-start.8 = (f32[288,128]{1,0:T(8,128)S(1)}, f32[288,128]{1,0:T(8,128)S(1)}, u32[]{:S(2)}, u32[]{:S(2)}) collective-permute-start(f32[288,128]{1,0:T(8,128)S(1)} %get-tuple-element.67), channel_id=1, source_target_pairs={{0,4},{4,0},{8,12},{12,8},{1,5},{5,1},{9,13},{13,9},{2,6},{6,2},{1... | collective-permute-start | bytes 442376 | tf_op jit(solution)/shard_map/ppermute | solution.py:434
  14.6 0.0 collective-permute-start.4
  14.6 1.5 %collective-permute-start.10 = (f32[192,128]{1,0:T(8,128)S(1)}, f32[192,128]{1,0:T(8,128)S(1)}, u32[]{:S(2)}, u32[]{:S(2)}) collective-permute-start(f32[192,128]{1,0:T(8,128)S(1)} %get-tuple-element.69), channel_id=1, source_target_pairs={{0,12},{4,8},{8,4},{12,0},{1,13},{5,9},{9,5},{13,1},{2,14},{6,10},... | collective-permute-start | bytes 294920 | tf_op jit(solution)/shard_map/ppermute | solution.py:434
  16.1 1.5 %collective-permute-start.5 = (f32[16,384]{1,0:T(8,128)S(1)}, f32[16,384]{1,0:T(8,128)S(1)}, u32[]{:S(2)}, u32[]{:S(2)}) collective-permute-start(f32[16,384]{1,0:T(8,128)S(1)} %get-tuple-element.57), channel_id=1, source_target_pairs={{0,2},{2,0},{1,3},{3,1},{4,6},{6,4},{5,7},{7,5},{8,10},{10,8},{9,1... | collective-permute-start | bytes 73736 | tf_op jit(solution)/shard_map/ppermute | solution.py:420
  17.6 0.1 collective-permute-start.9
  17.7 2.2 %collective-permute-done.5.refs_0_ = f32[16,384]{1,0:T(8,128)S(1)} collective-permute-done((f32[16,384]{1,0:T(8,128)S(1)}, f32[16,384]{1,0:T(8,128)S(1)}, u32[]{:S(2)}, u32[]{:S(2)}) %collective-permute-start.5) | collective-permute-done | bytes 24608 | tf_op jit(solution)/shard_map/ppermute | solution.py:420
  19.9 0.0 collective-permute-done.4.zface
  19.9 1.4 %step_two.1 = (f32[4088,128]{1,0:T(8,128)S(1)}, f32[2576,128]{1,0:T(8,128)S(1)}, f32[48,128]{1,0:T(8,128)S(1)}, f32[24,128]{1,0:T(8,128)S(1)}, f32[120,128]{1,0:T(8,128)S(1)}) custom-call(f32[4088,128]{1,0:T(8,128)S(1)} %get-tuple-element.54.pad_in, f32[528,128]{1,0:T(8,128)S(1)} %get-tuple-element.55.factor, ...), custom_call_target="tpu_custom_call", output_to_operand_aliasing={{0}: (0, {})} | custom-call | tf_op jit(solution)/shard_map/step_two/pallas_call | solution.py:511
  21.4 0.1 collective-permute-start.7
  21.4 1.1 %collective-permute-start.6 = (f32[24,128]{1,0:T(8,128)S(1)}, f32[24,128]{1,0:T(8,128)S(1)}, u32[]{:S(2)}, u32[]{:S(2)}) collective-permute-start(f32[24,128]{1,0:T(8,128)S(1)} %get-tuple-element.62), channel_id=1, source_target_pairs={{0,4},{4,0},{8,12},{12,8},{1,5},{5,1},{9,13},{13,9},{2,6},{6,2},{1... | collective-permute-start | bytes 36872 | tf_op jit(solution)/shard_map/ppermute | solution.py:420
  22.6 1.1 %flush.1.flushed = f32[2560,128]{1,0:T(8,128)} custom-call(f32[2576,128]{1,0:T(8,128)S(1)} %get-tuple-element.59.state.state_in), custom_call_target="tpu_custom_call" | custom-call | tf_op jit(solution)/shard_map/flush/pallas_call | solution.py:529
  23.7 1.5 %collective-permute-done.6.refs_0_ = f32[24,128]{1,0:T(8,128)S(1)} collective-permute-done((f32[24,128]{1,0:T(8,128)S(1)}, f32[24,128]{1,0:T(8,128)S(1)}, u32[]{:S(2)}, u32[]{:S(2)}) %collective-permute-start.6) | collective-permute-done | bytes 12320 | tf_op jit(solution)/shard_map/ppermute | solution.py:420
  25.2 0.0 collective-permute-done.9.refs_7_
  25.2 0.0 collective-permute-done.10.refs_8_
  25.2 0.0 collective-permute-done.7.refs_1_
  25.2 0.0 collective-permute-done.8.refs_6_
  25.2 1.1 %finish.1 = (f32[2560,128]{1,0:T(8,128)}, f32[2576,128]{1,0:T(8,128)S(1)}, f32[256,128]{1,0:T(8,128)}, f32[2,5,4,16]{3,2,1,0:T(4,128)}) custom-call(f32[160,128]{1,0:T(8,128)S(1)} %get-tuple-element.45.from_left, f32[160,128]{1,0:T(8,128)S(1)} %get-tuple-element.46.from_right, ...), custom_call_target="tpu_custom_call", output_to_operand_aliasing={{0}: (2, {}), {1}: (3, {})} | custom-call | tf_op jit(solution)/shard_map/finish/pallas_call | solution.py:539
Async XLA Ops:
  2.5 7.4 %collective-permute-start = (f32[160,128]{1,0:T(8,128)S(1)}, f32[160,128]{1,0:T(8,128)S(1)}, u32[]{:S(2)}, u32[]{:S(2)}) collective-permute-start(f32[160,128]{1,0:T(8,128)S(1)} %get-tuple-element.47), channel_id=1, source_target_pairs={{0,4},{4,0},{8,12},{12,8},{1,5},{5,1},{9,13},{13,9},{2,6},{6,2},{1... | collective-permute-start | bytes 245768 | tf_op jit(solution)/shard_map/ppermute | solution.py:420
  5.6 4.3 %collective-permute-start.1 = (f32[160,128]{1,0:T(8,128)S(1)}, f32[160,128]{1,0:T(8,128)S(1)}, u32[]{:S(2)}, u32[]{:S(2)}) collective-permute-start(f32[160,128]{1,0:T(8,128)S(1)} %get-tuple-element.48), channel_id=1, source_target_pairs={{0,1},{1,0},{4,8},{5,9},{8,4},{9,5},{12,13},{13,12},{2,3},{3,2},{6... | collective-permute-start | bytes 245768 | tf_op jit(solution)/shard_map/ppermute | solution.py:430
  5.6 4.3 %collective-permute-start.2 = (f32[80,128]{1,0:T(8,128)S(1)}, f32[80,128]{1,0:T(8,128)S(1)}, u32[]{:S(2)}, u32[]{:S(2)}) collective-permute-start(f32[80,128]{1,0:T(8,128)S(1)} %get-tuple-element.49), channel_id=1, source_target_pairs={{0,1},{1,0},{2,3},{3,2},{4,5},{5,4},{6,7},{7,6},{8,9},{9,8},{10,11... | collective-permute-start | bytes 122888 | tf_op jit(solution)/shard_map/ppermute | solution.py:420
  6.1 3.8 %collective-permute-start.3 = (f32[16,384]{1,0:T(8,128)S(1)}, f32[16,384]{1,0:T(8,128)S(1)}, u32[]{:S(2)}, u32[]{:S(2)}) collective-permute-start(f32[16,384]{1,0:T(8,128)S(1)} %get-tuple-element.50), channel_id=1, source_target_pairs={{0,2},{2,0},{1,3},{3,1},{4,6},{6,4},{5,7},{7,5},{8,10},{10,8},{9,1... | collective-permute-start | bytes 73736 | tf_op jit(solution)/shard_map/ppermute | solution.py:420
  11.9 13.3 %collective-permute-start.8 = (f32[288,128]{1,0:T(8,128)S(1)}, f32[288,128]{1,0:T(8,128)S(1)}, u32[]{:S(2)}, u32[]{:S(2)}) collective-permute-start(f32[288,128]{1,0:T(8,128)S(1)} %get-tuple-element.67), channel_id=1, source_target_pairs={{0,4},{4,0},{8,12},{12,8},{1,5},{5,1},{9,13},{13,9},{2,6},{6,2},{1... | collective-permute-start | bytes 442376 | tf_op jit(solution)/shard_map/ppermute | solution.py:434
  14.6 5.3 %collective-permute-start.4 = (f32[80,128]{1,0:T(8,128)S(1)}, f32[80,128]{1,0:T(8,128)S(1)}, u32[]{:S(2)}, u32[]{:S(2)}) collective-permute-start(f32[80,128]{1,0:T(8,128)S(1)} %get-tuple-element.56), channel_id=1, source_target_pairs={{0,1},{1,0},{2,3},{3,2},{4,5},{5,4},{6,7},{7,6},{8,9},{9,8},{10,11... | collective-permute-start | bytes 122888 | tf_op jit(solution)/shard_map/ppermute | solution.py:420
  14.6 10.6 %collective-permute-start.10 = (f32[192,128]{1,0:T(8,128)S(1)}, f32[192,128]{1,0:T(8,128)S(1)}, u32[]{:S(2)}, u32[]{:S(2)}) collective-permute-start(f32[192,128]{1,0:T(8,128)S(1)} %get-tuple-element.69), channel_id=1, source_target_pairs={{0,12},{4,8},{8,4},{12,0},{1,13},{5,9},{9,5},{13,1},{2,14},{6,10},... | collective-permute-start | bytes 294920 | tf_op jit(solution)/shard_map/ppermute | solution.py:434
  16.1 3.8 %collective-permute-start.5 = (f32[16,384]{1,0:T(8,128)S(1)}, f32[16,384]{1,0:T(8,128)S(1)}, u32[]{:S(2)}, u32[]{:S(2)}) collective-permute-start(f32[16,384]{1,0:T(8,128)S(1)} %get-tuple-element.57), channel_id=1, source_target_pairs={{0,2},{2,0},{1,3},{3,1},{4,6},{6,4},{5,7},{7,5},{8,10},{10,8},{9,1... | collective-permute-start | bytes 73736 | tf_op jit(solution)/shard_map/ppermute | solution.py:420
  17.6 7.6 %collective-permute-start.9 = (f32[128,128]{1,0:T(8,128)S(1)}, f32[128,128]{1,0:T(8,128)S(1)}, u32[]{:S(2)}, u32[]{:S(2)}) collective-permute-start(f32[128,128]{1,0:T(8,128)S(1)} %get-tuple-element.68), channel_id=1, source_target_pairs={{0,8},{4,12},{8,0},{12,4},{1,9},{5,13},{9,1},{13,5},{2,10},{6,14},... | collective-permute-start | bytes 196616 | tf_op jit(solution)/shard_map/ppermute | solution.py:434
  21.4 3.8 %collective-permute-start.7 = (f32[120,128]{1,0:T(8,128)S(1)}, f32[120,128]{1,0:T(8,128)S(1)}, u32[]{:S(2)}, u32[]{:S(2)}) collective-permute-start(f32[120,128]{1,0:T(8,128)S(1)} %get-tuple-element.63), channel_id=1, source_target_pairs={{0,1},{1,0},{4,8},{5,9},{8,4},{9,5},{12,13},{13,12},{2,3},{3,2},{6... | collective-permute-start | bytes 184328 | tf_op jit(solution)/shard_map/ppermute | solution.py:430
  21.4 3.8 %collective-permute-start.6 = (f32[24,128]{1,0:T(8,128)S(1)}, f32[24,128]{1,0:T(8,128)S(1)}, u32[]{:S(2)}, u32[]{:S(2)}) collective-permute-start(f32[24,128]{1,0:T(8,128)S(1)} %get-tuple-element.62), channel_id=1, source_target_pairs={{0,4},{4,0},{8,12},{12,8},{1,5},{5,1},{9,13},{13,9},{2,6},{6,2},{1... | collective-permute-start | bytes 36872 | tf_op jit(solution)/shard_map/ppermute | solution.py:420

commit v6 on v5

--- a/solution.py
+++ b/solution.py
@@ -63,11 +63,15 @@
     return [jnp.where(even, d.tiles - 1, 0), jnp.where(even, 0, d.tiles - 1)]
 
 
-def add_edges(d, packed, pad, f, lane):
+def add_edges(d, packed, pad, f, lane, raw=None):
     pair = lax.rem(lax.shift_right_logical(lane + 1, 1), LANES // 2)
     g = f // d.per_group
     for z in range(d.levels):
-        cells = pad[pl.ds(base_row(d, f, z) + FRONT, d.tiles), :]
+        if raw is None:
+            cells = pad[pl.ds(base_row(d, f, z) + FRONT, d.tiles), :]
+        else:
+            cells = raw[f, z]
+            pad[pl.ds(base_row(d, f, z) + FRONT, d.tiles), :] = cells
         place = lane_of(d, f, z)
         moved = pltpu.roll(cells, place, 1) if place else cells
         packed[g] = jnp.where(pair == place // 2, moved, packed[g])
@@ -88,24 +92,28 @@
 def pack_kernel(d, fields, *refs):
     n_small = len(refs[: (len(refs) - 5 - d.y_sends) // 2])
     small, refs = refs[:n_small], refs[n_small:]
-    small_out, (pad, xa, xb, zface), yq = refs[:n_small], refs[n_small : n_small + 4], refs[n_small + 4 : -1]
-    sems = refs[-1]
+    small_out, (pad, xa, xb, zface), yq = refs[:n_small], refs[n_small : n_small + 4], refs[n_small + 4 : -2]
+    raw, sems = refs[-2:]
     lane = lax.broadcasted_iota(jnp.int32, (d.tiles, LANES), 1)
     copies = []
     for f in range(FIELDS):
-        blocks = pad.at[pl.ds(base_row(d, f, 0), d.levels * d.block), :].reshape(d.levels, d.block, LANES)
-        copies.append(pltpu.make_async_copy(fields.at[f], blocks.at[:, pl.ds(FRONT, d.tiles), :], sems.at[f]))
+        copies.append(pltpu.make_async_copy(fields.at[f], raw.at[f], sems.at[f]))
     moves = [
         pltpu.make_async_copy(source, target, sems.at[FIELDS + i])
         for i, (source, target) in enumerate(zip(small, small_out))
     ]
     for copy in copies + moves:
         copy.start()
+    zero_x = jnp.zeros((d.levels, LANES), F32)
+    for f in range(FIELDS):
+        set_x_halos(d, pad, f, zero_x, zero_x)
+        for z in (-1, d.levels):
+            pad[pl.ds(base_row(d, f, z) + FRONT, d.tiles), :] = jnp.zeros((d.tiles, LANES), F32)
     z_out = jnp.where(lax.axis_index("gz") == 0, d.levels - 1, 0)
     packed = [jnp.zeros((d.tiles, LANES), F32)] * d.groups
     for f in range(FIELDS):
         copies[f].wait()
-        packed = add_edges(d, packed, pad, f, lane)
+        packed = add_edges(d, packed, pad, f, lane, raw)
         for out, tile in zip((xa, xb), x_choices(d)):
             out[f * d.levels : (f + 1) * d.levels, :] = pad[
                 pl.ds(base_row(d, f, 0) + FRONT + tile, d.levels, stride=d.block), :
@@ -144,6 +152,14 @@
         pad[pl.ds(base_row(d, f, d.levels) + FRONT, d.tiles), :] = jnp.where(low, face, 0.0)
 
 
+def y_halo(d, yq, f, z):
+    g = f // d.per_group
+    halo = yq[0][:, g * LANES : (g + 1) * LANES]
+    if d.y_sends == 2:
+        halo = halo + yq[1][:, g * LANES : (g + 1) * LANES]
+    return pltpu.roll(halo, LANES - 1 - lane_of(d, f, z), 1)
+
+
 def stencil(d, pad, yq, wind, diff, f, z, lane):
     base = base_row(d, f, z)
     v = pad[pl.ds(pl.multiple_of(base + FRONT, 8), d.tiles), :]
@@ -151,11 +167,7 @@
     xp = pad[pl.ds(base + FRONT + 1, d.tiles), :]
     zm = pad[pl.ds(pl.multiple_of(base + FRONT - d.block, 8), d.tiles), :]
     zp = pad[pl.ds(pl.multiple_of(base + FRONT + d.block, 8), d.tiles), :]
-    g = f // d.per_group
-    halo = yq[0][:, g * LANES : (g + 1) * LANES]
-    if d.y_sends == 2:
-        halo = halo + yq[1][:, g * LANES : (g + 1) * LANES]
-    halo = pltpu.roll(halo, LANES - 1 - lane_of(d, f, z), 1)
+    halo = 0.0 if yq is None else y_halo(d, yq, f, z)
     yp = jnp.where(lane == d.columns - 1, halo, pltpu.roll(v, LANES - 1, 1))
     ym = jnp.where(lane == 0, halo, pltpu.roll(v, 1, 1))
     spread = STEP * diff[f]
@@ -174,7 +186,7 @@
 
 
 def prepare_kernel(d, pad, wall_type, wind, diff, count, slot_of, parent_of, *outs):
-    wall_coef, drag, from_left, from_right, masks, send_table, place_table, counts, tally = outs
+    new_pad, wall_coef, from_left, from_right, masks, send_table, place_table, counts, tally = outs
     me = lax.axis_index("gx")
     first_tile = me * d.tiles
     row = lax.broadcasted_iota(jnp.int32, (d.tiles, LANES), 0)
@@ -191,9 +203,14 @@
     coef = value * strength
     wall_coef[...] = coef
 
+    lane = lax.broadcasted_iota(jnp.int32, (d.tiles, LANES), 1)
+
     def level(z, carry):
-        at = [pl.ds(pl.multiple_of(base_row(d, f, z) + FRONT, 8), d.tiles) for f in range(3)]
-        drag[pl.ds(pl.multiple_of(z * d.tiles, 8), d.tiles), :] = STEP * (coef * speed(*(pad[a, :] for a in at)))
+        both = [stencil(d, pad, None, wind, diff, f, z, lane) for f in range(FIELDS)]
+        drag = STEP * (coef * speed(*(both[f][0] for f in range(3))))
+        for f in range(FIELDS):
+            new = both[f][1] - drag * both[f][0] if f < 3 else both[f][1]
+            new_pad[pl.ds(pl.multiple_of(base_row(d, f, z) + FRONT, 8), d.tiles), :] = new
         return carry
 
     lax.fori_loop(0, d.levels, level, 0, unroll=8)
@@ -246,29 +263,50 @@
 
 def step_one_kernel(d, pad_in, xa, xb, zface, *refs):
     yq = refs[: d.y_sends]
-    wall_coef, first_drag, wind, diff, send_table = refs[d.y_sends : d.y_sends + 5]
-    outs = refs[d.y_sends + 5 :]
+    wall_coef, from_left, from_right, wind, diff, send_table = refs[d.y_sends : d.y_sends + 6]
+    outs = refs[d.y_sends + 6 :]
     pad, new_pad, factor, z_out, head = outs[:5]
     yq_out = outs[5 : 5 + d.y_sends]
     stress = outs[5 + d.y_sends :]
-    for f in range(FIELDS):
-        set_x_halos(d, pad, f, *x_halos(d, xa, xb, slice(f * d.levels, (f + 1) * d.levels)))
-    set_z_halos(d, pad, zface)
+    low = lax.axis_index("gz") == 0
+    end = jnp.where(low, d.levels - 1, 0)
+    changed = []
+    for f in range(FIELDS):
+        cut = slice(f * d.levels, (f + 1) * d.levels)
+        left, right = x_halos(d, xa, xb, cut)
+        for tile, added in ((0, from_left[cut, :] * left), (d.tiles - 1, from_right[cut, :] * right)):
+            place = pl.ds(base_row(d, f, 0) + FRONT + tile, d.levels, stride=d.block)
+            changed.append((place, pad[place, :] + added))
+    for place, cells in changed:
+        pad[place, :] = cells
+    changed = []
+    for f in range(FIELDS):
+        wz = (0.5 * STEP) * wind[2, end]
+        weight = STEP * diff[f] + jnp.where(low, -wz, wz)
+        place = pl.ds(pl.multiple_of(base_row(d, f, end) + FRONT, 8), d.tiles)
+        changed.append((place, pad[place, :] + weight * zface[f * d.tiles : (f + 1) * d.tiles, :]))
+    for place, cells in changed:
+        pad[place, :] = cells
     lane = lax.broadcasted_iota(jnp.int32, (d.tiles, LANES), 1)
-    zeros = jnp.zeros((d.tiles, LANES), F32)
     coef = wall_coef[...]
+    last = jnp.where(lane == d.columns - 1, 1.0, 0.0)
+    zeroth = jnp.where(lane == 0, 1.0, 0.0)
 
     def level(z, carry):
-        both = [stencil(d, pad, yq, wind, diff, f, z, lane) for f in range(FIELDS)]
-        drag = first_drag[pl.ds(pl.multiple_of(z * d.tiles, 8), d.tiles), :]
-        news = [both[f][1] - drag * both[f][0] if f < 3 else both[f][1] for f in range(FIELDS)]
+        wy = (0.5 * STEP) * wind[1, z]
+        news = []
+        for f in range(FIELDS):
+            spread = STEP * diff[f]
+            place = pl.ds(pl.multiple_of(base_row(d, f, z) + FRONT, 8), d.tiles)
+            weight = (spread - wy) * last + (spread + wy) * zeroth
+            news.append(pad[place, :] + weight * y_halo(d, yq, f, z))
         for f in range(FIELDS):
             new_pad[pl.ds(pl.multiple_of(base_row(d, f, z) + FRONT, 8), d.tiles), :] = news[f]
         factor[pl.ds(pl.multiple_of(z * d.tiles, 8), d.tiles), :] = coef * speed(*news[:3])
         return carry
 
     lax.fori_loop(0, d.levels, level, 0, unroll=8)
-    packed = [zeros] * d.groups
+    packed = [jnp.zeros((d.tiles, LANES), F32)] * d.groups
     for f in range(FIELDS):
         packed = add_edges(d, packed, new_pad, f, lane)
     write_y(d, yq_out, packed, lane)
@@ -469,7 +507,7 @@
         + [pad_t, x_t, x_t, z_t, *y_ts],
         in_specs=[pl.BlockSpec(memory_space=pltpu.HBM)] * (1 + n_small),
         out_specs=[VM] + [SM] * (n_small - 1) + [VM] * (4 + d.y_sends),
-        scratch_shapes=[pltpu.SemaphoreType.DMA((FIELDS + n_small,))],
+        scratch_shapes=[pltpu.VMEM(fields.shape, F32), pltpu.SemaphoreType.DMA((FIELDS + n_small,))],
         compiler_params=params,
         name="pack",
     )(in_hbm(fields), *small))[: n_small + 4]
@@ -480,9 +518,9 @@
     def ints(n):
         return pltpu.SMEM((n,), jnp.int32)
 
-    wall_coef, drag, from_left, from_right, masks, send_table, place_table, counts = pl.pallas_call(
+    new_pad, wall_coef, from_left, from_right, masks, send_table, place_table, counts = pl.pallas_call(
         functools.partial(prepare_kernel, d),
-        out_shape=[pltpu.VMEM((tiles, LANES), F32), pltpu.VMEM((levels * tiles, LANES), F32), x_t, x_t]
+        out_shape=[pad_t, pltpu.VMEM((tiles, LANES), F32), x_t, x_t]
         + [pltpu.VMEM(((d.parents + 1) * tiles, LANES), F32)]
         + [ints(d.n_gx * d.capacity), ints(SLOTS + 1), ints(d.parents)],
         in_specs=[VM] * 2 + [SM] * 5,
@@ -496,12 +534,12 @@
         functools.partial(step_one_kernel, d),
         out_shape=[pad_t, pad_t, pltpu.VMEM(((levels + 1) * tiles, LANES), F32), z_t, x_t, *y_ts]
         + [pltpu.VMEM((d.part + d.riders(k), LANES), F32) for k in range(d.n_gx)],
-        in_specs=[VM] * (6 + d.y_sends) + [SM] * 3,
+        in_specs=[VM] * (7 + d.y_sends) + [SM] * 3,
         out_specs=[VM] * (5 + d.y_sends + d.n_gx),
         input_output_aliases={0: 0},
         compiler_params=params,
         name="step_one",
-    )(in_vmem(pad), *faces, in_vmem(wall_coef), in_vmem(drag), small[1], small[2], send_table)
+    )(in_vmem(new_pad), *faces, *[in_vmem(a) for a in (wall_coef, from_left, from_right)], small[1], small[2], send_table)
     yq, stress = rest[: d.y_sends], rest[d.y_sends :]
     faces = zy_swapped(d, zface, yq)
     stress = [stress[0]] + [in_vmem(crossed(stress[k], "gx", k)) for k in range(1, d.n_gx)]

time: 26.5 us -> 25.8 us (0.974)
  waiting for transfers between devices: 5.25 us -> 4.33 us
    pallas_call x1, Pallas kernels: 0.85 us -> 1.78 us  [body(): pl.pallas_call(functools.partial(prepare_kernel, d), out_shape=[pad_t, pl...]
    ppermute x6, waiting for transfers between devices: 5.23 us -> 4.32 us  [swapped(): lax.ppermute(block, axis, [(i, i ^ 1) for i in range(lax.axis_size(axis))])]
    pallas_call x1, Pallas kernels: 1.94 us -> 1.26 us  [body(): pl.pallas_call(functools.partial(step_one_kernel, d), out_shape=[pad_t, p...]
  transfers between devices with their start and end apart: 11 -> 11, of which waited for: 3 -> 3; matrix products, arithmetic and copies ran while one was open for 0% -> 0% of each run, Pallas kernels for 13% -> 17%
where the time goes in v6:
time: 25.8 us; the launch traced here: 25.6 us
  starting transfers between devices  12.1 us (47%)
  Pallas kernels  8.47 us (33%)
  waiting for transfers between devices  4.33 us (17%)
  between operations  0.7 us (3%)
    ppermute x6, starting transfers between devices, swapped(): lax.ppermute(block, axis, [(i, i ^ 1) for i in range(lax.axis_size(axis))])  7.73 us
    ppermute x3, starting transfers between devices, crossed(): lax.ppermute(block, axis, [(i, i ^ distance) for i in range(lax.axis_size...  4.32 us
    ppermute x6, waiting for transfers between devices, swapped(): lax.ppermute(block, axis, [(i, i ^ 1) for i in range(lax.axis_size(axis))])  4.32 us
    pallas_call x1, Pallas kernels, body(): pl.pallas_call(functools.partial(pack_kernel, d), out_shape=[pltpu.SMEM(a...  1.85 us
    pallas_call x1, Pallas kernels, body(): pl.pallas_call(functools.partial(prepare_kernel, d), out_shape=[pad_t, pl...  1.78 us
    pallas_call x1, Pallas kernels, body(): pl.pallas_call(functools.partial(step_two_kernel, d), out_shape=[pad_t, s...  1.42 us
    pallas_call x1, Pallas kernels, body(): pl.pallas_call(functools.partial(step_one_kernel, d), out_shape=[pad_t, p...  1.26 us
    pallas_call x1, Pallas kernels, body(): pl.pallas_call(functools.partial(finish_kernel, d), out_shape=[jax.ShapeD...  1.1 us
  transfers between devices with their start and end apart: 11, of which 3 were waited for; matrix products, arithmetic and copies ran while one was open for 0% of the time, Pallas kernels for 17%

profile of v6, /device:TPU:0, one launch (start us, length us, event | category | flops | bytes accessed | tf_op | source)
XLA Modules:
  0.0 25.6 jit_solution(16534922941280854839)
XLA Ops:
  0.6 1.9 %pack.1 = (s32[16,128]{1,0:T(8,128)S(1)}, f32[3,32]{1,0:T(4,128)S(4)}, f32[5]{0:T(128)S(4)}, s32[16]{0:T(128)S(4)}, s32[64]{0:T(128)S(4)}, /*index=5*/s32[64]{0:...) custom-call(f32[5,32,16,128]{3,2,1,0:T(8,128)} %fields.1, ...), custom_call_target="tpu_custom_call" | custom-call | tf_op jit(solution)/shard_map/pack/pallas_call | solution.py:504
  2.5 3.1 %collective-permute-start = (f32[160,128]{1,0:T(8,128)S(1)}, f32[160,128]{1,0:T(8,128)S(1)}, u32[]{:S(2)}, u32[]{:S(2)}) collective-permute-start(f32[160,128]{1,0:T(8,128)S(1)} %get-tuple-element.48), channel_id=1, source_target_pairs={{0,4},{4,0},{8,12},{12,8},{1,5},{5,1},{9,13},{13,9},{2,6},{6,2},{1... | collective-permute-start | bytes 245768 | tf_op jit(solution)/shard_map/ppermute | solution.py:458
  5.6 0.0 collective-permute-start.1
  5.6 0.5 %collective-permute-start.2 = (f32[80,128]{1,0:T(8,128)S(1)}, f32[80,128]{1,0:T(8,128)S(1)}, u32[]{:S(2)}, u32[]{:S(2)}) collective-permute-start(f32[80,128]{1,0:T(8,128)S(1)} %get-tuple-element.50), channel_id=1, source_target_pairs={{0,1},{1,0},{2,3},{3,2},{4,5},{5,4},{6,7},{7,6},{8,9},{9,8},{10,11... | collective-permute-start | bytes 122888 | tf_op jit(solution)/shard_map/ppermute | solution.py:458
  6.1 1.5 %collective-permute-start.3 = (f32[16,384]{1,0:T(8,128)S(1)}, f32[16,384]{1,0:T(8,128)S(1)}, u32[]{:S(2)}, u32[]{:S(2)}) collective-permute-start(f32[16,384]{1,0:T(8,128)S(1)} %get-tuple-element.51), channel_id=1, source_target_pairs={{0,2},{2,0},{1,3},{3,1},{4,6},{6,4},{5,7},{7,5},{8,10},{10,8},{9,1... | collective-permute-start | bytes 73736 | tf_op jit(solution)/shard_map/ppermute | solution.py:458
  7.6 1.8 %prepare.1 = (f32[4088,128]{1,0:T(8,128)S(1)}, f32[16,128]{1,0:T(8,128)S(1)}, f32[160,128]{1,0:T(8,128)S(1)}, f32[160,128]{1,0:T(8,128)S(1)}, f32[48,128]{1,0:T(...) custom-call(f32[4088,128]{1,0:T(8,128)S(1)} %get-tuple-element.38.pad, ...), custom_call_target="tpu_custom_call" | custom-call | tf_op jit(solution)/shard_map/prepare/pallas_call | solution.py:521
  9.4 0.5 %collective-permute-done.3.refs_0_ = f32[16,384]{1,0:T(8,128)S(1)} collective-permute-done((f32[16,384]{1,0:T(8,128)S(1)}, f32[16,384]{1,0:T(8,128)S(1)}, u32[]{:S(2)}, u32[]{:S(2)}) %collective-permute-start.3) | collective-permute-done | bytes 24608 | tf_op jit(solution)/shard_map/ppermute | solution.py:458
  9.9 0.0 collective-permute-done.2.zface
  9.9 0.0 collective-permute-done.xa
  9.9 0.0 collective-permute-done.1.xb
  9.9 1.3 %step_one.1 = (f32[4088,128]{1,0:T(8,128)S(1)}, f32[4088,128]{1,0:T(8,128)S(1)}, f32[528,128]{1,0:T(8,128)S(1)}, f32[80,128]{1,0:T(8,128)S(1)}, f32[160,128]{1,0...) custom-call(f32[4088,128]{1,0:T(8,128)S(1)} %get-tuple-element.47.pa, ...), custom_call_target="tpu_custom_call", output_to_operand_aliasing={{0}: (0, {})} | custom-call | tf_op jit(solution)/shard_map/step_one/pallas_call | solution.py:533
  11.2 2.7 %collective-permute-start.8 = (f32[288,128]{1,0:T(8,128)S(1)}, f32[288,128]{1,0:T(8,128)S(1)}, u32[]{:S(2)}, u32[]{:S(2)}) collective-permute-start(f32[288,128]{1,0:T(8,128)S(1)} %get-tuple-element.67), channel_id=1, source_target_pairs={{0,4},{4,0},{8,12},{12,8},{1,5},{5,1},{9,13},{13,9},{2,6},{6,2},{1... | collective-permute-start | bytes 442376 | tf_op jit(solution)/shard_map/ppermute | solution.py:472
  13.9 0.0 collective-permute-start.4
  13.9 1.5 %collective-permute-start.10 = (f32[192,128]{1,0:T(8,128)S(1)}, f32[192,128]{1,0:T(8,128)S(1)}, u32[]{:S(2)}, u32[]{:S(2)}) collective-permute-start(f32[192,128]{1,0:T(8,128)S(1)} %get-tuple-element.69), channel_id=1, source_target_pairs={{0,12},{4,8},{8,4},{12,0},{1,13},{5,9},{9,5},{13,1},{2,14},{6,10},... | collective-permute-start | bytes 294920 | tf_op jit(solution)/shard_map/ppermute | solution.py:472
  15.4 1.5 %collective-permute-start.5 = (f32[16,384]{1,0:T(8,128)S(1)}, f32[16,384]{1,0:T(8,128)S(1)}, u32[]{:S(2)}, u32[]{:S(2)}) collective-permute-start(f32[16,384]{1,0:T(8,128)S(1)} %get-tuple-element.57), channel_id=1, source_target_pairs={{0,2},{2,0},{1,3},{3,1},{4,6},{6,4},{5,7},{7,5},{8,10},{10,8},{9,1... | collective-permute-start | bytes 73736 | tf_op jit(solution)/shard_map/ppermute | solution.py:458
  16.9 0.1 collective-permute-start.9
  17.0 2.2 %collective-permute-done.5.refs_0_ = f32[16,384]{1,0:T(8,128)S(1)} collective-permute-done((f32[16,384]{1,0:T(8,128)S(1)}, f32[16,384]{1,0:T(8,128)S(1)}, u32[]{:S(2)}, u32[]{:S(2)}) %collective-permute-start.5) | collective-permute-done | bytes 24608 | tf_op jit(solution)/shard_map/ppermute | solution.py:458
  19.2 0.0 collective-permute-done.4.zface
  19.2 1.4 %step_two.1 = (f32[4088,128]{1,0:T(8,128)S(1)}, f32[2576,128]{1,0:T(8,128)S(1)}, f32[48,128]{1,0:T(8,128)S(1)}, f32[24,128]{1,0:T(8,128)S(1)}, f32[120,128]{1,0:T(8,128)S(1)}) custom-call(f32[4088,128]{1,0:T(8,128)S(1)} %get-tuple-element.54.pad_in, f32[528,128]{1,0:T(8,128)S(1)} %get-tuple-element.55.factor, ...), custom_call_target="tpu_custom_call", output_to_operand_aliasing={{0}: (0, {})} | custom-call | tf_op jit(solution)/shard_map/step_two/pallas_call | solution.py:549
  20.7 0.1 collective-permute-start.7
  20.7 1.1 %collective-permute-start.6 = (f32[24,128]{1,0:T(8,128)S(1)}, f32[24,128]{1,0:T(8,128)S(1)}, u32[]{:S(2)}, u32[]{:S(2)}) collective-permute-start(f32[24,128]{1,0:T(8,128)S(1)} %get-tuple-element.62), channel_id=1, source_target_pairs={{0,4},{4,0},{8,12},{12,8},{1,5},{5,1},{9,13},{13,9},{2,6},{6,2},{1... | collective-permute-start | bytes 36872 | tf_op jit(solution)/shard_map/ppermute | solution.py:458
  21.9 1.1 %flush.1.flushed = f32[2560,128]{1,0:T(8,128)} custom-call(f32[2576,128]{1,0:T(8,128)S(1)} %get-tuple-element.59.state.state_in), custom_call_target="tpu_custom_call" | custom-call | tf_op jit(solution)/shard_map/flush/pallas_call | solution.py:567
  23.0 1.5 %collective-permute-done.6.refs_0_ = f32[24,128]{1,0:T(8,128)S(1)} collective-permute-done((f32[24,128]{1,0:T(8,128)S(1)}, f32[24,128]{1,0:T(8,128)S(1)}, u32[]{:S(2)}, u32[]{:S(2)}) %collective-permute-start.6) | collective-permute-done | bytes 12320 | tf_op jit(solution)/shard_map/ppermute | solution.py:458
  24.5 0.0 collective-permute-done.9.refs_7_
  24.5 0.0 collective-permute-done.10.refs_8_
  24.5 0.0 collective-permute-done.7.refs_1_
  24.5 0.0 collective-permute-done.8.refs_6_
  24.5 1.1 %finish.1 = (f32[2560,128]{1,0:T(8,128)}, f32[2576,128]{1,0:T(8,128)S(1)}, f32[256,128]{1,0:T(8,128)}, f32[2,5,4,16]{3,2,1,0:T(4,128)}) custom-call(f32[160,128]{1,0:T(8,128)S(1)} %get-tuple-element.45.refs_2_.from_left, f32[160,128]{1,0:T(8,128)S(1)} %get-tuple-element.46.refs_3_.from_right, ...), custom_call_target="tpu_custom_call", output_to_operand_aliasing={{0}: (2, {}), {1}: (3, {})} | custom-call | tf_op jit(solution)/shard_map/finish/pallas_call | solution.py:577
Async XLA Ops:
  2.5 7.4 %collective-permute-start = (f32[160,128]{1,0:T(8,128)S(1)}, f32[160,128]{1,0:T(8,128)S(1)}, u32[]{:S(2)}, u32[]{:S(2)}) collective-permute-start(f32[160,128]{1,0:T(8,128)S(1)} %get-tuple-element.48), channel_id=1, source_target_pairs={{0,4},{4,0},{8,12},{12,8},{1,5},{5,1},{9,13},{13,9},{2,6},{6,2},{1... | collective-permute-start | bytes 245768 | tf_op jit(solution)/shard_map/ppermute | solution.py:458
  5.6 4.3 %collective-permute-start.1 = (f32[160,128]{1,0:T(8,128)S(1)}, f32[160,128]{1,0:T(8,128)S(1)}, u32[]{:S(2)}, u32[]{:S(2)}) collective-permute-start(f32[160,128]{1,0:T(8,128)S(1)} %get-tuple-element.49), channel_id=1, source_target_pairs={{0,1},{1,0},{4,8},{5,9},{8,4},{9,5},{12,13},{13,12},{2,3},{3,2},{6... | collective-permute-start | bytes 245768 | tf_op jit(solution)/shard_map/ppermute | solution.py:468
  5.6 4.3 %collective-permute-start.2 = (f32[80,128]{1,0:T(8,128)S(1)}, f32[80,128]{1,0:T(8,128)S(1)}, u32[]{:S(2)}, u32[]{:S(2)}) collective-permute-start(f32[80,128]{1,0:T(8,128)S(1)} %get-tuple-element.50), channel_id=1, source_target_pairs={{0,1},{1,0},{2,3},{3,2},{4,5},{5,4},{6,7},{7,6},{8,9},{9,8},{10,11... | collective-permute-start | bytes 122888 | tf_op jit(solution)/shard_map/ppermute | solution.py:458
  6.1 3.8 %collective-permute-start.3 = (f32[16,384]{1,0:T(8,128)S(1)}, f32[16,384]{1,0:T(8,128)S(1)}, u32[]{:S(2)}, u32[]{:S(2)}) collective-permute-start(f32[16,384]{1,0:T(8,128)S(1)} %get-tuple-element.51), channel_id=1, source_target_pairs={{0,2},{2,0},{1,3},{3,1},{4,6},{6,4},{5,7},{7,5},{8,10},{10,8},{9,1... | collective-permute-start | bytes 73736 | tf_op jit(solution)/shard_map/ppermute | solution.py:458
  11.2 13.3 %collective-permute-start.8 = (f32[288,128]{1,0:T(8,128)S(1)}, f32[288,128]{1,0:T(8,128)S(1)}, u32[]{:S(2)}, u32[]{:S(2)}) collective-permute-start(f32[288,128]{1,0:T(8,128)S(1)} %get-tuple-element.67), channel_id=1, source_target_pairs={{0,4},{4,0},{8,12},{12,8},{1,5},{5,1},{9,13},{13,9},{2,6},{6,2},{1... | collective-permute-start | bytes 442376 | tf_op jit(solution)/shard_map/ppermute | solution.py:472
  13.9 5.3 %collective-permute-start.4 = (f32[80,128]{1,0:T(8,128)S(1)}, f32[80,128]{1,0:T(8,128)S(1)}, u32[]{:S(2)}, u32[]{:S(2)}) collective-permute-start(f32[80,128]{1,0:T(8,128)S(1)} %get-tuple-element.56), channel_id=1, source_target_pairs={{0,1},{1,0},{2,3},{3,2},{4,5},{5,4},{6,7},{7,6},{8,9},{9,8},{10,11... | collective-permute-start | bytes 122888 | tf_op jit(solution)/shard_map/ppermute | solution.py:458
  13.9 10.6 %collective-permute-start.10 = (f32[192,128]{1,0:T(8,128)S(1)}, f32[192,128]{1,0:T(8,128)S(1)}, u32[]{:S(2)}, u32[]{:S(2)}) collective-permute-start(f32[192,128]{1,0:T(8,128)S(1)} %get-tuple-element.69), channel_id=1, source_target_pairs={{0,12},{4,8},{8,4},{12,0},{1,13},{5,9},{9,5},{13,1},{2,14},{6,10},... | collective-permute-start | bytes 294920 | tf_op jit(solution)/shard_map/ppermute | solution.py:472
  15.4 3.8 %collective-permute-start.5 = (f32[16,384]{1,0:T(8,128)S(1)}, f32[16,384]{1,0:T(8,128)S(1)}, u32[]{:S(2)}, u32[]{:S(2)}) collective-permute-start(f32[16,384]{1,0:T(8,128)S(1)} %get-tuple-element.57), channel_id=1, source_target_pairs={{0,2},{2,0},{1,3},{3,1},{4,6},{6,4},{5,7},{7,5},{8,10},{10,8},{9,1... | collective-permute-start | bytes 73736 | tf_op jit(solution)/shard_map/ppermute | solution.py:458
  16.9 7.6 %collective-permute-start.9 = (f32[128,128]{1,0:T(8,128)S(1)}, f32[128,128]{1,0:T(8,128)S(1)}, u32[]{:S(2)}, u32[]{:S(2)}) collective-permute-start(f32[128,128]{1,0:T(8,128)S(1)} %get-tuple-element.68), channel_id=1, source_target_pairs={{0,8},{4,12},{8,0},{12,4},{1,9},{5,13},{9,1},{13,5},{2,10},{6,14},... | collective-permute-start | bytes 196616 | tf_op jit(solution)/shard_map/ppermute | solution.py:472
  20.7 3.8 %collective-permute-start.7 = (f32[120,128]{1,0:T(8,128)S(1)}, f32[120,128]{1,0:T(8,128)S(1)}, u32[]{:S(2)}, u32[]{:S(2)}) collective-permute-start(f32[120,128]{1,0:T(8,128)S(1)} %get-tuple-element.63), channel_id=1, source_target_pairs={{0,1},{1,0},{4,8},{5,9},{8,4},{9,5},{12,13},{13,12},{2,3},{3,2},{6... | collective-permute-start | bytes 184328 | tf_op jit(solution)/shard_map/ppermute | solution.py:468
  20.7 3.8 %collective-permute-start.6 = (f32[24,128]{1,0:T(8,128)S(1)}, f32[24,128]{1,0:T(8,128)S(1)}, u32[]{:S(2)}, u32[]{:S(2)}) collective-permute-start(f32[24,128]{1,0:T(8,128)S(1)} %get-tuple-element.62), channel_id=1, source_target_pairs={{0,4},{4,0},{8,12},{12,8},{1,5},{5,1},{9,13},{13,9},{2,6},{6,2},{1... | collective-permute-start | bytes 36872 | tf_op jit(solution)/shard_map/ppermute | solution.py:458

commit v7 on v6

--- a/solution.py
+++ b/solution.py
@@ -329,32 +329,62 @@
             stress[k][c * d.levels : (c + 1) * d.levels, :] = factor[pl.ds(tile, d.levels, stride=d.tiles), :]
 
 
-def step_two_kernel(d, pad_in, factor, zface, *refs):
+def local_two_kernel(d, pad_in, factor, wind, diff, pad, raw):
+    zero_x = jnp.zeros((d.levels, LANES), F32)
+    for f in range(FIELDS):
+        set_x_halos(d, pad, f, zero_x, zero_x)
+        for z in (-1, d.levels):
+            pad[pl.ds(base_row(d, f, z) + FRONT, d.tiles), :] = jnp.zeros((d.tiles, LANES), F32)
+    lane = lax.broadcasted_iota(jnp.int32, (d.tiles, LANES), 1)
+    rows = d.levels * d.tiles
+
+    def level(z, carry):
+        drag = STEP * factor[pl.ds(pl.multiple_of(z * d.tiles, 8), d.tiles), :]
+        for f in range(FIELDS):
+            v, new = stencil(d, pad, None, wind, diff, f, z, lane)
+            if f < 3:
+                new = new - drag * v
+            raw[pl.ds(pl.multiple_of(f * rows + z * d.tiles, 8), d.tiles), :] = new
+        return carry
+
+    lax.fori_loop(0, d.levels, level, 0, unroll=8)
+
+
+def step_two_kernel(d, raw_in, pad, zface, *refs):
     yq = refs[: d.y_sends]
     masks_in, wind, diff = refs[d.y_sends : d.y_sends + 3]
-    pad, new_fields, own_sums, sent_sums, sent_b, coarse = refs[-6:]
-    zero_x = jnp.zeros((d.levels, LANES), F32)
-    for f in range(FIELDS):
-        set_x_halos(d, pad, f, zero_x, zero_x)
-    set_z_halos(d, pad, zface)
+    raw, new_fields, own_sums, sent_sums, sent_b, coarse = refs[-6:]
+    rows = d.levels * d.tiles
+    low = lax.axis_index("gz") == 0
+    end = jnp.where(low, d.levels - 1, 0)
+    changed = []
+    for f in range(FIELDS):
+        wz = (0.5 * STEP) * wind[2, end]
+        weight = STEP * diff[f] + jnp.where(low, -wz, wz)
+        place = pl.ds(pl.multiple_of(f * rows + end * d.tiles, 8), d.tiles)
+        changed.append((place, raw[place, :] + weight * zface[f * d.tiles : (f + 1) * d.tiles, :]))
+    for place, cells in changed:
+        raw[place, :] = cells
     lane = lax.broadcasted_iota(jnp.int32, (d.tiles, LANES), 1)
+    last = jnp.where(lane == d.columns - 1, 1.0, 0.0)
+    zeroth = jnp.where(lane == 0, 1.0, 0.0)
     zeros = jnp.zeros((d.tiles, LANES), F32)
     masks = [masks_in[p * d.tiles : (p + 1) * d.tiles, :] for p in range(d.parents + 1)]
     coarse_levels = d.levels // RATIO
     coarse[...] = jnp.zeros_like(coarse)
-    rows = d.levels * d.tiles
     per_parent = coarse.shape[0] // (d.parents + 1)
 
     def coarse_level(k, carry):
         def level(i, sums):
             z = k * RATIO + i
-            drag = STEP * factor[pl.ds(pl.multiple_of(z * d.tiles, 8), d.tiles), :]
+            wy = (0.5 * STEP) * wind[1, z]
             added = []
             for f in range(FIELDS):
-                v, new = stencil(d, pad, yq, wind, diff, f, z, lane)
-                if f < 3:
-                    new = new - drag * v
-                new_fields[pl.ds(pl.multiple_of(f * rows + z * d.tiles, 8), d.tiles), :] = new
+                spread = STEP * diff[f]
+                place = pl.ds(pl.multiple_of(f * rows + z * d.tiles, 8), d.tiles)
+                weight = (spread - wy) * last + (spread + wy) * zeroth
+                new = raw[place, :] + weight * y_halo(d, yq, f, z)
+                new_fields[place, :] = new
                 added.append(sums[f] + new)
             return tuple(added)
 
@@ -546,10 +576,19 @@
 
     per_parent = -(-FIELDS * (levels // RATIO) // 8) * 8
     state_t = pltpu.VMEM((rows + tiles, LANES), F32)
+    new_pad, raw = pl.pallas_call(
+        functools.partial(local_two_kernel, d),
+        out_shape=[pad_t, state_t],
+        in_specs=[VM] * 2 + [SM] * 2,
+        out_specs=[VM] * 2,
+        input_output_aliases={0: 0},
+        compiler_params=params,
+        name="local_two",
+    )(in_vmem(new_pad), in_vmem(factor), small[1], small[2])
     _, state, own_sums, sent_sums, sent_b = pl.pallas_call(
         functools.partial(step_two_kernel, d),
         out_shape=[
-            pad_t,
+            state_t,
             state_t,
             pltpu.VMEM((d.parents * per_parent, LANES), F32),
             pltpu.VMEM((per_parent, LANES), F32),
@@ -561,7 +600,7 @@
         input_output_aliases={0: 0},
         compiler_params=params,
         name="step_two",
-    )(in_vmem(new_pad), in_vmem(factor), *faces, in_vmem(masks), small[1], small[2])
+    )(in_vmem(raw), in_vmem(new_pad), *faces, in_vmem(masks), small[1], small[2])
     got = x_swapped(sent_sums, sent_b)
 
     flushed = pl.pallas_call(

time: 25.8 us -> 25.4 us (0.984)
  waiting for transfers between devices: 4.33 us -> 2.1 us
  starting transfers between devices: 12.1 us -> 13.4 us
  Pallas kernels: 8.47 us -> 9.04 us
    ppermute x6, waiting for transfers between devices: 4.32 us -> 2.09 us  [swapped(): lax.ppermute(block, axis, [(i, i ^ 1) for i in range(lax.axis_size(axis))])]
    ppermute x6, starting transfers between devices: 7.73 us -> 9.02 us  [swapped(): lax.ppermute(block, axis, [(i, i ^ 1) for i in range(lax.axis_size(axis))])]
    pallas_call x1 -> x2, Pallas kernels: 1.42 us -> 1.99 us  [the longest x1 1.27 us: body(): pl.pallas_call(functools.partial(local_two_kernel, d), out_shape=[pad_t,...]
  transfers between devices with their start and end apart: 11 -> 11, of which waited for: 3 -> 3; matrix products, arithmetic and copies ran while one was open for 0% -> 0% of each run, Pallas kernels for 17% -> 19%
where the time goes in v7:
time: 25.4 us; the launch traced here: 25.3 us
  starting transfers between devices  13.4 us (53%)
  Pallas kernels  9.04 us (36%)
  waiting for transfers between devices  2.1 us (8%)
  between operations  0.71 us (3%)
    ppermute x6, starting transfers between devices, swapped(): lax.ppermute(block, axis, [(i, i ^ 1) for i in range(lax.axis_size(axis))])  9.02 us
    ppermute x3, starting transfers between devices, crossed(): lax.ppermute(block, axis, [(i, i ^ distance) for i in range(lax.axis_size...  4.33 us
    ppermute x6, waiting for transfers between devices, swapped(): lax.ppermute(block, axis, [(i, i ^ 1) for i in range(lax.axis_size(axis))])  2.09 us
    pallas_call x1, Pallas kernels, body(): pl.pallas_call(functools.partial(pack_kernel, d), out_shape=[pltpu.SMEM(a...  1.85 us
    pallas_call x1, Pallas kernels, body(): pl.pallas_call(functools.partial(prepare_kernel, d), out_shape=[pad_t, pl...  1.78 us
    pallas_call x1, Pallas kernels, body(): pl.pallas_call(functools.partial(step_one_kernel, d), out_shape=[pad_t, p...  1.27 us
    pallas_call x1, Pallas kernels, body(): pl.pallas_call(functools.partial(local_two_kernel, d), out_shape=[pad_t,...  1.27 us
    pallas_call x1, Pallas kernels, body(): pl.pallas_call(functools.partial(finish_kernel, d), out_shape=[jax.ShapeD...  1.09 us
  transfers between devices with their start and end apart: 11, of which 3 were waited for; matrix products, arithmetic and copies ran while one was open for 0% of the time, Pallas kernels for 19%

profile of v7, /device:TPU:0, one launch (start us, length us, event | category | flops | bytes accessed | tf_op | source)
XLA Modules:
  0.0 25.3 jit_solution(15820931365073951018)
XLA Ops:
  0.6 1.9 %pack.1 = (s32[16,128]{1,0:T(8,128)S(1)}, f32[3,32]{1,0:T(4,128)S(4)}, f32[5]{0:T(128)S(4)}, s32[16]{0:T(128)S(4)}, s32[64]{0:T(128)S(4)}, /*index=5*/s32[64]{0:...) custom-call(f32[5,32,16,128]{3,2,1,0:T(8,128)} %fields.1, ...), custom_call_target="tpu_custom_call" | custom-call | tf_op jit(solution)/shard_map/pack/pallas_call | solution.py:534
  2.5 3.1 %collective-permute-start = (f32[160,128]{1,0:T(8,128)S(1)}, f32[160,128]{1,0:T(8,128)S(1)}, u32[]{:S(2)}, u32[]{:S(2)}) collective-permute-start(f32[160,128]{1,0:T(8,128)S(1)} %get-tuple-element.50), channel_id=1, source_target_pairs={{0,4},{4,0},{8,12},{12,8},{1,5},{5,1},{9,13},{13,9},{2,6},{6,2},{1... | collective-permute-start | bytes 245768 | tf_op jit(solution)/shard_map/ppermute | solution.py:488
  5.6 0.0 collective-permute-start.1
  5.6 0.5 %collective-permute-start.2 = (f32[80,128]{1,0:T(8,128)S(1)}, f32[80,128]{1,0:T(8,128)S(1)}, u32[]{:S(2)}, u32[]{:S(2)}) collective-permute-start(f32[80,128]{1,0:T(8,128)S(1)} %get-tuple-element.52), channel_id=1, source_target_pairs={{0,1},{1,0},{2,3},{3,2},{4,5},{5,4},{6,7},{7,6},{8,9},{9,8},{10,11... | collective-permute-start | bytes 122888 | tf_op jit(solution)/shard_map/ppermute | solution.py:488
  6.1 1.5 %collective-permute-start.3 = (f32[16,384]{1,0:T(8,128)S(1)}, f32[16,384]{1,0:T(8,128)S(1)}, u32[]{:S(2)}, u32[]{:S(2)}) collective-permute-start(f32[16,384]{1,0:T(8,128)S(1)} %get-tuple-element.53), channel_id=1, source_target_pairs={{0,2},{2,0},{1,3},{3,1},{4,6},{6,4},{5,7},{7,5},{8,10},{10,8},{9,1... | collective-permute-start | bytes 73736 | tf_op jit(solution)/shard_map/ppermute | solution.py:488
  7.6 1.8 %prepare.1 = (f32[4088,128]{1,0:T(8,128)S(1)}, f32[16,128]{1,0:T(8,128)S(1)}, f32[160,128]{1,0:T(8,128)S(1)}, f32[160,128]{1,0:T(8,128)S(1)}, f32[48,128]{1,0:T(...) custom-call(f32[4088,128]{1,0:T(8,128)S(1)} %get-tuple-element.40.pad, ...), custom_call_target="tpu_custom_call" | custom-call | tf_op jit(solution)/shard_map/prepare/pallas_call | solution.py:551
  9.4 0.5 %collective-permute-done.3.refs_0_ = f32[16,384]{1,0:T(8,128)S(1)} collective-permute-done((f32[16,384]{1,0:T(8,128)S(1)}, f32[16,384]{1,0:T(8,128)S(1)}, u32[]{:S(2)}, u32[]{:S(2)}) %collective-permute-start.3) | collective-permute-done | bytes 24608 | tf_op jit(solution)/shard_map/ppermute | solution.py:488
  9.9 0.0 collective-permute-done.2.zface
  9.9 0.0 collective-permute-done.xa
  9.9 0.0 collective-permute-done.1.xb
  9.9 1.3 %step_one.1 = (f32[4088,128]{1,0:T(8,128)S(1)}, f32[4088,128]{1,0:T(8,128)S(1)}, f32[528,128]{1,0:T(8,128)S(1)}, f32[80,128]{1,0:T(8,128)S(1)}, f32[160,128]{1,0...) custom-call(f32[4088,128]{1,0:T(8,128)S(1)} %get-tuple-element.49.pa, ...), custom_call_target="tpu_custom_call", output_to_operand_aliasing={{0}: (0, {})} | custom-call | tf_op jit(solution)/shard_map/step_one/pallas_call | solution.py:563
  11.2 2.7 %collective-permute-start.8 = (f32[288,128]{1,0:T(8,128)S(1)}, f32[288,128]{1,0:T(8,128)S(1)}, u32[]{:S(2)}, u32[]{:S(2)}) collective-permute-start(f32[288,128]{1,0:T(8,128)S(1)} %get-tuple-element.71), channel_id=1, source_target_pairs={{0,4},{4,0},{8,12},{12,8},{1,5},{5,1},{9,13},{13,9},{2,6},{6,2},{1... | collective-permute-start | bytes 442376 | tf_op jit(solution)/shard_map/ppermute | solution.py:502
  13.9 0.0 collective-permute-start.4
  13.9 1.5 %collective-permute-start.10 = (f32[192,128]{1,0:T(8,128)S(1)}, f32[192,128]{1,0:T(8,128)S(1)}, u32[]{:S(2)}, u32[]{:S(2)}) collective-permute-start(f32[192,128]{1,0:T(8,128)S(1)} %get-tuple-element.73), channel_id=1, source_target_pairs={{0,12},{4,8},{8,4},{12,0},{1,13},{5,9},{9,5},{13,1},{2,14},{6,10},... | collective-permute-start | bytes 294920 | tf_op jit(solution)/shard_map/ppermute | solution.py:502
  15.4 1.5 %collective-permute-start.5 = (f32[16,384]{1,0:T(8,128)S(1)}, f32[16,384]{1,0:T(8,128)S(1)}, u32[]{:S(2)}, u32[]{:S(2)}) collective-permute-start(f32[16,384]{1,0:T(8,128)S(1)} %get-tuple-element.61), channel_id=1, source_target_pairs={{0,2},{2,0},{1,3},{3,1},{4,6},{6,4},{5,7},{7,5},{8,10},{10,8},{9,1... | collective-permute-start | bytes 73736 | tf_op jit(solution)/shard_map/ppermute | solution.py:488
  16.9 0.1 collective-permute-start.9
  17.0 1.3 %local_two.1 = (f32[4088,128]{1,0:T(8,128)S(1)}, f32[2576,128]{1,0:T(8,128)S(1)}) custom-call(f32[4088,128]{1,0:T(8,128)S(1)} %get-tuple-element.56.pad_in, f32[528,128]{1,0:T(8,128)S(1)} %get-tuple-element.57.factor, f32[3,32]{1,0:T(4,128)S(4)} %get-tuple-element.42.wind.refs_4_.refs_2_, ...), custom_call_target="tpu_custom_call", output_to_operand_aliasing={{0}: (0, {})} | custom-call | tf_op jit(solution)/shard_map/local_two/pallas_call | solution.py:579
  18.3 0.9 %collective-permute-done.5.refs_0_ = f32[16,384]{1,0:T(8,128)S(1)} collective-permute-done((f32[16,384]{1,0:T(8,128)S(1)}, f32[16,384]{1,0:T(8,128)S(1)}, u32[]{:S(2)}, u32[]{:S(2)}) %collective-permute-start.5) | collective-permute-done | bytes 24608 | tf_op jit(solution)/shard_map/ppermute | solution.py:488
  19.2 0.0 collective-permute-done.4.zface
  19.2 0.7 %step_two.1 = (f32[2576,128]{1,0:T(8,128)S(1)}, f32[2576,128]{1,0:T(8,128)S(1)}, f32[48,128]{1,0:T(8,128)S(1)}, f32[24,128]{1,0:T(8,128)S(1)}, f32[120,128]{1,0:T(8,128)S(1)}) custom-call(f32[2576,128]{1,0:T(8,128)S(1)} %get-tuple-element.58.raw_in, f32[4088,128]{1,0:T(8,128)S(1)} %get-tuple-element.59.pad, ...), custom_call_target="tpu_custom_call", output_to_operand_aliasing={{0}: (0, {})} | custom-call | tf_op jit(solution)/shard_map/step_two/pallas_call | solution.py:588
  20.0 0.1 collective-permute-start.7
  20.0 2.4 %collective-permute-start.6 = (f32[24,128]{1,0:T(8,128)S(1)}, f32[24,128]{1,0:T(8,128)S(1)}, u32[]{:S(2)}, u32[]{:S(2)}) collective-permute-start(f32[24,128]{1,0:T(8,128)S(1)} %get-tuple-element.66), channel_id=1, source_target_pairs={{0,4},{4,0},{8,12},{12,8},{1,5},{5,1},{9,13},{13,9},{2,6},{6,2},{1... | collective-permute-start | bytes 36872 | tf_op jit(solution)/shard_map/ppermute | solution.py:488
  22.5 1.1 %flush.1.flushed = f32[2560,128]{1,0:T(8,128)} custom-call(f32[2576,128]{1,0:T(8,128)S(1)} %get-tuple-element.63.state.state_in), custom_call_target="tpu_custom_call" | custom-call | tf_op jit(solution)/shard_map/flush/pallas_call | solution.py:606
  23.6 0.6 %collective-permute-done.6.refs_0_ = f32[24,128]{1,0:T(8,128)S(1)} collective-permute-done((f32[24,128]{1,0:T(8,128)S(1)}, f32[24,128]{1,0:T(8,128)S(1)}, u32[]{:S(2)}, u32[]{:S(2)}) %collective-permute-start.6) | collective-permute-done | bytes 12320 | tf_op jit(solution)/shard_map/ppermute | solution.py:488
  24.2 0.0 collective-permute-done.9.refs_7_
  24.2 0.0 collective-permute-done.10.refs_8_
  24.2 0.0 collective-permute-done.7.refs_1_
  24.2 0.0 collective-permute-done.8.refs_6_
  24.2 1.1 %finish.1 = (f32[2560,128]{1,0:T(8,128)}, f32[2576,128]{1,0:T(8,128)S(1)}, f32[256,128]{1,0:T(8,128)}, f32[2,5,4,16]{3,2,1,0:T(4,128)}) custom-call(f32[160,128]{1,0:T(8,128)S(1)} %get-tuple-element.47.refs_2_.from_left, f32[160,128]{1,0:T(8,128)S(1)} %get-tuple-element.48.refs_3_.from_right, ...), custom_call_target="tpu_custom_call", output_to_operand_aliasing={{0}: (2, {}), {1}: (3, {})} | custom-call | tf_op jit(solution)/shard_map/finish/pallas_call | solution.py:616
Async XLA Ops:
  2.5 7.4 %collective-permute-start = (f32[160,128]{1,0:T(8,128)S(1)}, f32[160,128]{1,0:T(8,128)S(1)}, u32[]{:S(2)}, u32[]{:S(2)}) collective-permute-start(f32[160,128]{1,0:T(8,128)S(1)} %get-tuple-element.50), channel_id=1, source_target_pairs={{0,4},{4,0},{8,12},{12,8},{1,5},{5,1},{9,13},{13,9},{2,6},{6,2},{1... | collective-permute-start | bytes 245768 | tf_op jit(solution)/shard_map/ppermute | solution.py:488
  5.6 4.3 %collective-permute-start.1 = (f32[160,128]{1,0:T(8,128)S(1)}, f32[160,128]{1,0:T(8,128)S(1)}, u32[]{:S(2)}, u32[]{:S(2)}) collective-permute-start(f32[160,128]{1,0:T(8,128)S(1)} %get-tuple-element.51), channel_id=1, source_target_pairs={{0,1},{1,0},{4,8},{5,9},{8,4},{9,5},{12,13},{13,12},{2,3},{3,2},{6... | collective-permute-start | bytes 245768 | tf_op jit(solution)/shard_map/ppermute | solution.py:498
  5.6 4.3 %collective-permute-start.2 = (f32[80,128]{1,0:T(8,128)S(1)}, f32[80,128]{1,0:T(8,128)S(1)}, u32[]{:S(2)}, u32[]{:S(2)}) collective-permute-start(f32[80,128]{1,0:T(8,128)S(1)} %get-tuple-element.52), channel_id=1, source_target_pairs={{0,1},{1,0},{2,3},{3,2},{4,5},{5,4},{6,7},{7,6},{8,9},{9,8},{10,11... | collective-permute-start | bytes 122888 | tf_op jit(solution)/shard_map/ppermute | solution.py:488
  6.1 3.8 %collective-permute-start.3 = (f32[16,384]{1,0:T(8,128)S(1)}, f32[16,384]{1,0:T(8,128)S(1)}, u32[]{:S(2)}, u32[]{:S(2)}) collective-permute-start(f32[16,384]{1,0:T(8,128)S(1)} %get-tuple-element.53), channel_id=1, source_target_pairs={{0,2},{2,0},{1,3},{3,1},{4,6},{6,4},{5,7},{7,5},{8,10},{10,8},{9,1... | collective-permute-start | bytes 73736 | tf_op jit(solution)/shard_map/ppermute | solution.py:488
  11.2 13.0 %collective-permute-start.8 = (f32[288,128]{1,0:T(8,128)S(1)}, f32[288,128]{1,0:T(8,128)S(1)}, u32[]{:S(2)}, u32[]{:S(2)}) collective-permute-start(f32[288,128]{1,0:T(8,128)S(1)} %get-tuple-element.71), channel_id=1, source_target_pairs={{0,4},{4,0},{8,12},{12,8},{1,5},{5,1},{9,13},{13,9},{2,6},{6,2},{1... | collective-permute-start | bytes 442376 | tf_op jit(solution)/shard_map/ppermute | solution.py:502
  13.9 5.3 %collective-permute-start.4 = (f32[80,128]{1,0:T(8,128)S(1)}, f32[80,128]{1,0:T(8,128)S(1)}, u32[]{:S(2)}, u32[]{:S(2)}) collective-permute-start(f32[80,128]{1,0:T(8,128)S(1)} %get-tuple-element.60), channel_id=1, source_target_pairs={{0,1},{1,0},{2,3},{3,2},{4,5},{5,4},{6,7},{7,6},{8,9},{9,8},{10,11... | collective-permute-start | bytes 122888 | tf_op jit(solution)/shard_map/ppermute | solution.py:488
  13.9 10.2 %collective-permute-start.10 = (f32[192,128]{1,0:T(8,128)S(1)}, f32[192,128]{1,0:T(8,128)S(1)}, u32[]{:S(2)}, u32[]{:S(2)}) collective-permute-start(f32[192,128]{1,0:T(8,128)S(1)} %get-tuple-element.73), channel_id=1, source_target_pairs={{0,12},{4,8},{8,4},{12,0},{1,13},{5,9},{9,5},{13,1},{2,14},{6,10},... | collective-permute-start | bytes 294920 | tf_op jit(solution)/shard_map/ppermute | solution.py:502
  15.4 3.8 %collective-permute-start.5 = (f32[16,384]{1,0:T(8,128)S(1)}, f32[16,384]{1,0:T(8,128)S(1)}, u32[]{:S(2)}, u32[]{:S(2)}) collective-permute-start(f32[16,384]{1,0:T(8,128)S(1)} %get-tuple-element.61), channel_id=1, source_target_pairs={{0,2},{2,0},{1,3},{3,1},{4,6},{6,4},{5,7},{7,5},{8,10},{10,8},{9,1... | collective-permute-start | bytes 73736 | tf_op jit(solution)/shard_map/ppermute | solution.py:488
  16.9 7.3 %collective-permute-start.9 = (f32[128,128]{1,0:T(8,128)S(1)}, f32[128,128]{1,0:T(8,128)S(1)}, u32[]{:S(2)}, u32[]{:S(2)}) collective-permute-start(f32[128,128]{1,0:T(8,128)S(1)} %get-tuple-element.72), channel_id=1, source_target_pairs={{0,8},{4,12},{8,0},{12,4},{1,9},{5,13},{9,1},{13,5},{2,10},{6,14},... | collective-permute-start | bytes 196616 | tf_op jit(solution)/shard_map/ppermute | solution.py:502
  20.0 4.2 %collective-permute-start.7 = (f32[120,128]{1,0:T(8,128)S(1)}, f32[120,128]{1,0:T(8,128)S(1)}, u32[]{:S(2)}, u32[]{:S(2)}) collective-permute-start(f32[120,128]{1,0:T(8,128)S(1)} %get-tuple-element.67), channel_id=1, source_target_pairs={{0,1},{1,0},{4,8},{5,9},{8,4},{9,5},{12,13},{13,12},{2,3},{3,2},{6... | collective-permute-start | bytes 184328 | tf_op jit(solution)/shard_map/ppermute | solution.py:498
  20.0 4.1 %collective-permute-start.6 = (f32[24,128]{1,0:T(8,128)S(1)}, f32[24,128]{1,0:T(8,128)S(1)}, u32[]{:S(2)}, u32[]{:S(2)}) collective-permute-start(f32[24,128]{1,0:T(8,128)S(1)} %get-tuple-element.66), channel_id=1, source_target_pairs={{0,4},{4,0},{8,12},{12,8},{1,5},{5,1},{9,13},{13,9},{2,6},{6,2},{1... | collective-permute-start | bytes 36872 | tf_op jit(solution)/shard_map/ppermute | solution.py:488

commit v8 on v7

--- a/solution.py
+++ b/solution.py
@@ -329,7 +329,7 @@
             stress[k][c * d.levels : (c + 1) * d.levels, :] = factor[pl.ds(tile, d.levels, stride=d.tiles), :]
 
 
-def local_two_kernel(d, pad_in, factor, wind, diff, pad, raw):
+def local_two_kernel(d, pad_in, factor, masks_in, wind, diff, pad, raw, tail):
     zero_x = jnp.zeros((d.levels, LANES), F32)
     for f in range(FIELDS):
         set_x_halos(d, pad, f, zero_x, zero_x)
@@ -338,22 +338,79 @@
     lane = lax.broadcasted_iota(jnp.int32, (d.tiles, LANES), 1)
     rows = d.levels * d.tiles
 
-    def level(z, carry):
-        drag = STEP * factor[pl.ds(pl.multiple_of(z * d.tiles, 8), d.tiles), :]
+    zeros = jnp.zeros((d.tiles, LANES), F32)
+    mask = masks_in[d.parents * d.tiles :, :]
+    tail[...] = jnp.zeros_like(tail)
+    coarse_levels = d.levels // RATIO
+
+    def coarse_level(k, carry):
+        def level(i, sums):
+            z = k * RATIO + i
+            drag = STEP * factor[pl.ds(pl.multiple_of(z * d.tiles, 8), d.tiles), :]
+            added = []
+            for f in range(FIELDS):
+                v, new = stencil(d, pad, None, wind, diff, f, z, lane)
+                if f < 3:
+                    new = new - drag * v
+                raw[pl.ds(pl.multiple_of(f * rows + z * d.tiles, 8), d.tiles), :] = new
+                added.append(sums[f] + new)
+            return tuple(added)
+
+        sums = lax.fori_loop(0, RATIO, level, (zeros,) * FIELDS, unroll=8)
         for f in range(FIELDS):
-            v, new = stencil(d, pad, None, wind, diff, f, z, lane)
-            if f < 3:
-                new = new - drag * v
-            raw[pl.ds(pl.multiple_of(f * rows + z * d.tiles, 8), d.tiles), :] = new
+            tail[pl.ds(f * coarse_levels + k, 1), :] = jnp.sum(sums[f] * mask, axis=0, keepdims=True)
         return carry
 
-    lax.fori_loop(0, d.levels, level, 0, unroll=8)
-
-
-def step_two_kernel(d, raw_in, pad, zface, *refs):
+    lax.fori_loop(0, coarse_levels, coarse_level, 0)
+
+
+def tail_kernel(d, tail, pad, zface, *refs):
+    yq = refs[: d.y_sends]
+    masks_in, wind, diff, sent_sums, sent_b, sums = refs[d.y_sends :]
+    mask = masks_in[d.parents * d.tiles :, :]
+    coarse_levels = d.levels // RATIO
+    low = lax.axis_index("gz") == 0
+    end = jnp.where(low, d.levels - 1, 0)
+    end_block = jnp.where(low, coarse_levels - 1, 0)
+    wz = (0.5 * STEP) * wind[2, end]
+    lane = lax.broadcasted_iota(jnp.int32, (8, LANES), 1)
+    last = jnp.where(lane == d.columns - 1, 1.0, 0.0)
+    zeroth = jnp.where(lane == 0, 1.0, 0.0)
+    halos = []
+    for g in range(d.groups):
+        halo = yq[0][:, g * LANES : (g + 1) * LANES]
+        if d.y_sends == 2:
+            halo = halo + yq[1][:, g * LANES : (g + 1) * LANES]
+        halos.append(jnp.broadcast_to(jnp.sum(halo * mask, axis=0, keepdims=True), (8, LANES)))
+    sums[...] = tail[...]
+    lines = [[jnp.zeros((8, LANES), F32)] * coarse_levels for _ in range(FIELDS)]
+    for z in range(d.levels):
+        wy = (0.5 * STEP) * wind[1, z]
+        for f in range(FIELDS):
+            spread = STEP * diff[f]
+            weight = (spread - wy) * last + (spread + wy) * zeroth
+            moved = pltpu.roll(halos[f // d.per_group], LANES - 1 - lane_of(d, f, z), 1)
+            lines[f][z // RATIO] = lines[f][z // RATIO] + weight * moved
+    for f in range(FIELDS):
+        face = jnp.sum(zface[f * d.tiles : (f + 1) * d.tiles, :] * mask, axis=0, keepdims=True)
+        face = (STEP * diff[f] + jnp.where(low, -wz, wz)) * face
+        for k in range(coarse_levels):
+            line = lines[f][k][:1, :] + jnp.where(end_block == k, face, 0.0)
+            at = f * coarse_levels + k
+            sums[at : at + 1, :] = sums[at : at + 1, :] + line
+    sent_sums[...] = sums[...]
+    second = x_choices(d)[1]
+    for f in range(d.late):
+        sent_b[f * d.levels : (f + 1) * d.levels, :] = pad[
+            pl.ds(base_row(d, f, 0) + FRONT + second, d.levels, stride=d.block), :
+        ]
+    sent_b[d.late * d.levels :, :] = sums[...]
+
+
+def step_two_kernel(d, raw_in, zface, *refs):
     yq = refs[: d.y_sends]
     masks_in, wind, diff = refs[d.y_sends : d.y_sends + 3]
-    raw, new_fields, own_sums, sent_sums, sent_b, coarse = refs[-6:]
+    raw, new_fields, coarse = refs[-3:]
     rows = d.levels * d.tiles
     low = lax.axis_index("gz") == 0
     end = jnp.where(low, d.levels - 1, 0)
@@ -369,10 +426,10 @@
     last = jnp.where(lane == d.columns - 1, 1.0, 0.0)
     zeroth = jnp.where(lane == 0, 1.0, 0.0)
     zeros = jnp.zeros((d.tiles, LANES), F32)
-    masks = [masks_in[p * d.tiles : (p + 1) * d.tiles, :] for p in range(d.parents + 1)]
+    masks = [masks_in[p * d.tiles : (p + 1) * d.tiles, :] for p in range(d.parents)]
     coarse_levels = d.levels // RATIO
     coarse[...] = jnp.zeros_like(coarse)
-    per_parent = coarse.shape[0] // (d.parents + 1)
+    per_parent = coarse.shape[0] // d.parents
 
     def coarse_level(k, carry):
         def level(i, sums):
@@ -389,30 +446,36 @@
             return tuple(added)
 
         sums = lax.fori_loop(0, RATIO, level, (zeros,) * FIELDS, unroll=8)
-        for p in range(d.parents + 1):
+        for p in range(d.parents):
             for f in range(FIELDS):
                 line = jnp.sum(sums[f] * masks[p], axis=0, keepdims=True)
                 coarse[pl.ds(p * per_parent + f * coarse_levels + k, 1), :] = line
         return carry
 
     lax.fori_loop(0, coarse_levels, coarse_level, 0)
-    own_sums[...] = coarse[: d.parents * per_parent, :]
-    sent_sums[...] = coarse[d.parents * per_parent :, :]
-    second = x_choices(d)[1]
-    for f in range(d.late):
-        sent_b[f * d.levels : (f + 1) * d.levels, :] = pad[
-            pl.ds(base_row(d, f, 0) + FRONT + second, d.levels, stride=d.block), :
-        ]
-    sent_b[d.late * d.levels :, :] = coarse[d.parents * per_parent :, :]
-
-
-def flush_kernel(d, state, new_fields, sem):
+
+
+def flush_kernel(d, state, from_right, head, own_sums, parent_of, new_fields, sums, terms, sem):
     copy = pltpu.make_async_copy(state.at[pl.ds(0, new_fields.shape[0]), :], new_fields, sem.at[0])
     copy.start()
+    coarse_levels = d.levels // RATIO
+    terms[...] = jnp.zeros_like(terms)
+    for f in range(FIELDS):
+        cut = slice(f * d.levels, (f + 1) * d.levels)
+        term = from_right[cut, :] * head[cut, :]
+        terms[f * coarse_levels : (f + 1) * coarse_levels, :] = jnp.sum(
+            term.reshape(coarse_levels, RATIO, LANES), axis=1
+        )
+    me = lax.axis_index("gx")
+    before = jnp.maximum(me * d.tiles - 1, 0)
+    counts = (me > 0) & (parent_of[before] == me * d.parents)
+    per_parent = terms.shape[0]
+    sums[:per_parent, :] = own_sums[:per_parent, :] + jnp.where(counts, terms[...], 0.0)
+    sums[per_parent:, :] = own_sums[per_parent:, :]
     copy.wait()
 
 
-def finish_kernel(d, from_left, from_right, flushed, state_in, head, coarse, *refs):
+def finish_kernel(d, from_left, from_right, flushed, state_in, coarse, *refs):
     got_a, got_b, parent_of, place_table, counts = refs[:5]
     stress, refs = refs[5 : 5 + d.n_gx], refs[5:]
     new_fields, state, wall_stress, parent_mean, terms, gathered, placed, mean_out, sems = refs[d.n_gx :]
@@ -439,7 +502,6 @@
             b = stress[3][d.part + (f - d.late) * d.levels : d.part + (f - d.late + 1) * d.levels, :]
         left, right = left_right(d, a, b)
         left, right = from_left[cut, :] * left, from_right[cut, :] * right
-        ahead = from_right[cut, :] * head[cut, :]
         for tile, added in ((0, left), (d.tiles - 1, right)):
             place = pl.ds(f * rows + tile, d.levels, stride=d.tiles)
             state[place, :] = state[place, :] + added
@@ -450,31 +512,34 @@
             ]
             copies.append(pltpu.make_async_copy(*ends, sems.at[2 * f + i]))
             copies[-1].start()
-        for i, term in enumerate((left, right, ahead)):
+        for i, term in enumerate((left, right)):
             terms[i * per_parent + f * coarse_levels : i * per_parent + (f + 1) * coarse_levels, :] = jnp.sum(
                 term.reshape(coarse_levels, RATIO, LANES), axis=1
             )
     filled = FIELDS * coarse_levels
     if filled < per_parent:
-        for i in range(3):
+        for i in range(2):
             terms[i * per_parent + filled : (i + 1) * per_parent, :] = jnp.zeros((per_parent - filled, LANES), F32)
     got = jnp.where(even, got_b[d.late * d.levels :, :], got_a[...])
     first_tile = me * d.tiles
     first_parent = parent_of[first_tile] - me * d.parents
     last_parent = parent_of[first_tile + d.tiles - 1] - me * d.parents
-    before = jnp.maximum(first_tile - 1, 0)
-    ahead_counts = (me > 0) & (parent_of[before] == me * d.parents)
     pick_row = lax.broadcasted_iota(jnp.int32, (LANES, LANES), 0)
     pick_lane = lax.broadcasted_iota(jnp.int32, (LANES, LANES), 1)
     pick = jnp.where(pick_row // RATIO == pick_lane, 1.0, 0.0)
+    totals = []
     for p in range(d.parents):
         total = coarse[p * per_parent : (p + 1) * per_parent, :]
         total = total + jnp.where(first_parent == p, terms[:per_parent, :], 0.0)
         total = total + jnp.where(last_parent == p, terms[per_parent : 2 * per_parent, :], 0.0)
         if p == 0:
             total = total + jnp.where(me == 0, 0.0, got)
-            total = total + jnp.where(ahead_counts, terms[2 * per_parent :, :], 0.0)
-        total = jnp.dot(total, pick, precision=lax.Precision.HIGHEST, preferred_element_type=F32)
+        totals.append(total)
+    summed = jnp.dot(
+        jnp.concatenate(totals, axis=0), pick, precision=lax.Precision.HIGHEST, preferred_element_type=F32
+    )
+    for p in range(d.parents):
+        total = summed[p * per_parent : (p + 1) * per_parent, :]
         mean = total / (jnp.full(total.shape, counts[p], jnp.int32).astype(F32) * (RATIO * RATIO))
         for f in range(FIELDS):
             mean_out[p, f] = mean[f * coarse_levels : (f + 1) * coarse_levels, : d.columns // RATIO]
@@ -576,42 +641,47 @@
 
     per_parent = -(-FIELDS * (levels // RATIO) // 8) * 8
     state_t = pltpu.VMEM((rows + tiles, LANES), F32)
-    new_pad, raw = pl.pallas_call(
+    new_pad, raw, tail = pl.pallas_call(
         functools.partial(local_two_kernel, d),
-        out_shape=[pad_t, state_t],
-        in_specs=[VM] * 2 + [SM] * 2,
-        out_specs=[VM] * 2,
+        out_shape=[pad_t, state_t, pltpu.VMEM((per_parent, LANES), F32)],
+        in_specs=[VM] * 3 + [SM] * 2,
+        out_specs=[VM] * 3,
         input_output_aliases={0: 0},
         compiler_params=params,
         name="local_two",
-    )(in_vmem(new_pad), in_vmem(factor), small[1], small[2])
-    _, state, own_sums, sent_sums, sent_b = pl.pallas_call(
-        functools.partial(step_two_kernel, d),
+    )(in_vmem(new_pad), in_vmem(factor), in_vmem(masks), small[1], small[2])
+    sent_sums, sent_b = pl.pallas_call(
+        functools.partial(tail_kernel, d),
         out_shape=[
-            state_t,
-            state_t,
-            pltpu.VMEM((d.parents * per_parent, LANES), F32),
             pltpu.VMEM((per_parent, LANES), F32),
             pltpu.VMEM((d.late * levels + per_parent, LANES), F32),
         ],
         in_specs=[VM] * (4 + d.y_sends) + [SM] * 2,
-        out_specs=[VM] * 5,
-        scratch_shapes=[pltpu.VMEM(((d.parents + 1) * per_parent, LANES), F32)],
+        out_specs=[VM] * 2,
+        scratch_shapes=[pltpu.VMEM((per_parent, LANES), F32)],
+        compiler_params=params,
+        name="tail",
+    )(in_vmem(tail), in_vmem(new_pad), *faces, in_vmem(masks), small[1], small[2])
+    _, state, own_sums = pl.pallas_call(
+        functools.partial(step_two_kernel, d),
+        out_shape=[state_t, state_t, pltpu.VMEM((d.parents * per_parent, LANES), F32)],
+        in_specs=[VM] * (3 + d.y_sends) + [SM] * 2,
+        out_specs=[VM] * 3,
         input_output_aliases={0: 0},
         compiler_params=params,
         name="step_two",
-    )(in_vmem(raw), in_vmem(new_pad), *faces, in_vmem(masks), small[1], small[2])
+    )(in_vmem(raw), *faces, in_vmem(masks), small[1], small[2])
     got = x_swapped(sent_sums, sent_b)
 
-    flushed = pl.pallas_call(
+    flushed, own_sums = pl.pallas_call(
         functools.partial(flush_kernel, d),
-        out_shape=jax.ShapeDtypeStruct((rows, LANES), F32),
-        in_specs=[VM],
-        out_specs=hbm,
-        scratch_shapes=[pltpu.SemaphoreType.DMA((1,))],
+        out_shape=[jax.ShapeDtypeStruct((rows, LANES), F32), pltpu.VMEM((d.parents * per_parent, LANES), F32)],
+        in_specs=[VM] * 4 + [SM],
+        out_specs=[hbm, VM],
+        scratch_shapes=[pltpu.VMEM((per_parent, LANES), F32), pltpu.SemaphoreType.DMA((1,))],
         compiler_params=params,
         name="flush",
-    )(in_vmem(state))
+    )(*[in_vmem(a) for a in (state, from_right, head, own_sums)], small[5])
 
     new_fields, _, wall_stress, parent_mean = pl.pallas_call(
         functools.partial(finish_kernel, d),
@@ -621,10 +691,10 @@
             jax.ShapeDtypeStruct((levels * SLOTS, LANES), F32),
             jax.ShapeDtypeStruct((d.parents, FIELDS, levels // RATIO, columns // RATIO), F32),
         ],
-        in_specs=[VM] * 2 + [hbm] + [VM] * 5 + [SM] * 3 + [VM] * d.n_gx,
+        in_specs=[VM] * 2 + [hbm] + [VM] * 4 + [SM] * 3 + [VM] * d.n_gx,
         out_specs=[hbm, VM, hbm, hbm],
         scratch_shapes=[
-            pltpu.VMEM((3 * per_parent, LANES), F32),
+            pltpu.VMEM((2 * per_parent, LANES), F32),
             pltpu.VMEM((d.n_gx * d.capacity * levels, LANES), F32),
             pltpu.VMEM(((levels + 1) * SLOTS, LANES), F32),
             pltpu.VMEM((d.parents, FIELDS, levels // RATIO, columns // RATIO), F32),
@@ -637,7 +707,8 @@
         in_vmem(from_left),
         in_vmem(from_right),
         flushed,
-        *[in_vmem(a) for a in (state, head, own_sums)],
+        in_vmem(state),
+        in_vmem(own_sums),
         *got,
         small[5],
         place_table,

time: 25.4 us -> 25.2 us (level)
  waiting for transfers between devices: 2.1 us -> 1.47 us
  Pallas kernels: 9.04 us -> 9.32 us
    ppermute x6, waiting for transfers between devices: 2.09 us -> 1.46 us  [swapped(): lax.ppermute(block, axis, [(i, i ^ 1) for i in range(lax.axis_size(axis))])]
    pallas_call x1 -> x2, Pallas kernels: 1.06 us -> 1.35 us  [the longest x1 1.07 us: body(): pl.pallas_call(functools.partial(flush_kernel, d), out_shape=[jax.ShapeDt...]
  transfers between devices with their start and end apart: 11 -> 11, of which waited for: 3 -> 3; matrix products, arithmetic and copies ran while one was open for 0% -> 0% of each run, Pallas kernels for 19% -> 21%
where the time goes in v8:
time: 25.2 us; the launch traced here: 25 us
  starting transfers between devices  13.5 us (54%)
  Pallas kernels  9.32 us (37%)
  waiting for transfers between devices  1.47 us (6%)
  between operations  0.71 us (3%)
    ppermute x6, starting transfers between devices, swapped(): lax.ppermute(block, axis, [(i, i ^ 1) for i in range(lax.axis_size(axis))])  9.13 us
    ppermute x3, starting transfers between devices, crossed(): lax.ppermute(block, axis, [(i, i ^ distance) for i in range(lax.axis_size...  4.33 us
    pallas_call x1, Pallas kernels, body(): pl.pallas_call(functools.partial(pack_kernel, d), out_shape=[pltpu.SMEM(a...  1.85 us
    pallas_call x1, Pallas kernels, body(): pl.pallas_call(functools.partial(prepare_kernel, d), out_shape=[pad_t, pl...  1.78 us
    ppermute x6, waiting for transfers between devices, swapped(): lax.ppermute(block, axis, [(i, i ^ 1) for i in range(lax.axis_size(axis))])  1.46 us
    pallas_call x1, Pallas kernels, body(): pl.pallas_call(functools.partial(local_two_kernel, d), out_shape=[pad_t,...  1.38 us
    pallas_call x1, Pallas kernels, body(): pl.pallas_call(functools.partial(step_one_kernel, d), out_shape=[pad_t, p...  1.26 us
    pallas_call x1, Pallas kernels, body(): pl.pallas_call(functools.partial(flush_kernel, d), out_shape=[jax.ShapeDt...  1.07 us
  transfers between devices with their start and end apart: 11, of which 3 were waited for; matrix products, arithmetic and copies ran while one was open for 0% of the time, Pallas kernels for 21%

profile of v8, /device:TPU:0, one launch (start us, length us, event | category | flops | bytes accessed | tf_op | source)
XLA Modules:
  0.0 25.0 jit_solution(2176462425880852676)
XLA Ops:
  0.6 1.9 %pack.1 = (s32[16,128]{1,0:T(8,128)S(1)}, f32[3,32]{1,0:T(4,128)S(4)}, f32[5]{0:T(128)S(4)}, s32[16]{0:T(128)S(4)}, s32[64]{0:T(128)S(4)}, /*index=5*/s32[64]{0:...) custom-call(f32[5,32,16,128]{3,2,1,0:T(8,128)} %fields.1, ...), custom_call_target="tpu_custom_call" | custom-call | tf_op jit(solution)/shard_map/pack/pallas_call | solution.py:599
  2.5 3.1 %collective-permute-start = (f32[160,128]{1,0:T(8,128)S(1)}, f32[160,128]{1,0:T(8,128)S(1)}, u32[]{:S(2)}, u32[]{:S(2)}) collective-permute-start(f32[160,128]{1,0:T(8,128)S(1)} %get-tuple-element.53), channel_id=1, source_target_pairs={{0,4},{4,0},{8,12},{12,8},{1,5},{5,1},{9,13},{13,9},{2,6},{6,2},{1... | collective-permute-start | bytes 245768 | tf_op jit(solution)/shard_map/ppermute | solution.py:553
  5.6 0.0 collective-permute-start.1
  5.6 0.5 %collective-permute-start.2 = (f32[80,128]{1,0:T(8,128)S(1)}, f32[80,128]{1,0:T(8,128)S(1)}, u32[]{:S(2)}, u32[]{:S(2)}) collective-permute-start(f32[80,128]{1,0:T(8,128)S(1)} %get-tuple-element.55), channel_id=1, source_target_pairs={{0,1},{1,0},{2,3},{3,2},{4,5},{5,4},{6,7},{7,6},{8,9},{9,8},{10,11... | collective-permute-start | bytes 122888 | tf_op jit(solution)/shard_map/ppermute | solution.py:553
  6.1 1.5 %collective-permute-start.3 = (f32[16,384]{1,0:T(8,128)S(1)}, f32[16,384]{1,0:T(8,128)S(1)}, u32[]{:S(2)}, u32[]{:S(2)}) collective-permute-start(f32[16,384]{1,0:T(8,128)S(1)} %get-tuple-element.56), channel_id=1, source_target_pairs={{0,2},{2,0},{1,3},{3,1},{4,6},{6,4},{5,7},{7,5},{8,10},{10,8},{9,1... | collective-permute-start | bytes 73736 | tf_op jit(solution)/shard_map/ppermute | solution.py:553
  7.6 1.8 %prepare.1 = (f32[4088,128]{1,0:T(8,128)S(1)}, f32[16,128]{1,0:T(8,128)S(1)}, f32[160,128]{1,0:T(8,128)S(1)}, f32[160,128]{1,0:T(8,128)S(1)}, f32[48,128]{1,0:T(...) custom-call(f32[4088,128]{1,0:T(8,128)S(1)} %get-tuple-element.43.pad, ...), custom_call_target="tpu_custom_call" | custom-call | tf_op jit(solution)/shard_map/prepare/pallas_call | solution.py:616
  9.4 0.5 %collective-permute-done.3.refs_0_ = f32[16,384]{1,0:T(8,128)S(1)} collective-permute-done((f32[16,384]{1,0:T(8,128)S(1)}, f32[16,384]{1,0:T(8,128)S(1)}, u32[]{:S(2)}, u32[]{:S(2)}) %collective-permute-start.3) | collective-permute-done | bytes 24608 | tf_op jit(solution)/shard_map/ppermute | solution.py:553
  9.9 0.0 collective-permute-done.2.zface
  9.9 0.0 collective-permute-done.xa
  9.9 0.0 collective-permute-done.1.xb
  9.9 1.3 %step_one.1 = (f32[4088,128]{1,0:T(8,128)S(1)}, f32[4088,128]{1,0:T(8,128)S(1)}, f32[528,128]{1,0:T(8,128)S(1)}, f32[80,128]{1,0:T(8,128)S(1)}, f32[160,128]{1,0...) custom-call(f32[4088,128]{1,0:T(8,128)S(1)} %get-tuple-element.52.pa, ...), custom_call_target="tpu_custom_call", output_to_operand_aliasing={{0}: (0, {})} | custom-call | tf_op jit(solution)/shard_map/step_one/pallas_call | solution.py:628
  11.2 2.7 %collective-permute-start.8 = (f32[288,128]{1,0:T(8,128)S(1)}, f32[288,128]{1,0:T(8,128)S(1)}, u32[]{:S(2)}, u32[]{:S(2)}) collective-permute-start(f32[288,128]{1,0:T(8,128)S(1)} %get-tuple-element.77), channel_id=1, source_target_pairs={{0,4},{4,0},{8,12},{12,8},{1,5},{5,1},{9,13},{13,9},{2,6},{6,2},{1... | collective-permute-start | bytes 442376 | tf_op jit(solution)/shard_map/ppermute | solution.py:567
  13.9 0.0 collective-permute-start.4
  13.9 1.5 %collective-permute-start.10 = (f32[192,128]{1,0:T(8,128)S(1)}, f32[192,128]{1,0:T(8,128)S(1)}, u32[]{:S(2)}, u32[]{:S(2)}) collective-permute-start(f32[192,128]{1,0:T(8,128)S(1)} %get-tuple-element.79), channel_id=1, source_target_pairs={{0,12},{4,8},{8,4},{12,0},{1,13},{5,9},{9,5},{13,1},{2,14},{6,10},... | collective-permute-start | bytes 294920 | tf_op jit(solution)/shard_map/ppermute | solution.py:567
  15.4 1.5 %collective-permute-start.5 = (f32[16,384]{1,0:T(8,128)S(1)}, f32[16,384]{1,0:T(8,128)S(1)}, u32[]{:S(2)}, u32[]{:S(2)}) collective-permute-start(f32[16,384]{1,0:T(8,128)S(1)} %get-tuple-element.64), channel_id=1, source_target_pairs={{0,2},{2,0},{1,3},{3,1},{4,6},{6,4},{5,7},{7,5},{8,10},{10,8},{9,1... | collective-permute-start | bytes 73736 | tf_op jit(solution)/shard_map/ppermute | solution.py:553
  16.9 0.1 collective-permute-start.9
  17.0 1.4 %local_two.1 = (f32[4088,128]{1,0:T(8,128)S(1)}, f32[2576,128]{1,0:T(8,128)S(1)}, f32[24,128]{1,0:T(8,128)S(1)}) custom-call(f32[4088,128]{1,0:T(8,128)S(1)} %get-tuple-element.59.pad_in, f32[528,128]{1,0:T(8,128)S(1)} %get-tuple-element.60.factor, f32[48,128]{1,0:T(8,128)S(1)} %get-tuple-element.61.masks_in.refs_1_, ...), custom_call_target="tpu_custom_call", output_to_operand_aliasing={{0}: (0, {})} | custom-call | tf_op jit(solution)/shard_map/local_two/pallas_call | solution.py:644
  18.4 0.8 %collective-permute-done.5.refs_0_ = f32[16,384]{1,0:T(8,128)S(1)} collective-permute-done((f32[16,384]{1,0:T(8,128)S(1)}, f32[16,384]{1,0:T(8,128)S(1)}, u32[]{:S(2)}, u32[]{:S(2)}) %collective-permute-start.5) | collective-permute-done | bytes 24608 | tf_op jit(solution)/shard_map/ppermute | solution.py:553
  19.2 0.0 collective-permute-done.4.zface
  19.2 0.3 %tail.1 = (f32[24,128]{1,0:T(8,128)S(1)}, f32[120,128]{1,0:T(8,128)S(1)}) custom-call(f32[24,128]{1,0:T(8,128)S(1)} %get-tuple-element.70.tail, f32[4088,128]{1,0:T(8,128)S(1)} %get-tuple-element.71.pad, f32[80,128]{1,0:T(8,128)S(1)} %collective-permute-done.4.zface, f32[16,384]{1,0:T(8,128)S(1)} %collective-permute-done.5.refs_0_, ...), custom_call_target="tpu_custom_call" | custom-call | tf_op jit(solution)/shard_map/tail/pallas_call | solution.py:653
  19.5 0.1 collective-permute-start.7
  19.6 2.5 %collective-permute-start.6 = (f32[24,128]{1,0:T(8,128)S(1)}, f32[24,128]{1,0:T(8,128)S(1)}, u32[]{:S(2)}, u32[]{:S(2)}) collective-permute-start(f32[24,128]{1,0:T(8,128)S(1)} %get-tuple-element.72), channel_id=1, source_target_pairs={{0,4},{4,0},{8,12},{12,8},{1,5},{5,1},{9,13},{13,9},{2,6},{6,2},{1... | collective-permute-start | bytes 36872 | tf_op jit(solution)/shard_map/ppermute | solution.py:553
  22.1 0.7 %step_two.1 = (f32[2576,128]{1,0:T(8,128)S(1)}, f32[2576,128]{1,0:T(8,128)S(1)}, f32[48,128]{1,0:T(8,128)S(1)}) custom-call(f32[2576,128]{1,0:T(8,128)S(1)} %get-tuple-element.62.raw_in, f32[80,128]{1,0:T(8,128)S(1)} %collective-permute-done.4.zface, f32[16,384]{1,0:T(8,128)S(1)} %collective-permute-done.5.refs_0_, ...), custom_call_target="tpu_custom_call", output_to_operand_aliasing={{0}: (0, {})} | custom-call | tf_op jit(solution)/shard_map/step_two/pallas_call | solution.py:665
  22.8 1.1 %flush.1 = (f32[2560,128]{1,0:T(8,128)}, f32[48,128]{1,0:T(8,128)S(1)}) custom-call(f32[2576,128]{1,0:T(8,128)S(1)} %get-tuple-element.65.state.state_in, f32[160,128]{1,0:T(8,128)S(1)} %get-tuple-element.51.refs_3_.from_right, f32[160,128]{1,0:T(8,128)S(1)} %get-tuple-element.66.head, f32[48,128]{1,0:T(8,128)S(1)} %get-tuple-element.67.own_sums, ...), custom_call_target="tpu_custom_call" | custom-call | tf_op jit(solution)/shard_map/flush/pallas_call | solution.py:676
  23.9 0.1 collective-permute-done.6.refs_0_
  24.0 0.0 collective-permute-done.9.refs_7_
  24.0 0.0 collective-permute-done.10.refs_8_
  24.0 0.0 collective-permute-done.7.refs_1_
  24.0 0.0 collective-permute-done.8.refs_6_
  24.0 1.0 %finish.1 = (f32[2560,128]{1,0:T(8,128)}, f32[2576,128]{1,0:T(8,128)S(1)}, f32[256,128]{1,0:T(8,128)}, f32[2,5,4,16]{3,2,1,0:T(4,128)}) custom-call(f32[160,128]{1,0:T(8,128)S(1)} %get-tuple-element.50.refs_2_.from_left, f32[160,128]{1,0:T(8,128)S(1)} %get-tuple-element.51.refs_3_.from_right, ...), custom_call_target="tpu_custom_call", output_to_operand_aliasing={{0}: (2, {}), {1}: (3, {})} | custom-call | tf_op jit(solution)/shard_map/finish/pallas_call | solution.py:686
Async XLA Ops:
  2.5 7.4 %collective-permute-start = (f32[160,128]{1,0:T(8,128)S(1)}, f32[160,128]{1,0:T(8,128)S(1)}, u32[]{:S(2)}, u32[]{:S(2)}) collective-permute-start(f32[160,128]{1,0:T(8,128)S(1)} %get-tuple-element.53), channel_id=1, source_target_pairs={{0,4},{4,0},{8,12},{12,8},{1,5},{5,1},{9,13},{13,9},{2,6},{6,2},{1... | collective-permute-start | bytes 245768 | tf_op jit(solution)/shard_map/ppermute | solution.py:553
  5.6 4.3 %collective-permute-start.1 = (f32[160,128]{1,0:T(8,128)S(1)}, f32[160,128]{1,0:T(8,128)S(1)}, u32[]{:S(2)}, u32[]{:S(2)}) collective-permute-start(f32[160,128]{1,0:T(8,128)S(1)} %get-tuple-element.54), channel_id=1, source_target_pairs={{0,1},{1,0},{4,8},{5,9},{8,4},{9,5},{12,13},{13,12},{2,3},{3,2},{6... | collective-permute-start | bytes 245768 | tf_op jit(solution)/shard_map/ppermute | solution.py:563
  5.6 4.3 %collective-permute-start.2 = (f32[80,128]{1,0:T(8,128)S(1)}, f32[80,128]{1,0:T(8,128)S(1)}, u32[]{:S(2)}, u32[]{:S(2)}) collective-permute-start(f32[80,128]{1,0:T(8,128)S(1)} %get-tuple-element.55), channel_id=1, source_target_pairs={{0,1},{1,0},{2,3},{3,2},{4,5},{5,4},{6,7},{7,6},{8,9},{9,8},{10,11... | collective-permute-start | bytes 122888 | tf_op jit(solution)/shard_map/ppermute | solution.py:553
  6.1 3.8 %collective-permute-start.3 = (f32[16,384]{1,0:T(8,128)S(1)}, f32[16,384]{1,0:T(8,128)S(1)}, u32[]{:S(2)}, u32[]{:S(2)}) collective-permute-start(f32[16,384]{1,0:T(8,128)S(1)} %get-tuple-element.56), channel_id=1, source_target_pairs={{0,2},{2,0},{1,3},{3,1},{4,6},{6,4},{5,7},{7,5},{8,10},{10,8},{9,1... | collective-permute-start | bytes 73736 | tf_op jit(solution)/shard_map/ppermute | solution.py:553
  11.2 12.8 %collective-permute-start.8 = (f32[288,128]{1,0:T(8,128)S(1)}, f32[288,128]{1,0:T(8,128)S(1)}, u32[]{:S(2)}, u32[]{:S(2)}) collective-permute-start(f32[288,128]{1,0:T(8,128)S(1)} %get-tuple-element.77), channel_id=1, source_target_pairs={{0,4},{4,0},{8,12},{12,8},{1,5},{5,1},{9,13},{13,9},{2,6},{6,2},{1... | collective-permute-start | bytes 442376 | tf_op jit(solution)/shard_map/ppermute | solution.py:567
  13.9 5.3 %collective-permute-start.4 = (f32[80,128]{1,0:T(8,128)S(1)}, f32[80,128]{1,0:T(8,128)S(1)}, u32[]{:S(2)}, u32[]{:S(2)}) collective-permute-start(f32[80,128]{1,0:T(8,128)S(1)} %get-tuple-element.63), channel_id=1, source_target_pairs={{0,1},{1,0},{2,3},{3,2},{4,5},{5,4},{6,7},{7,6},{8,9},{9,8},{10,11... | collective-permute-start | bytes 122888 | tf_op jit(solution)/shard_map/ppermute | solution.py:553
  13.9 10.1 %collective-permute-start.10 = (f32[192,128]{1,0:T(8,128)S(1)}, f32[192,128]{1,0:T(8,128)S(1)}, u32[]{:S(2)}, u32[]{:S(2)}) collective-permute-start(f32[192,128]{1,0:T(8,128)S(1)} %get-tuple-element.79), channel_id=1, source_target_pairs={{0,12},{4,8},{8,4},{12,0},{1,13},{5,9},{9,5},{13,1},{2,14},{6,10},... | collective-permute-start | bytes 294920 | tf_op jit(solution)/shard_map/ppermute | solution.py:567
  15.4 3.8 %collective-permute-start.5 = (f32[16,384]{1,0:T(8,128)S(1)}, f32[16,384]{1,0:T(8,128)S(1)}, u32[]{:S(2)}, u32[]{:S(2)}) collective-permute-start(f32[16,384]{1,0:T(8,128)S(1)} %get-tuple-element.64), channel_id=1, source_target_pairs={{0,2},{2,0},{1,3},{3,1},{4,6},{6,4},{5,7},{7,5},{8,10},{10,8},{9,1... | collective-permute-start | bytes 73736 | tf_op jit(solution)/shard_map/ppermute | solution.py:553
  16.9 7.1 %collective-permute-start.9 = (f32[128,128]{1,0:T(8,128)S(1)}, f32[128,128]{1,0:T(8,128)S(1)}, u32[]{:S(2)}, u32[]{:S(2)}) collective-permute-start(f32[128,128]{1,0:T(8,128)S(1)} %get-tuple-element.78), channel_id=1, source_target_pairs={{0,8},{4,12},{8,0},{12,4},{1,9},{5,13},{9,1},{13,5},{2,10},{6,14},... | collective-permute-start | bytes 196616 | tf_op jit(solution)/shard_map/ppermute | solution.py:567
  19.5 4.5 %collective-permute-start.7 = (f32[120,128]{1,0:T(8,128)S(1)}, f32[120,128]{1,0:T(8,128)S(1)}, u32[]{:S(2)}, u32[]{:S(2)}) collective-permute-start(f32[120,128]{1,0:T(8,128)S(1)} %get-tuple-element.73), channel_id=1, source_target_pairs={{0,1},{1,0},{4,8},{5,9},{8,4},{9,5},{12,13},{13,12},{2,3},{3,2},{6... | collective-permute-start | bytes 184328 | tf_op jit(solution)/shard_map/ppermute | solution.py:563
  19.6 4.4 %collective-permute-start.6 = (f32[24,128]{1,0:T(8,128)S(1)}, f32[24,128]{1,0:T(8,128)S(1)}, u32[]{:S(2)}, u32[]{:S(2)}) collective-permute-start(f32[24,128]{1,0:T(8,128)S(1)} %get-tuple-element.72), channel_id=1, source_target_pairs={{0,4},{4,0},{8,12},{12,8},{1,5},{5,1},{9,13},{13,9},{2,6},{6,2},{1... | collective-permute-start | bytes 36872 | tf_op jit(solution)/shard_map/ppermute | solution.py:553

commit v9 on v8

--- a/solution.py
+++ b/solution.py
@@ -305,7 +305,7 @@
         factor[pl.ds(pl.multiple_of(z * d.tiles, 8), d.tiles), :] = coef * speed(*news[:3])
         return carry
 
-    lax.fori_loop(0, d.levels, level, 0, unroll=8)
+    lax.fori_loop(0, d.levels, level, 0, unroll=16)
     packed = [jnp.zeros((d.tiles, LANES), F32)] * d.groups
     for f in range(FIELDS):
         packed = add_edges(d, packed, new_pad, f, lane)

time: 25.2 us -> 25.1 us (level)
  no operation moved by 1% of the time
where the time goes in v9:
time: 25.1 us; the launch traced here: 24.9 us
  starting transfers between devices  13.5 us (54%)
  Pallas kernels  9.18 us (37%)
  waiting for transfers between devices  1.47 us (6%)
  between operations  0.71 us (3%)
    ppermute x6, starting transfers between devices, swapped(): lax.ppermute(block, axis, [(i, i ^ 1) for i in range(lax.axis_size(axis))])  9.13 us
    ppermute x3, starting transfers between devices, crossed(): lax.ppermute(block, axis, [(i, i ^ distance) for i in range(lax.axis_size...  4.33 us
    pallas_call x1, Pallas kernels, body(): pl.pallas_call(functools.partial(pack_kernel, d), out_shape=[pltpu.SMEM(a...  1.85 us
    pallas_call x1, Pallas kernels, body(): pl.pallas_call(functools.partial(prepare_kernel, d), out_shape=[pad_t, pl...  1.78 us
    ppermute x6, waiting for transfers between devices, swapped(): lax.ppermute(block, axis, [(i, i ^ 1) for i in range(lax.axis_size(axis))])  1.46 us
    pallas_call x1, Pallas kernels, body(): pl.pallas_call(functools.partial(local_two_kernel, d), out_shape=[pad_t,...  1.38 us
    pallas_call x1, Pallas kernels, body(): pl.pallas_call(functools.partial(step_one_kernel, d), out_shape=[pad_t, p...  1.12 us
    pallas_call x1, Pallas kernels, body(): pl.pallas_call(functools.partial(flush_kernel, d), out_shape=[jax.ShapeDt...  1.07 us
  transfers between devices with their start and end apart: 11, of which 3 were waited for; matrix products, arithmetic and copies ran while one was open for 0% of the time, Pallas kernels for 21%

profile of v9, /device:TPU:0, one launch (start us, length us, event | category | flops | bytes accessed | tf_op | source)
XLA Modules:
  0.0 24.9 jit_solution(2900017102166899069)
XLA Ops:
  0.6 1.9 %pack.1 = (s32[16,128]{1,0:T(8,128)S(1)}, f32[3,32]{1,0:T(4,128)S(4)}, f32[5]{0:T(128)S(4)}, s32[16]{0:T(128)S(4)}, s32[64]{0:T(128)S(4)}, /*index=5*/s32[64]{0:...) custom-call(f32[5,32,16,128]{3,2,1,0:T(8,128)} %fields.1, ...), custom_call_target="tpu_custom_call" | custom-call | tf_op jit(solution)/shard_map/pack/pallas_call | solution.py:599
  2.5 3.1 %collective-permute-start = (f32[160,128]{1,0:T(8,128)S(1)}, f32[160,128]{1,0:T(8,128)S(1)}, u32[]{:S(2)}, u32[]{:S(2)}) collective-permute-start(f32[160,128]{1,0:T(8,128)S(1)} %get-tuple-element.53), channel_id=1, source_target_pairs={{0,4},{4,0},{8,12},{12,8},{1,5},{5,1},{9,13},{13,9},{2,6},{6,2},{1... | collective-permute-start | bytes 245768 | tf_op jit(solution)/shard_map/ppermute | solution.py:553
  5.6 0.0 collective-permute-start.1
  5.6 0.5 %collective-permute-start.2 = (f32[80,128]{1,0:T(8,128)S(1)}, f32[80,128]{1,0:T(8,128)S(1)}, u32[]{:S(2)}, u32[]{:S(2)}) collective-permute-start(f32[80,128]{1,0:T(8,128)S(1)} %get-tuple-element.55), channel_id=1, source_target_pairs={{0,1},{1,0},{2,3},{3,2},{4,5},{5,4},{6,7},{7,6},{8,9},{9,8},{10,11... | collective-permute-start | bytes 122888 | tf_op jit(solution)/shard_map/ppermute | solution.py:553
  6.1 1.5 %collective-permute-start.3 = (f32[16,384]{1,0:T(8,128)S(1)}, f32[16,384]{1,0:T(8,128)S(1)}, u32[]{:S(2)}, u32[]{:S(2)}) collective-permute-start(f32[16,384]{1,0:T(8,128)S(1)} %get-tuple-element.56), channel_id=1, source_target_pairs={{0,2},{2,0},{1,3},{3,1},{4,6},{6,4},{5,7},{7,5},{8,10},{10,8},{9,1... | collective-permute-start | bytes 73736 | tf_op jit(solution)/shard_map/ppermute | solution.py:553
  7.6 1.8 %prepare.1 = (f32[4088,128]{1,0:T(8,128)S(1)}, f32[16,128]{1,0:T(8,128)S(1)}, f32[160,128]{1,0:T(8,128)S(1)}, f32[160,128]{1,0:T(8,128)S(1)}, f32[48,128]{1,0:T(...) custom-call(f32[4088,128]{1,0:T(8,128)S(1)} %get-tuple-element.43.pad, ...), custom_call_target="tpu_custom_call" | custom-call | tf_op jit(solution)/shard_map/prepare/pallas_call | solution.py:616
  9.4 0.5 %collective-permute-done.3.refs_0_ = f32[16,384]{1,0:T(8,128)S(1)} collective-permute-done((f32[16,384]{1,0:T(8,128)S(1)}, f32[16,384]{1,0:T(8,128)S(1)}, u32[]{:S(2)}, u32[]{:S(2)}) %collective-permute-start.3) | collective-permute-done | bytes 24608 | tf_op jit(solution)/shard_map/ppermute | solution.py:553
  9.9 0.0 collective-permute-done.2.zface
  9.9 0.0 collective-permute-done.xa
  9.9 0.0 collective-permute-done.1.xb
  9.9 1.1 %step_one.1 = (f32[4088,128]{1,0:T(8,128)S(1)}, f32[4088,128]{1,0:T(8,128)S(1)}, f32[528,128]{1,0:T(8,128)S(1)}, f32[80,128]{1,0:T(8,128)S(1)}, f32[160,128]{1,0...) custom-call(f32[4088,128]{1,0:T(8,128)S(1)} %get-tuple-element.52.pa, ...), custom_call_target="tpu_custom_call", output_to_operand_aliasing={{0}: (0, {})} | custom-call | tf_op jit(solution)/shard_map/step_one/pallas_call | solution.py:628
  11.1 2.7 %collective-permute-start.8 = (f32[288,128]{1,0:T(8,128)S(1)}, f32[288,128]{1,0:T(8,128)S(1)}, u32[]{:S(2)}, u32[]{:S(2)}) collective-permute-start(f32[288,128]{1,0:T(8,128)S(1)} %get-tuple-element.77), channel_id=1, source_target_pairs={{0,4},{4,0},{8,12},{12,8},{1,5},{5,1},{9,13},{13,9},{2,6},{6,2},{1... | collective-permute-start | bytes 442376 | tf_op jit(solution)/shard_map/ppermute | solution.py:567
  13.8 0.0 collective-permute-start.4
  13.8 1.5 %collective-permute-start.10 = (f32[192,128]{1,0:T(8,128)S(1)}, f32[192,128]{1,0:T(8,128)S(1)}, u32[]{:S(2)}, u32[]{:S(2)}) collective-permute-start(f32[192,128]{1,0:T(8,128)S(1)} %get-tuple-element.79), channel_id=1, source_target_pairs={{0,12},{4,8},{8,4},{12,0},{1,13},{5,9},{9,5},{13,1},{2,14},{6,10},... | collective-permute-start | bytes 294920 | tf_op jit(solution)/shard_map/ppermute | solution.py:567
  15.3 1.5 %collective-permute-start.5 = (f32[16,384]{1,0:T(8,128)S(1)}, f32[16,384]{1,0:T(8,128)S(1)}, u32[]{:S(2)}, u32[]{:S(2)}) collective-permute-start(f32[16,384]{1,0:T(8,128)S(1)} %get-tuple-element.64), channel_id=1, source_target_pairs={{0,2},{2,0},{1,3},{3,1},{4,6},{6,4},{5,7},{7,5},{8,10},{10,8},{9,1... | collective-permute-start | bytes 73736 | tf_op jit(solution)/shard_map/ppermute | solution.py:553
  16.8 0.1 collective-permute-start.9
  16.9 1.4 %local_two.1 = (f32[4088,128]{1,0:T(8,128)S(1)}, f32[2576,128]{1,0:T(8,128)S(1)}, f32[24,128]{1,0:T(8,128)S(1)}) custom-call(f32[4088,128]{1,0:T(8,128)S(1)} %get-tuple-element.59.pad_in, f32[528,128]{1,0:T(8,128)S(1)} %get-tuple-element.60.factor, f32[48,128]{1,0:T(8,128)S(1)} %get-tuple-element.61.masks_in.refs_1_, ...), custom_call_target="tpu_custom_call", output_to_operand_aliasing={{0}: (0, {})} | custom-call | tf_op jit(solution)/shard_map/local_two/pallas_call | solution.py:644
  18.3 0.8 %collective-permute-done.5.refs_0_ = f32[16,384]{1,0:T(8,128)S(1)} collective-permute-done((f32[16,384]{1,0:T(8,128)S(1)}, f32[16,384]{1,0:T(8,128)S(1)}, u32[]{:S(2)}, u32[]{:S(2)}) %collective-permute-start.5) | collective-permute-done | bytes 24608 | tf_op jit(solution)/shard_map/ppermute | solution.py:553
  19.1 0.0 collective-permute-done.4.zface
  19.1 0.3 %tail.1 = (f32[24,128]{1,0:T(8,128)S(1)}, f32[120,128]{1,0:T(8,128)S(1)}) custom-call(f32[24,128]{1,0:T(8,128)S(1)} %get-tuple-element.70.tail, f32[4088,128]{1,0:T(8,128)S(1)} %get-tuple-element.71.pad, f32[80,128]{1,0:T(8,128)S(1)} %collective-permute-done.4.zface, f32[16,384]{1,0:T(8,128)S(1)} %collective-permute-done.5.refs_0_, ...), custom_call_target="tpu_custom_call" | custom-call | tf_op jit(solution)/shard_map/tail/pallas_call | solution.py:653
  19.4 0.1 collective-permute-start.7
  19.5 2.5 %collective-permute-start.6 = (f32[24,128]{1,0:T(8,128)S(1)}, f32[24,128]{1,0:T(8,128)S(1)}, u32[]{:S(2)}, u32[]{:S(2)}) collective-permute-start(f32[24,128]{1,0:T(8,128)S(1)} %get-tuple-element.72), channel_id=1, source_target_pairs={{0,4},{4,0},{8,12},{12,8},{1,5},{5,1},{9,13},{13,9},{2,6},{6,2},{1... | collective-permute-start | bytes 36872 | tf_op jit(solution)/shard_map/ppermute | solution.py:553
  22.0 0.7 %step_two.1 = (f32[2576,128]{1,0:T(8,128)S(1)}, f32[2576,128]{1,0:T(8,128)S(1)}, f32[48,128]{1,0:T(8,128)S(1)}) custom-call(f32[2576,128]{1,0:T(8,128)S(1)} %get-tuple-element.62.raw_in, f32[80,128]{1,0:T(8,128)S(1)} %collective-permute-done.4.zface, f32[16,384]{1,0:T(8,128)S(1)} %collective-permute-done.5.refs_0_, ...), custom_call_target="tpu_custom_call", output_to_operand_aliasing={{0}: (0, {})} | custom-call | tf_op jit(solution)/shard_map/step_two/pallas_call | solution.py:665
  22.7 1.1 %flush.1 = (f32[2560,128]{1,0:T(8,128)}, f32[48,128]{1,0:T(8,128)S(1)}) custom-call(f32[2576,128]{1,0:T(8,128)S(1)} %get-tuple-element.65.state.state_in, f32[160,128]{1,0:T(8,128)S(1)} %get-tuple-element.51.refs_3_.from_right, f32[160,128]{1,0:T(8,128)S(1)} %get-tuple-element.66.head, f32[48,128]{1,0:T(8,128)S(1)} %get-tuple-element.67.own_sums, ...), custom_call_target="tpu_custom_call" | custom-call | tf_op jit(solution)/shard_map/flush/pallas_call | solution.py:676
  23.8 0.1 collective-permute-done.6.refs_0_
  23.9 0.0 collective-permute-done.9.refs_7_
  23.9 0.0 collective-permute-done.10.refs_8_
  23.9 0.0 collective-permute-done.7.refs_1_
  23.9 0.0 collective-permute-done.8.refs_6_
  23.9 1.0 %finish.1 = (f32[2560,128]{1,0:T(8,128)}, f32[2576,128]{1,0:T(8,128)S(1)}, f32[256,128]{1,0:T(8,128)}, f32[2,5,4,16]{3,2,1,0:T(4,128)}) custom-call(f32[160,128]{1,0:T(8,128)S(1)} %get-tuple-element.50.refs_2_.from_left, f32[160,128]{1,0:T(8,128)S(1)} %get-tuple-element.51.refs_3_.from_right, ...), custom_call_target="tpu_custom_call", output_to_operand_aliasing={{0}: (2, {}), {1}: (3, {})} | custom-call | tf_op jit(solution)/shard_map/finish/pallas_call | solution.py:686
Async XLA Ops:
  2.5 7.4 %collective-permute-start = (f32[160,128]{1,0:T(8,128)S(1)}, f32[160,128]{1,0:T(8,128)S(1)}, u32[]{:S(2)}, u32[]{:S(2)}) collective-permute-start(f32[160,128]{1,0:T(8,128)S(1)} %get-tuple-element.53), channel_id=1, source_target_pairs={{0,4},{4,0},{8,12},{12,8},{1,5},{5,1},{9,13},{13,9},{2,6},{6,2},{1... | collective-permute-start | bytes 245768 | tf_op jit(solution)/shard_map/ppermute | solution.py:553
  5.6 4.3 %collective-permute-start.1 = (f32[160,128]{1,0:T(8,128)S(1)}, f32[160,128]{1,0:T(8,128)S(1)}, u32[]{:S(2)}, u32[]{:S(2)}) collective-permute-start(f32[160,128]{1,0:T(8,128)S(1)} %get-tuple-element.54), channel_id=1, source_target_pairs={{0,1},{1,0},{4,8},{5,9},{8,4},{9,5},{12,13},{13,12},{2,3},{3,2},{6... | collective-permute-start | bytes 245768 | tf_op jit(solution)/shard_map/ppermute | solution.py:563
  5.6 4.3 %collective-permute-start.2 = (f32[80,128]{1,0:T(8,128)S(1)}, f32[80,128]{1,0:T(8,128)S(1)}, u32[]{:S(2)}, u32[]{:S(2)}) collective-permute-start(f32[80,128]{1,0:T(8,128)S(1)} %get-tuple-element.55), channel_id=1, source_target_pairs={{0,1},{1,0},{2,3},{3,2},{4,5},{5,4},{6,7},{7,6},{8,9},{9,8},{10,11... | collective-permute-start | bytes 122888 | tf_op jit(solution)/shard_map/ppermute | solution.py:553
  6.1 3.8 %collective-permute-start.3 = (f32[16,384]{1,0:T(8,128)S(1)}, f32[16,384]{1,0:T(8,128)S(1)}, u32[]{:S(2)}, u32[]{:S(2)}) collective-permute-start(f32[16,384]{1,0:T(8,128)S(1)} %get-tuple-element.56), channel_id=1, source_target_pairs={{0,2},{2,0},{1,3},{3,1},{4,6},{6,4},{5,7},{7,5},{8,10},{10,8},{9,1... | collective-permute-start | bytes 73736 | tf_op jit(solution)/shard_map/ppermute | solution.py:553
  11.1 12.8 %collective-permute-start.8 = (f32[288,128]{1,0:T(8,128)S(1)}, f32[288,128]{1,0:T(8,128)S(1)}, u32[]{:S(2)}, u32[]{:S(2)}) collective-permute-start(f32[288,128]{1,0:T(8,128)S(1)} %get-tuple-element.77), channel_id=1, source_target_pairs={{0,4},{4,0},{8,12},{12,8},{1,5},{5,1},{9,13},{13,9},{2,6},{6,2},{1... | collective-permute-start | bytes 442376 | tf_op jit(solution)/shard_map/ppermute | solution.py:567
  13.8 5.3 %collective-permute-start.4 = (f32[80,128]{1,0:T(8,128)S(1)}, f32[80,128]{1,0:T(8,128)S(1)}, u32[]{:S(2)}, u32[]{:S(2)}) collective-permute-start(f32[80,128]{1,0:T(8,128)S(1)} %get-tuple-element.63), channel_id=1, source_target_pairs={{0,1},{1,0},{2,3},{3,2},{4,5},{5,4},{6,7},{7,6},{8,9},{9,8},{10,11... | collective-permute-start | bytes 122888 | tf_op jit(solution)/shard_map/ppermute | solution.py:553
  13.8 10.1 %collective-permute-start.10 = (f32[192,128]{1,0:T(8,128)S(1)}, f32[192,128]{1,0:T(8,128)S(1)}, u32[]{:S(2)}, u32[]{:S(2)}) collective-permute-start(f32[192,128]{1,0:T(8,128)S(1)} %get-tuple-element.79), channel_id=1, source_target_pairs={{0,12},{4,8},{8,4},{12,0},{1,13},{5,9},{9,5},{13,1},{2,14},{6,10},... | collective-permute-start | bytes 294920 | tf_op jit(solution)/shard_map/ppermute | solution.py:567
  15.3 3.8 %collective-permute-start.5 = (f32[16,384]{1,0:T(8,128)S(1)}, f32[16,384]{1,0:T(8,128)S(1)}, u32[]{:S(2)}, u32[]{:S(2)}) collective-permute-start(f32[16,384]{1,0:T(8,128)S(1)} %get-tuple-element.64), channel_id=1, source_target_pairs={{0,2},{2,0},{1,3},{3,1},{4,6},{6,4},{5,7},{7,5},{8,10},{10,8},{9,1... | collective-permute-start | bytes 73736 | tf_op jit(solution)/shard_map/ppermute | solution.py:553
  16.8 7.1 %collective-permute-start.9 = (f32[128,128]{1,0:T(8,128)S(1)}, f32[128,128]{1,0:T(8,128)S(1)}, u32[]{:S(2)}, u32[]{:S(2)}) collective-permute-start(f32[128,128]{1,0:T(8,128)S(1)} %get-tuple-element.78), channel_id=1, source_target_pairs={{0,8},{4,12},{8,0},{12,4},{1,9},{5,13},{9,1},{13,5},{2,10},{6,14},... | collective-permute-start | bytes 196616 | tf_op jit(solution)/shard_map/ppermute | solution.py:567
  19.4 4.5 %collective-permute-start.7 = (f32[120,128]{1,0:T(8,128)S(1)}, f32[120,128]{1,0:T(8,128)S(1)}, u32[]{:S(2)}, u32[]{:S(2)}) collective-permute-start(f32[120,128]{1,0:T(8,128)S(1)} %get-tuple-element.73), channel_id=1, source_target_pairs={{0,1},{1,0},{4,8},{5,9},{8,4},{9,5},{12,13},{13,12},{2,3},{3,2},{6... | collective-permute-start | bytes 184328 | tf_op jit(solution)/shard_map/ppermute | solution.py:563
  19.5 4.4 %collective-permute-start.6 = (f32[24,128]{1,0:T(8,128)S(1)}, f32[24,128]{1,0:T(8,128)S(1)}, u32[]{:S(2)}, u32[]{:S(2)}) collective-permute-start(f32[24,128]{1,0:T(8,128)S(1)} %get-tuple-element.72), channel_id=1, source_target_pairs={{0,4},{4,0},{8,12},{12,8},{1,5},{5,1},{9,13},{13,9},{2,6},{6,2},{1... | collective-permute-start | bytes 36872 | tf_op jit(solution)/shard_map/ppermute | solution.py:553
